TPU v7x, 128 devices: a whole 4x4x4 slice. The times are simulated.
128 devices in a mesh: row: 16 (over z_hi, y, core), col: 8 (over x, z_lo).
Axes of the slice: x: 4, y: 4, z: 4 (z_hi: 2, z_lo: 2; z = z_hi * 2 + z_lo), core: 2. Of those that a mesh axis runs over, the one named last changes fastest.
Arguments:
- amplitudes: bfloat16 [2, 16384, 2048], P(None, 'row', 'col'), may hold values from -6 to 6
- integrals: bfloat16 [2, 2048, 16384], P(None, 'row', 'col'), may hold values from -0.09375 to 0.09375
- tile_mask: int32 [2, 128, 16], P(None, 'row', 'col'), may hold values 0 or 1
- next_owner: int32 [16384, 1], P(('row', 'col')), may hold values from 0 to 127; in each aligned block of 128 rows (0 to 127, 128 to 255, ...) at most 2 rows name the same one
Outputs:
- relaid: bfloat16 [128, 256, 128, 128], P(('row', 'col'))
Inputs may be any that keep to these rules, and one draw needn't show every extreme that they name: `next_owner`: among the 128 rows of one grid position, no owner is named more than 2 times, a bound that some block reaches.
All inputs are finite; a program needn't handle non-finite values. No bound on the sum of `tile_mask` on one device may be relied on, other than what follows from the above.
Results may differ from a plain program's by a relative error of at most 0.001.
Values may be sent and summed in bfloat16 or wider, within the bound.
No kernel may reach another device: no remote copies, remote signals or barrier semaphores. Data moves between devices by JAX's collectives and lax.ppermute only.
A program may use at most 128 MiB of HBM per device.

v0:
```python
import jax
import jax.numpy as jnp
from jax import lax
from jax.sharding import PartitionSpec as P

TILE = 128


def local(amplitudes, integrals, tile_mask, next_owner):
    panels, m_rows, kp_local = amplitudes.shape
    n_cols = integrals.shape[2]
    tile_rows = m_rows // TILE
    k_tiles = kp_local // TILE
    n_tiles = n_cols // TILE
    kept_tiles = tile_mask.astype(jnp.bfloat16)
    masked = (
        amplitudes.reshape(panels, tile_rows, TILE, k_tiles, TILE) * kept_tiles[:, :, None, :, None]
    )
    masked = masked.reshape(panels, m_rows, kp_local)
    slab_sum = jnp.zeros((m_rows, n_cols), jnp.float32)
    for panel_step in range(panels):
        gathered = lax.all_gather(integrals[panel_step], "row", axis=0, tiled=True)
        slab_sum = slab_sum + jnp.dot(
            lax.all_gather(masked[panel_step], "col", axis=1, tiled=True),
            gathered,
            preferred_element_type=jnp.float32,
        )
    result_slab = slab_sum.astype(jnp.bfloat16)
    tiles_here = tile_rows * n_tiles
    result_tiles = result_slab.reshape(tile_rows, TILE, n_tiles, TILE).transpose(0, 2, 1, 3)
    result_tiles = result_tiles.reshape(tiles_here, TILE, TILE)
    row_count = lax.axis_size("row")
    col_count = lax.axis_size("col")
    devices = row_count * col_count
    capacity = 2 * tiles_here // devices
    owners = next_owner[:, 0]
    matches = (owners[:, None] == jnp.arange(devices, dtype=jnp.int32)[None, :]).astype(jnp.int32)
    ranking = jnp.sum((jnp.cumsum(matches, axis=0) - 1) * matches, axis=1)
    slot_index = owners * capacity + ranking
    outgoing = (
        jnp.zeros((devices * capacity, TILE, TILE), jnp.bfloat16).at[slot_index].set(result_tiles)
    )
    arrived = lax.all_to_all(outgoing, ("row", "col"), split_axis=0, concat_axis=0, tiled=True)
    return arrived[None]


def solution(mesh):
    return jax.shard_map(
        local,
        mesh=mesh,
        in_specs=(
            P(None, "row", "col"),
            P(None, "row", "col"),
            P(None, "row", "col"),
            P(("row", "col"), None),
        ),
        out_specs=P(("row", "col"), None, None, None),
        check_vma=False,
    )
```

profile of v0, /device:TPU:0, one launch (start us, length us, event | category | flops | bytes accessed | tf_op | source)
XLA Modules:
  0.0 516.9 jit_solution(10995536112798147996)
XLA Ops:
  6.5 1.4 reshape.16
  8.0 0.7 convert_element_type.10
  8.7 0.1 copy.5
  8.8 1.0 broadcast_multiply_fusion
  9.7 0.7 fusion.12
  10.5 0.9 copy.12
  11.4 0.0 all-gather.9.cloned.1.call-update
  11.4 0.0 all-gather.13.cloned.1.call-start
  11.4 0.0 copy-done
  11.4 1.1 fusion.11
  12.6 0.0 all-gather.13.cloned.1.call-update
  12.6 0.0 all-gather.7.cloned.1.call-start
  12.6 0.9 copy.13
  13.5 0.0 all-gather.7.cloned.1.call-update
  13.5 0.2 all-gather.11.cloned.1.call-start
  13.8 0.3 all-gather.11.cloned.1.call-update
  14.1 0.1 fusion.9
  14.2 0.2 reduce_window_sum.11
  14.4 0.2 select_reduce_fusion
  14.6 90.4 %all-gather.9.cloned.1.call-done = bf16[1024,2048]{1,0:T(8,128)(2,1)} async-done(((bf16[1024,256]{1,0:T(8,128)(2,1)}), bf16[1024,2048]{1,0:T(8,128)(2,1)}) %all-gather.9.cloned.1.call-update) | async-done | bytes 4194320 | tf_op jit(solution)/shard_map/all_gather | solution.py:24
  105.0 77.9 %all-gather.13.cloned.1.call-done = bf16[1,2048,2048]{2,1,0:T(8,128)(2,1)} async-done(((bf16[1,128,2048]{2,1,0:T(8,128)(2,1)}), bf16[1,2048,2048]{2,1,0:T(8,128)(2,1)}) %all-gather.13.cloned.1.call-update) | async-done | bytes 8388624 | tf_op jit(solution)/shard_map/all_gather | solution.py:22
  182.9 14.5 %fusion = f32[1024,2048]{1,0:T(8,128)} fusion(bf16[1024,2048]{1,0:T(8,128)(2,1)} %all-gather.9.cloned.1.call-done, bf16[1,2048,2048]{2,1,0:T(8,128)(2,1)} %all-gather.13.cloned.1.call-done), kind=kOutput, calls=%fused_computation.1 | convolution fusion | flops 8589934592 | bytes 20971520 | tf_op jit(solution)/shard_map/dot_general | solution.py:23
  197.3 75.8 %all-gather.7.cloned.1.call-done = bf16[1024,2048]{1,0:T(8,128)(2,1)} async-done(((bf16[1024,256]{1,0:T(8,128)(2,1)}), bf16[1024,2048]{1,0:T(8,128)(2,1)}) %all-gather.7.cloned.1.call-update) | async-done | bytes 4194320 | tf_op jit(solution)/shard_map/all_gather | solution.py:24
  273.1 79.2 %all-gather.11.cloned.1.call-done = bf16[1,2048,2048]{2,1,0:T(8,128)(2,1)} async-done(((bf16[1,128,2048]{2,1,0:T(8,128)(2,1)}), bf16[1,2048,2048]{2,1,0:T(8,128)(2,1)}) %all-gather.11.cloned.1.call-update) | async-done | bytes 8388624 | tf_op jit(solution)/shard_map/all_gather | solution.py:22
  352.3 13.7 %fusion.6 = bf16[128,8,16,128]{3,1,2,0:T(8,128)(2,1)S(1)} fusion(f32[1024,2048]{1,0:T(8,128)} %fusion, bf16[1024,2048]{1,0:T(8,128)(2,1)} %all-gather.7.cloned.1.call-done, bf16[1,2048,2048]{2,1,0:T(8,128)(2,1)} %all-gather.11.cloned.1.call-done), kind=kOutput, calls=%fused_computation.7 | convolution fusion | flops 8594128896 | bytes 25165824 | tf_op jit(solution)/shard_map/dot_general | solution.py:23
  366.0 1.4 copy.9
  367.4 0.7 bitcast_bitcast_fusion
  368.2 3.1 copy.6
  371.3 5.5 %broadcast_in_dim.4 = bf16[256,128,128]{2,1,0:T(8,128)(2,1)} broadcast(bf16[]{:T(256)} %constant.5.clone.1), dimensions={} | broadcast | bytes 8388610 | tf_op jit(solution)/shard_map/broadcast_in_dim | solution.py:41
  376.8 19.3 %scatter_fusion = bf16[256,128,128]{2,1,0:T(8,128)(2,1)} fusion(bf16[256,128,128]{2,1,0:T(8,128)(2,1)} %broadcast_in_dim.4, s32[128]{0:T(128)S(1)} %fusion.10, bf16[128,128,128]{2,1,0:T(8,128)(2,1)} %bitcast.40), kind=kCustom, calls=%fused_computation | custom fusion | bytes 12583424 | tf_op jit(solution)/shard_map/scatter | solution.py:41
  396.1 103.8 %all_to_all.5 = bf16[256,128,128]{2,1,0:T(8,128)(2,1)} all-to-all(bf16[256,128,128]{2,1,0:T(8,128)(2,1)} %scatter_fusion), channel_id=1, replica_groups=mesh['row'=16,'col'=8] {'row','col'}, dimensions={0} | all-to-all | bytes 16777216 | tf_op jit(solution)/shard_map/all_to_all | solution.py:43
  499.8 10.5 %copy.16 = bf16[1,256,128,128]{3,2,1,0:T(8,128)(2,1)} copy(bf16[1,256,128,128]{3,2,1,0:T(8,128)(2,1)} %bitcast.39) | data formatting | bytes 16777216
  (5 shorter events, 0.0 us)
Async XLA Ops:
  6.5 4.9 copy-start
  6.5 7.6 %copy-start.1 = (s32[128,1]{0,1:T(1,128)S(1)}, s32[128,1]{0,1:T(1,128)}, u32[]{:S(2)}) copy-start(s32[128,1]{0,1:T(1,128)} %param.7) | copy-start | bytes 1540
  6.5 98.5 %all-gather.9.cloned.1.call-start = ((), (), s32[]{:S(2)}) async-start(), calls=%async_computation.2 | async-start | bytes 4718592 | tf_op jit(solution)/shard_map/all_gather | solution.py:24
  11.4 171.5 %all-gather.13.cloned.1.call-start = ((), (), s32[]{:S(2)}) async-start(), calls=%async_computation.4 | async-start | bytes 8912896 | tf_op jit(solution)/shard_map/all_gather | solution.py:22
  12.6 260.5 %all-gather.7.cloned.1.call-start = ((), (), s32[]{:S(2)}) async-start(), calls=%async_computation.1 | async-start | bytes 4718592 | tf_op jit(solution)/shard_map/all_gather | solution.py:24
  13.5 338.8 %all-gather.11.cloned.1.call-start = ((), (), s32[]{:S(2)}) async-start(), calls=%async_computation.3 | async-start | bytes 8912896 | tf_op jit(solution)/shard_map/all_gather | solution.py:22
Sparse Core Ops, SparseCore 0:
  11.5 93.4 all-gather.8
  107.5 75.3 all-gather.12
  184.5 88.6 all-gather.6
  275.4 76.8 all-gather.10
where the time goes:
time: 517 us
  waiting for transfers between devices  324 us (63%)
  blocking collectives  104 us (20%)
  local copies, waits for them, and re-layouts  45.7 us (9%)
  matrix products  28.2 us (5%)
  between operations  13.2 us (3%)
    all_gather x2, waiting for transfers between devices, local(): lax.all_gather(masked[panel_step], 'col', axis=1, tiled=True)  166 us
    all_gather x2, waiting for transfers between devices, local(): gathered = lax.all_gather(integrals[panel_step], 'row', axis=0, tiled=True)  157 us
    all_to_all x1, blocking collectives, local(): lax.all_to_all(outgoing, ('row', 'col'), split_axis=0, concat_axis=0, til...  104 us
    dot_general x2, matrix products, local(): jnp.dot(lax.all_gather(masked[panel_step], 'col', axis=1, tiled=True), ga...  28.2 us
    scatter x1, local copies, waits for them, and re-layouts, local(): jnp.zeros((devices * capacity, TILE, TILE), jnp.bfloat16).at[slot_index]  19.3 us
    unnamed x8, local copies, waits for them, and re-layouts  13.7 us
  transfers between devices with their start and end apart: 4, of which 4 were waited for; matrix products, arithmetic and copies ran while one was open for 3% of the time, Pallas kernels for 0%

commit v1 on v0

v1 whole, which is shorter than its diff:
```python
import jax
import jax.numpy as jnp
from jax import lax
from jax.experimental import pallas as pl
from jax.experimental.pallas import tpu as pltpu
from jax.sharding import PartitionSpec as P

TILE = 128
AXES = ("row", "col")
ROWS, COLS, DEPTH = 1024, 2048, 256
CHUNKS = 8
WIDE = 512
SLOTS = 256


def index_of(x, y, z, core):
    return ((z // 2) * 8 + y * 2 + core) * 8 + x * 2 + z % 2


def pairs(move):
    found = []
    for row in range(16):
        for col in range(8):
            place = (col // 2, (row // 2) % 4, (row // 8) * 2 + col % 2, row % 2)
            found.append((row * 8 + col, index_of(*move(*place))))
    return found


def along_x(step):
    return pairs(lambda x, y, z, core: ((x + step) % 4, y, z, core))


def along_y(step):
    return pairs(lambda x, y, z, core: (x, (y + step) % 4, z, core))


def across_z(bit):
    return pairs(lambda x, y, z, core: (x, y, z ^ bit, core))


def mate():
    return pairs(lambda x, y, z, core: (x, y, z, 1 - core))


def send(value, where):
    return lax.ppermute(value, AXES, where)


def mask_kernel(mask_ref, a_ref, out_ref):
    for panel in range(2):
        for i in range(ROWS // TILE):
            for k in range(DEPTH // TILE):
                at = (panel, pl.ds(i * TILE, TILE), pl.ds(k * TILE, TILE))
                kept = mask_ref[(panel * 8 + i) * 2 + k] != 0
                block = a_ref[at]
                out_ref[at] = jnp.where(kept, block, jnp.zeros_like(block))


def apply_mask(amplitudes, tile_mask):
    return pl.pallas_call(
        mask_kernel,
        out_shape=jax.ShapeDtypeStruct(amplitudes.shape, amplitudes.dtype),
        in_specs=[
            pl.BlockSpec(memory_space=pltpu.SMEM),
            pl.BlockSpec(memory_space=pltpu.VMEM),
        ],
        out_specs=pl.BlockSpec(memory_space=pltpu.VMEM),
        compiler_params=pltpu.CompilerParams(vmem_limit_bytes=8 << 20),
        cost_estimate=pl.CostEstimate(flops=0, bytes_accessed=2 << 20, transcendentals=0),
    )(tile_mask.reshape(-1), amplitudes)


def contract_kernel(place_ref, slot_ref, source_ref, *refs):
    (own_a, z_a, xm_a, xp_a, cm_a, cp_a, dm_a, dp_a) = refs[:8]
    b_here, b_mate = refs[8:17], refs[17:26]
    out_ref = refs[26]
    a_all, b_all, tiles, zero, a_sem, b_sem, out_sem = refs[27:]
    x, z_lo, y, z_hi, core = (place_ref[i] for i in range(5))

    def chunk_a(dx, dz):
        return ((x + dx) % 4) * 2 + jnp.bitwise_xor(z_lo, dz)

    def chunk_b(dy, dz):
        return jnp.bitwise_xor(z_hi, dz) * 4 + (y + dy) % 4

    plan_a = []
    for ref, dx, dz in ((own_a, 0, 0), (z_a, 0, 1), (xm_a, 3, 0), (xp_a, 1, 0), (cm_a, 3, 1), (cp_a, 1, 1)):
        plan_a += [(ref, 0, chunk_a(dx, dz), 0), (ref, 1, chunk_a(dx, dz), 1)]
    plan_a += [(cm_a, 2, chunk_a(2, 0), 0), (cp_a, 2, chunk_a(2, 0), 1)]
    plan_a += [(dm_a, 0, chunk_a(2, 1), 0), (dp_a, 0, chunk_a(2, 1), 1)]
    where_b = ((0, 0), (3, 0), (1, 0), (2, 0), (0, 1), (3, 1), (1, 1), (2, 1), (2, 1))

    def b_copies(part):
        columns = pl.ds(part * WIDE, WIDE)
        for held, side in ((b_here, core), (b_mate, 1 - core)):
            for n, (dy, dz) in enumerate(where_b):
                chunk = chunk_b(dy, dz)
                depth = pl.ds(pl.multiple_of(side * TILE, TILE), TILE)
                for panel in range(2):
                    if n >= 7 and panel != n - 7:
                        continue
                    yield pltpu.make_async_copy(
                        held[n].at[0 if n >= 7 else panel, :, columns],
                        b_all.at[part % 2, chunk, panel, depth, :],
                        b_sem.at[part % 2],
                    )

    for copy in b_copies(0):
        copy.start()
    for ref, panel_from, chunk, panel in plan_a:
        pltpu.make_async_copy(ref.at[panel_from], a_all.at[chunk, panel], a_sem).start()
    zero[...] = jnp.zeros_like(zero)

    def clear(slot, carry):
        @pl.when(source_ref[slot] < 0)
        def _():
            pltpu.make_async_copy(zero, out_ref.at[slot], out_sem).start()

        return carry

    lax.fori_loop(0, SLOTS, clear, 0)
    pltpu.make_async_copy(a_all, a_all, a_sem).wait()
    for part in range(COLS // WIDE):
        if part + 1 < COLS // WIDE:
            for copy in b_copies(part + 1):
                copy.start()
        held = b_all.at[part % 2]
        pltpu.make_async_copy(held, held, b_sem.at[part % 2]).wait()
        right = b_all[part % 2].reshape(CHUNKS * 2 * DEPTH, WIDE)

        def rows(i, carry):
            at = pl.ds(pl.multiple_of(i * 256, 256), 256)
            total = jnp.zeros((256, WIDE), jnp.float32)
            left = jnp.concatenate(
                [a_all[c, p, at, :] for c in range(CHUNKS) for p in range(2)], axis=1
            )
            total = jnp.dot(left, right, preferred_element_type=jnp.float32).astype(jnp.bfloat16)
            for di in range(2):
                for j in range(WIDE // TILE):
                    number = (i * 2 + di) * (COLS // TILE) + part * (WIDE // TILE) + j
                    tiles[number] = total[di * TILE : (di + 1) * TILE, j * TILE : (j + 1) * TILE]
                    pltpu.make_async_copy(tiles.at[number], out_ref.at[slot_ref[number]], out_sem).start()
            return carry

        lax.fori_loop(0, ROWS // 256, rows, 0)
    pltpu.make_async_copy(out_ref, out_ref, out_sem).wait()


def contract(place, slots, sources, a_parts, b_here, b_mate):
    return pl.pallas_call(
        contract_kernel,
        out_shape=jax.ShapeDtypeStruct((SLOTS, TILE, TILE), jnp.bfloat16),
        in_specs=[pl.BlockSpec(memory_space=pltpu.SMEM)] * 3 + [pl.BlockSpec(memory_space=pl.ANY)] * 26,
        out_specs=pl.BlockSpec(memory_space=pl.ANY),
        scratch_shapes=[
            pltpu.VMEM((CHUNKS, 2, ROWS, DEPTH), jnp.bfloat16),
            pltpu.VMEM((2, CHUNKS, 2, DEPTH, WIDE), jnp.bfloat16),
            pltpu.VMEM((128, TILE, TILE), jnp.bfloat16),
            pltpu.VMEM((TILE, TILE), jnp.bfloat16),
            pltpu.SemaphoreType.DMA(()),
            pltpu.SemaphoreType.DMA((2,)),
            pltpu.SemaphoreType.DMA(()),
        ],
        compiler_params=pltpu.CompilerParams(vmem_limit_bytes=40 << 20),
        cost_estimate=pl.CostEstimate(flops=2 * 1024 * 2048 * 4096, bytes_accessed=40 << 20, transcendentals=0),
    )(place, slots, sources, *a_parts, *b_here, *b_mate)


def after(value, *earlier):
    return lax.optimization_barrier((value, *earlier))[0]


def local(amplitudes, integrals, tile_mask, next_owner):
    row, col = lax.axis_index("row"), lax.axis_index("col")
    place = jnp.stack([col // 2, col % 2, (row // 2) % 4, row // 8, row % 2]).astype(jnp.int32)

    owners = next_owner[:, 0]
    before = jnp.arange(TILE)[None, :] < jnp.arange(TILE)[:, None]
    rank = jnp.sum(((owners[None, :] == owners[:, None]) & before).astype(jnp.int32), axis=1)
    slots = owners * 2 + rank
    tile_at = slots[None, :] == jnp.arange(SLOTS, dtype=jnp.int32)[:, None]
    sources = jnp.max(jnp.where(tile_at, jnp.arange(TILE, dtype=jnp.int32)[None, :], -1), axis=1)

    b = integrals
    a = apply_mask(amplitudes, tile_mask)
    b_ym, b_yp = send(b, along_y(1)), send(b, along_y(-1))
    a_xm, a_xp, a_z = send(a, along_x(1)), send(a, along_x(-1)), send(a, across_z(1))
    b_late = after(b, b_ym)
    b_z, b_y2 = send(b_late, across_z(2)), send(b_late, along_y(2))
    a_cm = send(jnp.concatenate([a_z, a_xm[:1]], axis=0), along_x(1))
    a_cp = send(jnp.concatenate([a_z, a_xp[1:]], axis=0), along_x(-1))
    b_zym, b_zyp = send(b_z, along_y(1)), send(b_z, along_y(-1))
    a_dm, a_dp = send(a_cm[:1], along_x(1)), send(a_cp[1:2], along_x(-1))
    b_em, b_ep = send(b_zym[:1], along_y(1)), send(b_zyp[1:], along_y(-1))

    b_here = (b, b_ym, b_yp, b_y2, b_z, b_zym, b_zyp, b_em, b_ep)
    b_mate = tuple(send(v, mate()) for v in b_here)
    outgoing = contract(place, slots, sources, (a, a_z, a_xm, a_xp, a_cm, a_cp, a_dm, a_dp), b_here, b_mate)
    arrived = lax.all_to_all(outgoing, AXES, split_axis=0, concat_axis=0, tiled=True)
    return arrived[None]


def solution(mesh):
    return jax.shard_map(
        local,
        mesh=mesh,
        in_specs=(
            P(None, "row", "col"),
            P(None, "row", "col"),
            P(None, "row", "col"),
            P(AXES, None),
        ),
        out_specs=P(AXES, None, None, None),
        check_vma=False,
    )
```

time: 517 us -> 283 us (0.55)
  waiting for transfers between devices: 324 us -> 95.3 us
  Pallas kernels: 0 us -> 28.6 us
  matrix products: 28.2 us -> 0 us
  starting transfers between devices: 0.31 us -> 28.2 us
  local copies, waits for them, and re-layouts: 45.7 us -> 25.2 us
  between operations: 13.2 us -> 0.31 us
    all_gather x4 -> x0, waiting for transfers between devices: 323 us -> none  [the longest x2 166 us: local(): lax.all_gather(masked[panel_step], 'col', axis=1, tiled=True)]
    ppermute x0 -> x24, waiting for transfers between devices: none -> 95.3 us  [send(): return lax.ppermute(value, AXES, where)]
    pallas_call x0 -> x2, Pallas kernels: none -> 28.6 us  [the longest x1 27.8 us: contract(): pl.pallas_call(contract_kernel, out_shape=jax.ShapeDtypeStruct((SLOTS, TI...]
    ppermute x0 -> x24, starting transfers between devices: none -> 28.2 us  [send(): return lax.ppermute(value, AXES, where)]
    dot_general x2 -> x0, matrix products: 28.2 us -> none  [local(): jnp.dot(lax.all_gather(masked[panel_step], 'col', axis=1, tiled=True), ga...]
    scatter x1 -> x0, local copies, waits for them, and re-layouts: 19.3 us -> none  [local(): jnp.zeros((devices * capacity, TILE, TILE), jnp.bfloat16).at[slot_index]]
    unnamed x8 -> x44, local copies, waits for them, and re-layouts: 13.7 us -> 21.5 us
    broadcast_in_dim x1 -> x0, local copies, waits for them, and re-layouts: 5.52 us -> none  [local(): jnp.zeros((devices * capacity, TILE, TILE), jnp.bfloat16).at[slot_index]]
  transfers between devices with their start and end apart: 4 -> 24, of which waited for: 4 -> 10; matrix products, arithmetic and copies ran while one was open for 3% -> 2% of each run, Pallas kernels for 0% -> 0%
where the time goes in v1:
time: 283 us; the launch traced here: 282 us
  blocking collectives  104 us (37%)
  waiting for transfers between devices  95.3 us (34%)
  Pallas kernels  28.6 us (10%)
  starting transfers between devices  28.2 us (10%)
  local copies, waits for them, and re-layouts  25.2 us (9%)
    all_to_all x1, blocking collectives, local(): lax.all_to_all(outgoing, AXES, split_axis=0, concat_axis=0, tiled=True)  104 us
    ppermute x24, waiting for transfers between devices, send(): return lax.ppermute(value, AXES, where)  95.3 us
    ppermute x24, starting transfers between devices, send(): return lax.ppermute(value, AXES, where)  28.2 us
    pallas_call x1, Pallas kernels, contract(): pl.pallas_call(contract_kernel, out_shape=jax.ShapeDtypeStruct((SLOTS, TI...  27.8 us
    unnamed x44, local copies, waits for them, and re-layouts  21.5 us
  transfers between devices with their start and end apart: 24, of which 10 were waited for; matrix products, arithmetic and copies ran while one was open for 2% of the time, Pallas kernels for 0%

profile of v1, /device:TPU:0, one launch (start us, length us, event | category | flops | bytes accessed | tf_op | source)
XLA Modules:
  0.0 282.1 jit_solution(18010050952265299467)
XLA Ops:
  0.0 1.7 collective-permute-start.7
  2.5 1.2 copy-done
  4.5 2.8 %collective-permute-start.2 = (bf16[2,1024,256]{2,1,0:T(8,128)(2,1)S(1)}, bf16[2,1024,256]{2,1,0:T(8,128)(2,1)S(1)}, u32[]{:S(2)}, u32[]{:S(2)}) collective-permute-start(bf16[2,1024,256]{2,1,0:T(8,128)(2,1)S(1)} %shard_map.46.refs_0_), channel_id=1, source_target_pairs={{0,6},{1,7},{2,0},{3,1},{4,2},{5,3},{6,4},{7,5},{8,14},{9,15},{10,... | collective-permute-start | bytes 3145736 | tf_op jit(solution)/shard_map/ppermute | solution.py:46
  7.4 1.9 collective-permute-start
  9.3 17.3 %collective-permute-done.7.refs_9_ = bf16[2,128,2048]{2,1,0:T(8,128)(2,1)} collective-permute-done((bf16[2,128,2048]{2,1,0:T(8,128)(2,1)}, bf16[2,128,2048]{2,1,0:T(8,128)(2,1)}, u32[]{:S(2)}, u32[]{:S(2)}) %collective-permute-start.7) | collective-permute-done | bytes 1048608 | tf_op jit(solution)/shard_map/ppermute | solution.py:46
  26.6 3.9 %collective-permute-start.10 = (bf16[2,128,2048]{2,1,0:T(8,128)(2,1)S(1)}, bf16[2,128,2048]{2,1,0:T(8,128)(2,1)S(1)}, u32[]{:S(2)}, u32[]{:S(2)}) collective-permute-start(bf16[2,128,2048]{2,1,0:T(8,128)(2,1)S(1)} %copy-done.3), channel_id=1, source_target_pairs={{0,64},{1,65},{2,66},{3,67},{4,68},{5,69},{6,70},{7,71},{8,72},{9,... | collective-permute-start | bytes 3145736 | tf_op jit(solution)/shard_map/ppermute | solution.py:46
  30.4 1.7 collective-permute-start.8
  34.1 2.2 collective-permute-start.4
  36.3 3.6 %collective-permute-start.9 = (bf16[2,128,2048]{2,1,0:T(8,128)(2,1)S(1)}, bf16[2,128,2048]{2,1,0:T(8,128)(2,1)S(1)}, u32[]{:S(2)}, u32[]{:S(2)}) collective-permute-start(bf16[2,128,2048]{2,1,0:T(8,128)(2,1)S(1)} %copy-done.3), channel_id=1, source_target_pairs={{0,32},{1,33},{2,34},{3,35},{4,36},{5,37},{6,38},{7,39},{8,40},{9,... | collective-permute-start | bytes 3145736 | tf_op jit(solution)/shard_map/ppermute | solution.py:46
  39.9 17.8 %collective-permute-done.10.refs_12_ = bf16[2,128,2048]{2,1,0:T(8,128)(2,1)S(1)} collective-permute-done((bf16[2,128,2048]{2,1,0:T(8,128)(2,1)S(1)}, bf16[2,128,2048]{2,1,0:T(8,128)(2,1)S(1)}, u32[]{:S(2)}, u32[]{:S(2)}) %collective-permute-start.10) | collective-permute-done | bytes 1048608 | tf_op jit(solution)/shard_map/ppermute | solution.py:46
  57.6 1.7 collective-permute-start.12
  60.2 3.8 %collective-permute-done.9.refs_11_ = bf16[2,128,2048]{2,1,0:T(8,128)(2,1)S(1)} collective-permute-done((bf16[2,128,2048]{2,1,0:T(8,128)(2,1)S(1)}, bf16[2,128,2048]{2,1,0:T(8,128)(2,1)S(1)}, u32[]{:S(2)}, u32[]{:S(2)}) %collective-permute-start.9) | collective-permute-done | bytes 1048608 | tf_op jit(solution)/shard_map/ppermute | solution.py:46
  63.9 4.9 %collective-permute-done.4.refs_5_ = bf16[3,1024,256]{2,1,0:T(8,128)(2,1)S(1)} collective-permute-done((bf16[3,1024,256]{2,1,0:T(8,128)(2,1)S(1)}, bf16[3,1024,256]{2,1,0:T(8,128)(2,1)S(1)}, u32[]{:S(2)}, u32[]{:S(2)}) %collective-permute-start.4) | collective-permute-done | bytes 1572896 | tf_op jit(solution)/shard_map/ppermute | solution.py:46
  68.9 30.5 %collective-permute-done.12.refs_14_ = bf16[2,128,2048]{2,1,0:T(8,128)(2,1)} collective-permute-done((bf16[2,128,2048]{2,1,0:T(8,128)(2,1)S(1)}, bf16[2,128,2048]{2,1,0:T(8,128)(2,1)}, u32[]{:S(2)}, u32[]{:S(2)}) %collective-permute-start.12) | collective-permute-done | bytes 1048608 | tf_op jit(solution)/shard_map/ppermute | solution.py:46
  99.9 1.1 slice.29
  101.0 1.1 slice.28
  102.2 2.8 %collective-permute-start.6 = (bf16[1,1024,256]{2,1,0:T(8,128)(2,1)S(1)}, bf16[1,1024,256]{2,1,0:T(8,128)(2,1)S(1)}, u32[]{:S(2)}, u32[]{:S(2)}) collective-permute-start(bf16[1,1024,256]{2,1,0:T(8,128)(2,1)S(1)} %slice.27), channel_id=1, source_target_pairs={{0,6},{1,7},{2,0},{3,1},{4,2},{5,3},{6,4},{7,5},{8,14},{9,15},{10,... | collective-permute-start | bytes 1572872 | tf_op jit(solution)/shard_map/ppermute | solution.py:46
  105.0 2.8 %collective-permute-start.14 = (bf16[1,128,2048]{2,1,0:T(8,128)(2,1)S(1)}, bf16[1,128,2048]{2,1,0:T(8,128)(2,1)}, u32[]{:S(2)}, u32[]{:S(2)}) collective-permute-start(bf16[1,128,2048]{2,1,0:T(8,128)(2,1)S(1)} %slice.29), channel_id=1, source_target_pairs={{0,48},{1,49},{2,50},{3,51},{4,52},{5,53},{6,54},{7,55},{8,56},{9,... | collective-permute-start | bytes 1572872 | tf_op jit(solution)/shard_map/ppermute | solution.py:46
  108.5 1.3 slice.26
  109.7 6.7 %collective-permute-done.6.refs_7_ = bf16[1,1024,256]{2,1,0:T(8,128)(2,1)S(1)} collective-permute-done((bf16[1,1024,256]{2,1,0:T(8,128)(2,1)S(1)}, bf16[1,1024,256]{2,1,0:T(8,128)(2,1)S(1)}, u32[]{:S(2)}, u32[]{:S(2)}) %collective-permute-start.6) | collective-permute-done | bytes 524320 | tf_op jit(solution)/shard_map/ppermute | solution.py:46
  117.2 1.2 collective-permute-start.5
  119.0 3.5 %collective-permute-done.13.refs_15_ = bf16[1,128,2048]{2,1,0:T(8,128)(2,1)} collective-permute-done((bf16[1,128,2048]{2,1,0:T(8,128)(2,1)S(1)}, bf16[1,128,2048]{2,1,0:T(8,128)(2,1)}, u32[]{:S(2)}, u32[]{:S(2)}) %collective-permute-start.13) | collective-permute-done | bytes 524320 | tf_op jit(solution)/shard_map/ppermute | solution.py:46
  123.0 9.7 %collective-permute-done.5.refs_6_ = bf16[1,1024,256]{2,1,0:T(8,128)(2,1)} collective-permute-done((bf16[1,1024,256]{2,1,0:T(8,128)(2,1)}, bf16[1,1024,256]{2,1,0:T(8,128)(2,1)}, u32[]{:S(2)}, u32[]{:S(2)}) %collective-permute-start.5) | collective-permute-done | bytes 524320 | tf_op jit(solution)/shard_map/ppermute | solution.py:46
  132.7 1.2 copy-done.2
  133.9 1.2 copy-done.4
  135.1 1.2 copy-done.6
  136.4 1.2 copy-done.8
  137.6 1.2 copy-done.10
  138.8 1.0 copy-done.12
  139.9 27.8 %shard_map.47 = bf16[256,128,128]{2,1,0:T(8,128)(2,1)} custom-call(s32[5]{0:T(128)S(1)} %stack.23.place_ref, s32[128]{0:T(128)S(1)} %multiply_add_fusion.slot_ref, s32[256]{0:T(256)S(1)} %select_reduce_fusion.source_ref, bf16[2,1024,256]{2,1,0:T(8,128)(2,1)S(1)} %shard_map.46.refs_0_, bf16[2,1024,256]{2,1,0:T(8,128)(2,1)S(1)} %collective-permute-done.refs_1_, ...), custom_call_target="tpu_custom_call" | custom-call | flops 17179869184 | bytes 41943040 | tf_op jit(solution)/shard_map/pallas_call | solution.py:150
  167.7 103.9 %all_to_all.5 = bf16[256,128,128]{2,1,0:T(8,128)(2,1)} all-to-all(bf16[256,128,128]{2,1,0:T(8,128)(2,1)} %shard_map.47), channel_id=1, replica_groups=mesh['row'=16,'col'=8] {'row','col'}, dimensions={0} | all-to-all | bytes 16777216 | tf_op jit(solution)/shard_map/all_to_all | solution.py:199
  271.6 10.5 %copy.9 = bf16[1,256,128,128]{3,2,1,0:T(8,128)(2,1)} copy(bf16[1,256,128,128]{3,2,1,0:T(8,128)(2,1)} %bitcast.8) | data formatting | bytes 16777216
  (75 shorter events, 7.3 us)
Async XLA Ops:
  0.0 26.6 %collective-permute-start.7 = (bf16[2,128,2048]{2,1,0:T(8,128)(2,1)}, bf16[2,128,2048]{2,1,0:T(8,128)(2,1)}, u32[]{:S(2)}, u32[]{:S(2)}) collective-permute-start(bf16[2,128,2048]{2,1,0:T(8,128)(2,1)} %refs_8_.1), channel_id=1, source_target_pairs={{0,16},{1,17},{2,18},{3,19},{4,20},{5,21},{6,22},{7,23},{8,24},{9,... | collective-permute-start | bytes 3145736 | tf_op jit(solution)/shard_map/ppermute | solution.py:46
  3.7 22.8 %copy-start.3 = (bf16[2,128,2048]{2,1,0:T(8,128)(2,1)S(1)}, bf16[2,128,2048]{2,1,0:T(8,128)(2,1)}, u32[]{:S(2)}) copy-start(bf16[2,128,2048]{2,1,0:T(8,128)(2,1)} %refs_8_.1) | copy-start | bytes 3145732
  4.5 27.7 %collective-permute-start.2 = (bf16[2,1024,256]{2,1,0:T(8,128)(2,1)S(1)}, bf16[2,1024,256]{2,1,0:T(8,128)(2,1)S(1)}, u32[]{:S(2)}, u32[]{:S(2)}) collective-permute-start(bf16[2,1024,256]{2,1,0:T(8,128)(2,1)S(1)} %shard_map.46.refs_0_), channel_id=1, source_target_pairs={{0,6},{1,7},{2,0},{3,1},{4,2},{5,3},{6,4},{7,5},{8,14},{9,15},{10,... | collective-permute-start | bytes 3145736 | tf_op jit(solution)/shard_map/ppermute | solution.py:46
  7.4 25.5 %collective-permute-start.1 = (bf16[2,1024,256]{2,1,0:T(8,128)(2,1)S(1)}, bf16[2,1024,256]{2,1,0:T(8,128)(2,1)S(1)}, u32[]{:S(2)}, u32[]{:S(2)}) collective-permute-start(bf16[2,1024,256]{2,1,0:T(8,128)(2,1)S(1)} %shard_map.46.refs_0_), channel_id=1, source_target_pairs={{0,2},{1,3},{2,4},{3,5},{4,6},{5,7},{6,0},{7,1},{8,10},{9,11},{10,... | collective-permute-start | bytes 3145736 | tf_op jit(solution)/shard_map/ppermute | solution.py:46
  7.4 26.6 %collective-permute-start = (bf16[2,1024,256]{2,1,0:T(8,128)(2,1)S(1)}, bf16[2,1024,256]{2,1,0:T(8,128)(2,1)S(1)}, u32[]{:S(2)}, u32[]{:S(2)}) collective-permute-start(bf16[2,1024,256]{2,1,0:T(8,128)(2,1)S(1)} %shard_map.46.refs_0_), channel_id=1, source_target_pairs={{0,1},{1,0},{2,3},{3,2},{4,5},{5,4},{6,7},{7,6},{8,9},{9,8},{10,11... | collective-permute-start | bytes 3145736 | tf_op jit(solution)/shard_map/ppermute | solution.py:46
  26.6 31.1 %collective-permute-start.10 = (bf16[2,128,2048]{2,1,0:T(8,128)(2,1)S(1)}, bf16[2,128,2048]{2,1,0:T(8,128)(2,1)S(1)}, u32[]{:S(2)}, u32[]{:S(2)}) collective-permute-start(bf16[2,128,2048]{2,1,0:T(8,128)(2,1)S(1)} %copy-done.3), channel_id=1, source_target_pairs={{0,64},{1,65},{2,66},{3,67},{4,68},{5,69},{6,70},{7,71},{8,72},{9,... | collective-permute-start | bytes 3145736 | tf_op jit(solution)/shard_map/ppermute | solution.py:46
  30.4 28.9 %collective-permute-start.8 = (bf16[2,128,2048]{2,1,0:T(8,128)(2,1)S(1)}, bf16[2,128,2048]{2,1,0:T(8,128)(2,1)S(1)}, u32[]{:S(2)}, u32[]{:S(2)}) collective-permute-start(bf16[2,128,2048]{2,1,0:T(8,128)(2,1)S(1)} %copy-done.3), channel_id=1, source_target_pairs={{0,48},{1,49},{2,50},{3,51},{4,52},{5,53},{6,54},{7,55},{8,56},{9,... | collective-permute-start | bytes 3145736 | tf_op jit(solution)/shard_map/ppermute | solution.py:46
  34.1 34.7 %collective-permute-start.4 = (bf16[3,1024,256]{2,1,0:T(8,128)(2,1)S(1)}, bf16[3,1024,256]{2,1,0:T(8,128)(2,1)S(1)}, u32[]{:S(2)}, u32[]{:S(2)}) collective-permute-start(bf16[3,1024,256]{2,1,0:T(8,128)(2,1)S(1)} %get-tuple-element.7), channel_id=1, source_target_pairs={{0,6},{1,7},{2,0},{3,1},{4,2},{5,3},{6,4},{7,5},{8,14},{9,15},{10,... | collective-permute-start | bytes 4718600 | tf_op jit(solution)/shard_map/ppermute | solution.py:46
  36.3 23.4 %collective-permute-start.15 = (bf16[2,128,2048]{2,1,0:T(8,128)(2,1)S(1)}, bf16[2,128,2048]{2,1,0:T(8,128)(2,1)S(1)}, u32[]{:S(2)}, u32[]{:S(2)}) collective-permute-start(bf16[2,128,2048]{2,1,0:T(8,128)(2,1)S(1)} %copy-done.3), channel_id=1, source_target_pairs={{0,8},{1,9},{2,10},{3,11},{4,12},{5,13},{6,14},{7,15},{8,0},{9,1},... | collective-permute-start | bytes 3145736 | tf_op jit(solution)/shard_map/ppermute | solution.py:46
  36.3 27.6 %collective-permute-start.9 = (bf16[2,128,2048]{2,1,0:T(8,128)(2,1)S(1)}, bf16[2,128,2048]{2,1,0:T(8,128)(2,1)S(1)}, u32[]{:S(2)}, u32[]{:S(2)}) collective-permute-start(bf16[2,128,2048]{2,1,0:T(8,128)(2,1)S(1)} %copy-done.3), channel_id=1, source_target_pairs={{0,32},{1,33},{2,34},{3,35},{4,36},{5,37},{6,38},{7,39},{8,40},{9,... | collective-permute-start | bytes 3145736 | tf_op jit(solution)/shard_map/ppermute | solution.py:46
  57.6 44.5 %copy-start.5 = (bf16[2,128,2048]{2,1,0:T(8,128)(2,1)}, bf16[2,128,2048]{2,1,0:T(8,128)(2,1)S(1)}, u32[]{:S(2)}) copy-start(bf16[2,128,2048]{2,1,0:T(8,128)(2,1)S(1)} %collective-permute-done.10.refs_12_) | copy-start | bytes 3145732
  57.6 41.7 %collective-permute-start.12 = (bf16[2,128,2048]{2,1,0:T(8,128)(2,1)S(1)}, bf16[2,128,2048]{2,1,0:T(8,128)(2,1)}, u32[]{:S(2)}, u32[]{:S(2)}) collective-permute-start(bf16[2,128,2048]{2,1,0:T(8,128)(2,1)S(1)} %collective-permute-done.10.refs_12_), channel_id=1, source_target_pairs={{0,48},{1,49},{2,50},{3,51},{4,52},{5,53},{6,54},{7,55},{8,56},{9,... | collective-permute-start | bytes 3145736 | tf_op jit(solution)/shard_map/ppermute | solution.py:46
  59.4 42.7 %copy-start.7 = (bf16[2,128,2048]{2,1,0:T(8,128)(2,1)}, bf16[2,128,2048]{2,1,0:T(8,128)(2,1)S(1)}, u32[]{:S(2)}) copy-start(bf16[2,128,2048]{2,1,0:T(8,128)(2,1)S(1)} %collective-permute-done.8.refs_10_) | copy-start | bytes 3145732
  59.4 40.0 %collective-permute-start.11 = (bf16[2,128,2048]{2,1,0:T(8,128)(2,1)S(1)}, bf16[2,128,2048]{2,1,0:T(8,128)(2,1)}, u32[]{:S(2)}, u32[]{:S(2)}) collective-permute-start(bf16[2,128,2048]{2,1,0:T(8,128)(2,1)S(1)} %collective-permute-done.10.refs_12_), channel_id=1, source_target_pairs={{0,16},{1,17},{2,18},{3,19},{4,20},{5,21},{6,22},{7,23},{8,24},{9,... | collective-permute-start | bytes 3145736 | tf_op jit(solution)/shard_map/ppermute | solution.py:46
  59.7 39.7 %copy-start.15 = (bf16[2,128,2048]{2,1,0:T(8,128)(2,1)}, bf16[2,128,2048]{2,1,0:T(8,128)(2,1)S(1)}, u32[]{:S(2)}) copy-start(bf16[2,128,2048]{2,1,0:T(8,128)(2,1)S(1)} %collective-permute-done.15.refs_17_) | copy-start | bytes 3145732
  59.7 48.1 %collective-permute-start.3 = (bf16[3,1024,256]{2,1,0:T(8,128)(2,1)S(1)}, bf16[3,1024,256]{2,1,0:T(8,128)(2,1)S(1)}, u32[]{:S(2)}, u32[]{:S(2)}) collective-permute-start(bf16[3,1024,256]{2,1,0:T(8,128)(2,1)S(1)} %get-tuple-element.8), channel_id=1, source_target_pairs={{0,2},{1,3},{2,4},{3,5},{4,6},{5,7},{6,0},{7,1},{8,10},{9,11},{10,... | collective-permute-start | bytes 4718600 | tf_op jit(solution)/shard_map/ppermute | solution.py:46
  63.9 38.2 %copy-start.9 = (bf16[2,128,2048]{2,1,0:T(8,128)(2,1)}, bf16[2,128,2048]{2,1,0:T(8,128)(2,1)S(1)}, u32[]{:S(2)}) copy-start(bf16[2,128,2048]{2,1,0:T(8,128)(2,1)S(1)} %collective-permute-done.9.refs_11_) | copy-start | bytes 3145732
  63.9 38.2 %collective-permute-start.17 = (bf16[2,128,2048]{2,1,0:T(8,128)(2,1)S(1)}, bf16[2,128,2048]{2,1,0:T(8,128)(2,1)S(1)}, u32[]{:S(2)}, u32[]{:S(2)}) collective-permute-start(bf16[2,128,2048]{2,1,0:T(8,128)(2,1)S(1)} %collective-permute-done.8.refs_10_), channel_id=1, source_target_pairs={{0,8},{1,9},{2,10},{3,11},{4,12},{5,13},{6,14},{7,15},{8,0},{9,1},... | collective-permute-start | bytes 3145736 | tf_op jit(solution)/shard_map/ppermute | solution.py:46
  68.9 33.3 %copy-start.13 = (bf16[3,1024,256]{2,1,0:T(8,128)(2,1)}, bf16[3,1024,256]{2,1,0:T(8,128)(2,1)S(1)}, u32[]{:S(2)}) copy-start(bf16[3,1024,256]{2,1,0:T(8,128)(2,1)S(1)} %collective-permute-done.4.refs_5_) | copy-start | bytes 4718596
  68.9 36.1 %collective-permute-start.16 = (bf16[2,128,2048]{2,1,0:T(8,128)(2,1)}, bf16[2,128,2048]{2,1,0:T(8,128)(2,1)S(1)}, u32[]{:S(2)}, u32[]{:S(2)}) collective-permute-start(bf16[2,128,2048]{2,1,0:T(8,128)(2,1)} %collective-permute-done.7.refs_9_), channel_id=1, source_target_pairs={{0,8},{1,9},{2,10},{3,11},{4,12},{5,13},{6,14},{7,15},{8,0},{9,1},... | collective-permute-start | bytes 3145736 | tf_op jit(solution)/shard_map/ppermute | solution.py:46
  99.4 8.5 %collective-permute-start.19 = (bf16[2,128,2048]{2,1,0:T(8,128)(2,1)S(1)}, bf16[2,128,2048]{2,1,0:T(8,128)(2,1)S(1)}, u32[]{:S(2)}, u32[]{:S(2)}) collective-permute-start(bf16[2,128,2048]{2,1,0:T(8,128)(2,1)S(1)} %collective-permute-done.10.refs_12_), channel_id=1, source_target_pairs={{0,8},{1,9},{2,10},{3,11},{4,12},{5,13},{6,14},{7,15},{8,0},{9,1},... | collective-permute-start | bytes 3145736 | tf_op jit(solution)/shard_map/ppermute | solution.py:46
  99.4 8.6 %collective-permute-start.18 = (bf16[2,128,2048]{2,1,0:T(8,128)(2,1)S(1)}, bf16[2,128,2048]{2,1,0:T(8,128)(2,1)S(1)}, u32[]{:S(2)}, u32[]{:S(2)}) collective-permute-start(bf16[2,128,2048]{2,1,0:T(8,128)(2,1)S(1)} %collective-permute-done.9.refs_11_), channel_id=1, source_target_pairs={{0,8},{1,9},{2,10},{3,11},{4,12},{5,13},{6,14},{7,15},{8,0},{9,1},... | collective-permute-start | bytes 3145736 | tf_op jit(solution)/shard_map/ppermute | solution.py:46
  99.9 22.8 %copy-start.20 = (s32[128,1]{0,1:T(1,128)S(1)}, s32[128,1]{0,1:T(1,128)}, u32[]{:S(2)}) copy-start(s32[128,1]{0,1:T(1,128)} %param.7) | copy-start | bytes 1540
  102.1 20.4 %copy-start.16 = (bf16[2,128,2048]{2,1,0:T(8,128)(2,1)}, bf16[2,128,2048]{2,1,0:T(8,128)(2,1)S(1)}, u32[]{:S(2)}) copy-start(bf16[2,128,2048]{2,1,0:T(8,128)(2,1)S(1)} %collective-permute-done.17.refs_19_) | copy-start | bytes 3145732
  102.2 14.3 %collective-permute-start.6 = (bf16[1,1024,256]{2,1,0:T(8,128)(2,1)S(1)}, bf16[1,1024,256]{2,1,0:T(8,128)(2,1)S(1)}, u32[]{:S(2)}, u32[]{:S(2)}) collective-permute-start(bf16[1,1024,256]{2,1,0:T(8,128)(2,1)S(1)} %slice.27), channel_id=1, source_target_pairs={{0,6},{1,7},{2,0},{3,1},{4,2},{5,3},{6,4},{7,5},{8,14},{9,15},{10,... | collective-permute-start | bytes 1572872 | tf_op jit(solution)/shard_map/ppermute | solution.py:46
  105.0 14.0 %collective-permute-start.14 = (bf16[1,128,2048]{2,1,0:T(8,128)(2,1)S(1)}, bf16[1,128,2048]{2,1,0:T(8,128)(2,1)}, u32[]{:S(2)}, u32[]{:S(2)}) collective-permute-start(bf16[1,128,2048]{2,1,0:T(8,128)(2,1)S(1)} %slice.29), channel_id=1, source_target_pairs={{0,48},{1,49},{2,50},{3,51},{4,52},{5,53},{6,54},{7,55},{8,56},{9,... | collective-permute-start | bytes 1572872 | tf_op jit(solution)/shard_map/ppermute | solution.py:46
  107.8 14.7 %collective-permute-start.13 = (bf16[1,128,2048]{2,1,0:T(8,128)(2,1)S(1)}, bf16[1,128,2048]{2,1,0:T(8,128)(2,1)}, u32[]{:S(2)}, u32[]{:S(2)}) collective-permute-start(bf16[1,128,2048]{2,1,0:T(8,128)(2,1)S(1)} %slice.28), channel_id=1, source_target_pairs={{0,16},{1,17},{2,18},{3,19},{4,20},{5,21},{6,22},{7,23},{8,24},{9,... | collective-permute-start | bytes 1572872 | tf_op jit(solution)/shard_map/ppermute | solution.py:46
  107.9 24.8 %collective-permute-start.21 = (bf16[2,128,2048]{2,1,0:T(8,128)(2,1)}, bf16[2,128,2048]{2,1,0:T(8,128)(2,1)}, u32[]{:S(2)}, u32[]{:S(2)}) collective-permute-start(bf16[2,128,2048]{2,1,0:T(8,128)(2,1)} %collective-permute-done.12.refs_14_), channel_id=1, source_target_pairs={{0,8},{1,9},{2,10},{3,11},{4,12},{5,13},{6,14},{7,15},{8,0},{9,1},... | collective-permute-start | bytes 3145736 | tf_op jit(solution)/shard_map/ppermute | solution.py:46
  108.0 24.7 %collective-permute-start.20 = (bf16[2,128,2048]{2,1,0:T(8,128)(2,1)}, bf16[2,128,2048]{2,1,0:T(8,128)(2,1)}, u32[]{:S(2)}, u32[]{:S(2)}) collective-permute-start(bf16[2,128,2048]{2,1,0:T(8,128)(2,1)} %collective-permute-done.11.refs_13_), channel_id=1, source_target_pairs={{0,8},{1,9},{2,10},{3,11},{4,12},{5,13},{6,14},{7,15},{8,0},{9,1},... | collective-permute-start | bytes 3145736 | tf_op jit(solution)/shard_map/ppermute | solution.py:46
  117.2 15.4 %collective-permute-start.5 = (bf16[1,1024,256]{2,1,0:T(8,128)(2,1)}, bf16[1,1024,256]{2,1,0:T(8,128)(2,1)}, u32[]{:S(2)}, u32[]{:S(2)}) collective-permute-start(bf16[1,1024,256]{2,1,0:T(8,128)(2,1)} %slice.26), channel_id=1, source_target_pairs={{0,2},{1,3},{2,4},{3,5},{4,6},{5,7},{6,0},{7,1},{8,10},{9,11},{10,... | collective-permute-start | bytes 1572872 | tf_op jit(solution)/shard_map/ppermute | solution.py:46
  119.0 13.7 %collective-permute-start.23 = (bf16[1,128,2048]{2,1,0:T(8,128)(2,1)}, bf16[1,128,2048]{2,1,0:T(8,128)(2,1)}, u32[]{:S(2)}, u32[]{:S(2)}) collective-permute-start(bf16[1,128,2048]{2,1,0:T(8,128)(2,1)} %collective-permute-done.14.refs_16_), channel_id=1, source_target_pairs={{0,8},{1,9},{2,10},{3,11},{4,12},{5,13},{6,14},{7,15},{8,0},{9,1},... | collective-permute-start | bytes 1572872 | tf_op jit(solution)/shard_map/ppermute | solution.py:46
  122.5 10.2 %collective-permute-start.22 = (bf16[1,128,2048]{2,1,0:T(8,128)(2,1)}, bf16[1,128,2048]{2,1,0:T(8,128)(2,1)}, u32[]{:S(2)}, u32[]{:S(2)}) collective-permute-start(bf16[1,128,2048]{2,1,0:T(8,128)(2,1)} %collective-permute-done.13.refs_15_), channel_id=1, source_target_pairs={{0,8},{1,9},{2,10},{3,11},{4,12},{5,13},{6,14},{7,15},{8,0},{9,1},... | collective-permute-start | bytes 1572872 | tf_op jit(solution)/shard_map/ppermute | solution.py:46
  (13 other events, 71.6 us)

commit v2 on v0

v2 whole, which is shorter than its diff:
```python
import jax
import jax.numpy as jnp
from jax import lax
from jax.experimental import pallas as pl
from jax.experimental.pallas import tpu as pltpu
from jax.sharding import PartitionSpec as P

TILE = 128
AXES = ("row", "col")
ROWS, COLS, DEPTH = 1024, 2048, 256
UNITS = 16
HALF = UNITS // 2
WIDE = 512
SLOTS = 256
VMEM = pl.BlockSpec(memory_space=pltpu.VMEM)
SMEM = pl.BlockSpec(memory_space=pltpu.SMEM)
ANY = pl.BlockSpec(memory_space=pl.ANY)
HBM = pl.BlockSpec(memory_space=pltpu.HBM)


def index_of(x, y, z, core):
    return ((z // 2) * 8 + y * 2 + core) * 8 + x * 2 + z % 2


def pairs(move):
    found = []
    for row in range(16):
        for col in range(8):
            place = (col // 2, (row // 2) % 4, (row // 8) * 2 + col % 2, row % 2)
            found.append((row * 8 + col, index_of(*move(*place))))
    return found


def along_x(step):
    return pairs(lambda x, y, z, core: ((x + step) % 4, y, z, core))


def along_y(step):
    return pairs(lambda x, y, z, core: (x, (y + step) % 4, z, core))


def across_z(bit):
    return pairs(lambda x, y, z, core: (x, y, z ^ bit, core))


def mate():
    return pairs(lambda x, y, z, core: (x, y, z, 1 - core))


def send(value, where):
    return lax.ppermute(value, AXES, where)


def hbm(value):
    return pltpu.with_memory_space_constraint(value, pltpu.HBM)


def vmem(value):
    return pltpu.with_memory_space_constraint(value, pltpu.VMEM)


def mask_kernel(mask_ref, a_ref, out_ref):
    for panel in range(2):
        for i in range(ROWS // TILE):
            for k in range(DEPTH // TILE):
                at = (panel, pl.ds(i * TILE, TILE), pl.ds(k * TILE, TILE))
                kept = mask_ref[(panel * 8 + i) * 2 + k] != 0
                block = a_ref[at]
                out_ref[at] = jnp.where(kept, block, jnp.zeros_like(block))


def apply_mask(amplitudes, tile_mask):
    return pl.pallas_call(
        mask_kernel,
        out_shape=jax.ShapeDtypeStruct(amplitudes.shape, amplitudes.dtype),
        in_specs=[
            pl.BlockSpec(memory_space=pltpu.SMEM),
            pl.BlockSpec(memory_space=pltpu.VMEM),
        ],
        out_specs=pl.BlockSpec(memory_space=pltpu.VMEM),
        compiler_params=pltpu.CompilerParams(vmem_limit_bytes=8 << 20),
        cost_estimate=pl.CostEstimate(flops=0, bytes_accessed=2 << 20, transcendentals=0),
    )(tile_mask.reshape(-1), amplitudes)


ORDER = (
    (0, 0, 0), (3, 0, 0), (1, 0, 0), (2, 0, 0), (0, 1, 0), (0, 0, 1), (3, 0, 1), (1, 0, 1),
    (3, 1, 0), (1, 1, 0), (2, 1, 0), (2, 0, 1), (0, 1, 1), (3, 1, 1), (1, 1, 1), (2, 1, 1),
)
CAME = ((0, 0), (0, 1), (3, 0), (1, 0), (3, 1), (1, 1), (2, 0), (2, 1))


def homes():
    row, col = lax.axis_index("row"), lax.axis_index("col")
    x, z_lo, y, z_hi, core = col // 2, col % 2, (row // 2) % 4, row // 8, row % 2
    found = []
    for dx, dz in CAME:
        chunk = ((x + dx) % 4) * 2 + jnp.bitwise_xor(z_lo, dz)
        for side in range(2):
            key = (
                jnp.bitwise_xor(chunk // 4, z_hi) * 8
                + ((chunk % 4 - y + 4) % 4) * 2
                + jnp.bitwise_xor(core, side)
            )
            found.append(sum(jnp.where(key == z * 8 + y_off * 2 + other, n, 0) for n, (y_off, z, other) in enumerate(ORDER)))
    return jnp.stack(found).astype(jnp.int32)


def multiply(left_ref, pieces, held, held_sem, use):
    def fetch(part):
        columns = pl.ds(pl.multiple_of(part * WIDE, WIDE), WIDE)
        for n, (ref, first) in enumerate(pieces):
            pltpu.make_async_copy(
                ref.at[pl.ds(first, 2), :, columns], held.at[part % 2, pl.ds(2 * n, 2)], held_sem.at[part % 2]
            ).start()

    fetch(0)

    def step(part, carry):
        @pl.when(part + 1 < COLS // WIDE)
        def _():
            fetch(part + 1)

        here = held.at[part % 2]
        pltpu.make_async_copy(here, here, held_sem.at[part % 2]).wait()
        right = held[part % 2].reshape(HALF * DEPTH, WIDE)
        use(part, jnp.dot(left_ref[...], right, preferred_element_type=jnp.float32))
        return carry

    return lambda: lax.fori_loop(0, COLS // WIDE, step, 0)


def first_kernel(home_ref, *refs):
    own_a, z_a, xm_a, xp_a, zxm_a, zxp_a, fm_a, fp_a = refs[:8]
    own_b, ym_b, yp_b, y2_b, z_b, e1_b, a_all, total_ref, held, sem, held_sem = refs[8:]
    plan = [(ref, panel, n, panel) for n, ref in enumerate((own_a, z_a, xm_a, xp_a, zxm_a, zxp_a)) for panel in range(2)]
    plan += [(fm_a, 0, 6, 0), (fp_a, 0, 6, 1), (fm_a, 1, 7, 0), (fp_a, 1, 7, 1)]
    for ref, panel_there, n, panel in plan:
        for side in range(2):
            to = pl.multiple_of(home_ref[n * 2 + side] * DEPTH + panel * TILE, TILE)
            pltpu.make_async_copy(
                ref.at[panel_there, :, pl.ds(side * TILE, TILE)], a_all.at[:, pl.ds(to, TILE)], sem
            ).start()

    def use(part, value):
        total_ref[:, pl.ds(pl.multiple_of(part * WIDE, WIDE), WIDE)] = value

    pieces = ((own_b, 0), (ym_b, 0), (yp_b, 0), (y2_b, 0), (z_b, 0), (e1_b, 0), (e1_b, 2), (e1_b, 4))
    run = multiply(a_all.at[:, pl.ds(0, HALF * DEPTH)], pieces, held, held_sem, use)
    pltpu.make_async_copy(a_all, a_all, sem).wait()
    run()


def second_kernel(slot_ref, empty_ref, *refs):
    a_all, total_ref, zym_b, zyp_b, zy2_b, e2_b, zym_m, zyp_m, zy2_m, out_ref, held, held_sem = refs

    def use(part, value):
        columns = pl.ds(pl.multiple_of(part * WIDE, WIDE), WIDE)
        total = (total_ref[:, columns] + value).astype(jnp.bfloat16)
        for i in range(ROWS // TILE):
            for j in range(WIDE // TILE):
                number = i * (COLS // TILE) + part * (WIDE // TILE) + j
                out_ref[slot_ref[number]] = total[i * TILE : (i + 1) * TILE, j * TILE : (j + 1) * TILE]
                out_ref[empty_ref[number]] = jnp.zeros((TILE, TILE), jnp.bfloat16)

    pieces = ((zym_b, 0), (zyp_b, 0), (zy2_b, 0), (e2_b, 0), (e2_b, 2), (zym_m, 0), (zyp_m, 0), (zy2_m, 0))
    multiply(a_all.at[:, pl.ds(HALF * DEPTH, HALF * DEPTH)], pieces, held, held_sem, use)()


HELD = [pltpu.VMEM((2, 2 * HALF, TILE, WIDE), jnp.bfloat16)]


def first_product(home, a_parts, b_parts):
    return pl.pallas_call(
        first_kernel,
        out_shape=(
            jax.ShapeDtypeStruct((ROWS, UNITS * DEPTH), jnp.bfloat16),
            jax.ShapeDtypeStruct((ROWS, COLS), jnp.float32),
        ),
        in_specs=[SMEM] + [HBM] * 6 + [VMEM] * 2 + [HBM] * 6,
        out_specs=(VMEM, VMEM),
        scratch_shapes=[*HELD, pltpu.SemaphoreType.DMA(()), pltpu.SemaphoreType.DMA((2,))],
        compiler_params=pltpu.CompilerParams(vmem_limit_bytes=16 << 20),
        cost_estimate=pl.CostEstimate(flops=ROWS * COLS * 4096, bytes_accessed=1 << 20, transcendentals=0),
    )(home, *[hbm(v) for v in a_parts[:6]], *[vmem(v) for v in a_parts[6:]], *[hbm(v) for v in b_parts])


def second_product(slots, empties, a_all, total, b_parts):
    return pl.pallas_call(
        second_kernel,
        out_shape=jax.ShapeDtypeStruct((SLOTS, TILE, TILE), jnp.bfloat16),
        in_specs=[SMEM] * 2 + [VMEM] * 9,
        out_specs=VMEM,
        scratch_shapes=[*HELD, pltpu.SemaphoreType.DMA((2,))],
        compiler_params=pltpu.CompilerParams(vmem_limit_bytes=16 << 20),
        cost_estimate=pl.CostEstimate(flops=ROWS * COLS * 4096, bytes_accessed=1 << 20, transcendentals=0),
    )(slots, empties, vmem(a_all), vmem(total), *[vmem(v) for v in b_parts])


def write_kernel(arrived_ref, out_ref, sem):
    for part in range(8):
        at = pl.ds(part * (SLOTS // 8), SLOTS // 8)
        pltpu.make_async_copy(arrived_ref.at[at], out_ref.at[0, at], sem).start()
    pltpu.make_async_copy(out_ref, out_ref, sem).wait()


def write_out(arrived):
    return pl.pallas_call(
        write_kernel,
        out_shape=jax.ShapeDtypeStruct((1, SLOTS, TILE, TILE), jnp.bfloat16),
        in_specs=[VMEM],
        out_specs=ANY,
        scratch_shapes=[pltpu.SemaphoreType.DMA(())],
        compiler_params=pltpu.CompilerParams(vmem_limit_bytes=12 << 20),
    )(arrived)


def after(values, earlier):
    held = lax.optimization_barrier((tuple(values), tuple(earlier)))
    return held[0], held[1]


def local(amplitudes, integrals, tile_mask, next_owner):
    owners = next_owner[:, 0]
    before = jnp.arange(TILE)[None, :] < jnp.arange(TILE)[:, None]
    rank = jnp.sum(((owners[None, :] == owners[:, None]) & before).astype(jnp.int32), axis=1)
    slots = owners * 2 + rank
    every = jnp.arange(SLOTS, dtype=jnp.int32)
    empty = jnp.logical_not(jnp.any(slots[None, :] == every[:, None], axis=1))
    below = jnp.sum((empty[None, :] & (every[None, :] < every[:, None])).astype(jnp.int32), axis=1)
    pick = empty[None, :] & (below[None, :] == every[: SLOTS // 2, None])
    empties = jnp.sum(jnp.where(pick, every[None, :], 0), axis=1)
    home = homes()

    b = integrals
    a = apply_mask(amplitudes, tile_mask)
    b_ym, b_yp = send(b, along_y(1)), send(b, along_y(-1))
    a_xm, a_xp, a_z = send(a, along_x(1)), send(a, along_x(-1)), send(a, across_z(1))
    (b, a), (b_ym, b_yp, a_xm, a_xp, a_z) = after((b, a), (b_ym, b_yp, a_xm, a_xp, a_z))
    a_zxm, a_zxp = send(a_z, along_x(1)), send(a_z, along_x(-1))
    b_z, b_y2 = send(b, across_z(2)), send(b, along_y(2))
    e1 = send(jnp.concatenate([b, b_ym, b_yp], axis=0), mate())
    from_m = jnp.concatenate([a_xm[:1], a_zxm[:1]], axis=0)
    from_p = jnp.concatenate([a_xp[1:], a_zxp[1:]], axis=0)
    (from_m, from_p, b_z, b_y2), (a_xm, a_xp, a_zxm, a_zxp, e1, slots, empties, home) = after(
        (from_m, from_p, b_z, b_y2), (a_xm, a_xp, a_zxm, a_zxp, e1, slots, empties, home)
    )
    a_fm, a_fp = send(from_m, along_x(1)), send(from_p, along_x(-1))
    b_zym, b_zyp, b_zy2 = send(b_z, along_y(1)), send(b_z, along_y(-1)), send(b_y2, across_z(2))
    e2 = jnp.concatenate([b_y2, b_z], axis=0)
    (b_zym, b_zyp, b_zy2, e2), (a_fm, a_fp) = after((b_zym, b_zyp, b_zy2, e2), (a_fm, a_fp))
    late = (b_zym, b_zyp, b_zy2, *(send(v, mate()) for v in (e2, b_zym, b_zyp, b_zy2)))

    a_all, total = first_product(
        home, (a, a_z, a_xm, a_xp, a_zxm, a_zxp, a_fm, a_fp), (b, b_ym, b_yp, b_y2, b_z, e1)
    )
    outgoing = second_product(slots, empties, a_all, total, late)
    arrived = lax.all_to_all(outgoing, AXES, split_axis=0, concat_axis=0, tiled=True)
    return write_out(arrived)


def solution(mesh):
    return jax.shard_map(
        local,
        mesh=mesh,
        in_specs=(
            P(None, "row", "col"),
            P(None, "row", "col"),
            P(None, "row", "col"),
            P(AXES, None),
        ),
        out_specs=P(AXES, None, None, None),
        check_vma=False,
    )
```

time: 517 us -> 233 us (0.45)
  waiting for transfers between devices: 324 us -> 63 us
  local copies, waits for them, and re-layouts: 45.7 us -> 5.49 us
  Pallas kernels: 0 us -> 28.4 us
  matrix products: 28.2 us -> 0 us
  starting transfers between devices: 0.31 us -> 27.1 us
  between operations: 13.2 us -> 1.57 us
    all_gather x4 -> x0, waiting for transfers between devices: 323 us -> none  [the longest x2 166 us: local(): lax.all_gather(masked[panel_step], 'col', axis=1, tiled=True)]
    ppermute x0 -> x19, waiting for transfers between devices: none -> 63 us  [send(): return lax.ppermute(value, AXES, where)]
    pallas_call x0 -> x4, Pallas kernels: none -> 28.4 us  [the longest x1 13.4 us: first_product(): pl.pallas_call(first_kernel, out_shape=(jax.ShapeDtypeStruct((ROWS, UNITS...]
    dot_general x2 -> x0, matrix products: 28.2 us -> none  [local(): jnp.dot(lax.all_gather(masked[panel_step], 'col', axis=1, tiled=True), ga...]
    ppermute x0 -> x19, starting transfers between devices: none -> 27.1 us  [send(): return lax.ppermute(value, AXES, where)]
    scatter x1 -> x0, local copies, waits for them, and re-layouts: 19.3 us -> none  [local(): jnp.zeros((devices * capacity, TILE, TILE), jnp.bfloat16).at[slot_index]]
    unnamed x8 -> x17, local copies, waits for them, and re-layouts: 13.7 us -> 2.01 us
    broadcast_in_dim x1 -> x0, local copies, waits for them, and re-layouts: 5.52 us -> none  [local(): jnp.zeros((devices * capacity, TILE, TILE), jnp.bfloat16).at[slot_index]]
  transfers between devices with their start and end apart: 4 -> 19, of which waited for: 4 -> 11; matrix products, arithmetic and copies ran while one was open for 3% -> 3% of each run, Pallas kernels for 0% -> 6%
where the time goes in v2:
time: 233 us
  blocking collectives  101 us (43%)
  waiting for transfers between devices  63 us (27%)
  Pallas kernels  28.4 us (12%)
  starting transfers between devices  27.1 us (12%)
  other arithmetic  5.84 us (3%)
  local copies, waits for them, and re-layouts  5.49 us (2%)
    all_to_all x1, blocking collectives, local(): lax.all_to_all(outgoing, AXES, split_axis=0, concat_axis=0, tiled=True)  101 us
    ppermute x19, waiting for transfers between devices, send(): return lax.ppermute(value, AXES, where)  63 us
    ppermute x19, starting transfers between devices, send(): return lax.ppermute(value, AXES, where)  27.1 us
    pallas_call x1, Pallas kernels, first_product(): pl.pallas_call(first_kernel, out_shape=(jax.ShapeDtypeStruct((ROWS, UNITS...  13.4 us
    pallas_call x1, Pallas kernels, second_product(): pl.pallas_call(second_kernel, out_shape=jax.ShapeDtypeStruct((SLOTS, TILE...  10.9 us
  transfers between devices with their start and end apart: 19, of which 11 were waited for; matrix products, arithmetic and copies ran while one was open for 3% of the time, Pallas kernels for 6%

profile of v2, /device:TPU:0, one launch (start us, length us, event | category | flops | bytes accessed | tf_op | source)
XLA Modules:
  0.0 232.8 jit_solution(3961924074317814225)
XLA Ops:
  0.0 0.8 copy.7
  0.9 1.2 copy-done
  2.1 0.8 shard_map.46.refs_0_
  2.9 2.1 collective-permute-start.4
  5.0 2.8 %collective-permute-start.3 = (bf16[2,1024,256]{2,1,0:T(8,128)(2,1)S(1)}, bf16[2,1024,256]{2,1,0:T(8,128)(2,1)S(1)}, u32[]{:S(2)}, u32[]{:S(2)}) collective-permute-start(bf16[2,1024,256]{2,1,0:T(8,128)(2,1)S(1)} %shard_map.46.refs_0_), channel_id=1, source_target_pairs={{0,6},{1,7},{2,0},{3,1},{4,2},{5,3},{6,4},{7,5},{8,14},{9,15},{10,... | collective-permute-start | bytes 3145736 | tf_op jit(solution)/shard_map/ppermute | solution.py:51
  7.7 1.6 collective-permute-start
  9.3 1.7 collective-permute-start.1
  11.0 17.3 %collective-permute-done.4.refs_1_ = bf16[2,1024,256]{2,1,0:T(8,128)(2,1)} collective-permute-done((bf16[2,1024,256]{2,1,0:T(8,128)(2,1)S(1)}, bf16[2,1024,256]{2,1,0:T(8,128)(2,1)}, u32[]{:S(2)}, u32[]{:S(2)}) %collective-permute-start.4) | collective-permute-done | bytes 1048608 | tf_op jit(solution)/shard_map/ppermute | solution.py:51
  28.2 1.6 collective-permute-done.3.refs_3_
  29.9 3.4 %collective-permute-done.2.refs_2_ = bf16[2,1024,256]{2,1,0:T(8,128)(2,1)S(1)} collective-permute-done((bf16[2,1024,256]{2,1,0:T(8,128)(2,1)S(1)}, bf16[2,1024,256]{2,1,0:T(8,128)(2,1)S(1)}, u32[]{:S(2)}, u32[]{:S(2)}) %collective-permute-start.2) | collective-permute-done | bytes 1048608 | tf_op jit(solution)/shard_map/ppermute | solution.py:51
  33.6 3.3 %pad_maximum_fusion = bf16[6,128,2048]{2,1,0:T(8,128)(2,1)} fusion(bf16[2,128,2048]{2,1,0:T(8,128)(2,1)S(1)} %collective-permute-done.1.refs_10_, bf16[2,128,2048]{2,1,0:T(8,128)(2,1)S(1)} %collective-permute-done.refs_9_, bf16[2,128,2048]{2,1,0:T(8,128)(2,1)} %refs_8_), kind=kLoop, calls=%fused_computation | loop fusion | flops 3145728 | bytes 6291456 | tf_op jit(solution)/shard_map/concatenate | solution.py:242
  37.0 3.0 %collective-permute-start.6 = (bf16[2,1024,256]{2,1,0:T(8,128)(2,1)}, bf16[2,1024,256]{2,1,0:T(8,128)(2,1)}, u32[]{:S(2)}, u32[]{:S(2)}) collective-permute-start(bf16[2,1024,256]{2,1,0:T(8,128)(2,1)} %collective-permute-done.4.refs_1_), channel_id=1, source_target_pairs={{0,6},{1,7},{2,0},{3,1},{4,2},{5,3},{6,4},{7,5},{8,14},{9,15},{10,... | collective-permute-start | bytes 3145736 | tf_op jit(solution)/shard_map/ppermute | solution.py:51
  40.0 2.9 %collective-permute-start.8 = (bf16[2,128,2048]{2,1,0:T(8,128)(2,1)S(1)}, bf16[2,128,2048]{2,1,0:T(8,128)(2,1)}, u32[]{:S(2)}, u32[]{:S(2)}) collective-permute-start(bf16[2,128,2048]{2,1,0:T(8,128)(2,1)S(1)} %copy-done.3), channel_id=1, source_target_pairs={{0,32},{1,33},{2,34},{3,35},{4,36},{5,37},{6,38},{7,39},{8,40},{9,... | collective-permute-start | bytes 3145736 | tf_op jit(solution)/shard_map/ppermute | solution.py:51
  42.9 3.6 %collective-permute-start.7 = (bf16[2,128,2048]{2,1,0:T(8,128)(2,1)S(1)}, bf16[2,128,2048]{2,1,0:T(8,128)(2,1)}, u32[]{:S(2)}, u32[]{:S(2)}) collective-permute-start(bf16[2,128,2048]{2,1,0:T(8,128)(2,1)S(1)} %copy-done.3), channel_id=1, source_target_pairs={{0,64},{1,65},{2,66},{3,67},{4,68},{5,69},{6,70},{7,71},{8,72},{9,... | collective-permute-start | bytes 3145736 | tf_op jit(solution)/shard_map/ppermute | solution.py:51
  48.4 1.1 slice.17
  49.5 13.8 %collective-permute-done.6.refs_5_ = bf16[2,1024,256]{2,1,0:T(8,128)(2,1)} collective-permute-done((bf16[2,1024,256]{2,1,0:T(8,128)(2,1)}, bf16[2,1024,256]{2,1,0:T(8,128)(2,1)}, u32[]{:S(2)}, u32[]{:S(2)}) %collective-permute-start.6) | collective-permute-done | bytes 1048608 | tf_op jit(solution)/shard_map/ppermute | solution.py:51
  63.3 1.1 slice.21
  64.4 2.3 %collective-permute-done.5.refs_4_ = bf16[2,1024,256]{2,1,0:T(8,128)(2,1)} collective-permute-done((bf16[2,1024,256]{2,1,0:T(8,128)(2,1)}, bf16[2,1024,256]{2,1,0:T(8,128)(2,1)}, u32[]{:S(2)}, u32[]{:S(2)}) %collective-permute-start.5) | collective-permute-done | bytes 1048608 | tf_op jit(solution)/shard_map/ppermute | solution.py:51
  66.7 1.1 slice.20
  68.1 1.7 collective-permute-done.7.refs_12_
  69.8 3.2 %collective-permute-start.14 = (bf16[2,1024,256]{2,1,0:T(8,128)(2,1)S(1)}, bf16[2,1024,256]{2,1,0:T(8,128)(2,1)S(1)}, u32[]{:S(2)}, u32[]{:S(2)}) collective-permute-start(bf16[2,1024,256]{2,1,0:T(8,128)(2,1)S(1)} %pad_maximum_fusion.3), channel_id=1, source_target_pairs={{0,6},{1,7},{2,0},{3,1},{4,2},{5,3},{6,4},{7,5},{8,14},{9,15},{10,... | collective-permute-start | bytes 3145736 | tf_op jit(solution)/shard_map/ppermute | solution.py:51
  73.0 3.2 %collective-permute-start.12 = (bf16[2,128,2048]{2,1,0:T(8,128)(2,1)}, bf16[2,128,2048]{2,1,0:T(8,128)(2,1)S(1)}, u32[]{:S(2)}, u32[]{:S(2)}) collective-permute-start(bf16[2,128,2048]{2,1,0:T(8,128)(2,1)} %collective-permute-done.8.refs_11_), channel_id=1, source_target_pairs={{0,64},{1,65},{2,66},{3,67},{4,68},{5,69},{6,70},{7,71},{8,72},{9,... | collective-permute-start | bytes 3145736 | tf_op jit(solution)/shard_map/ppermute | solution.py:51
  76.2 1.6 collective-permute-start.11
  78.3 1.7 pad_maximum_fusion.1
  80.0 15.4 %collective-permute-done.13.refs_6_ = bf16[2,1024,256]{2,1,0:T(8,128)(2,1)S(1)} collective-permute-done((bf16[2,1024,256]{2,1,0:T(8,128)(2,1)S(1)}, bf16[2,1024,256]{2,1,0:T(8,128)(2,1)S(1)}, u32[]{:S(2)}, u32[]{:S(2)}) %collective-permute-start.13) | collective-permute-done | bytes 1048608 | tf_op jit(solution)/shard_map/ppermute | solution.py:51
  95.4 3.2 %collective-permute-done.12.refs_4_ = bf16[2,128,2048]{2,1,0:T(8,128)(2,1)S(1)} collective-permute-done((bf16[2,128,2048]{2,1,0:T(8,128)(2,1)}, bf16[2,128,2048]{2,1,0:T(8,128)(2,1)S(1)}, u32[]{:S(2)}, u32[]{:S(2)}) %collective-permute-start.12) | collective-permute-done | bytes 1048608 | tf_op jit(solution)/shard_map/ppermute | solution.py:51
  98.5 1.1 collective-permute-done.11.refs_3_
  99.7 2.9 %collective-permute-done.10.refs_2_ = bf16[2,128,2048]{2,1,0:T(8,128)(2,1)S(1)} collective-permute-done((bf16[2,128,2048]{2,1,0:T(8,128)(2,1)}, bf16[2,128,2048]{2,1,0:T(8,128)(2,1)S(1)}, u32[]{:S(2)}, u32[]{:S(2)}) %collective-permute-start.10) | collective-permute-done | bytes 1048608 | tf_op jit(solution)/shard_map/ppermute | solution.py:51
  103.6 13.4 %shard_map.47 = (bf16[1024,4096]{1,0:T(8,128)(2,1)S(1)}, f32[1024,2048]{1,0:T(8,128)S(1)}) custom-call(s32[16]{0:T(128)S(1)} %stack.67.home_ref, bf16[2,1024,256]{2,1,0:T(8,128)(2,1)} %copy-done.1, bf16[2,1024,256]{2,1,0:T(8,128)(2,1)} %collective-permute-done.4.refs_1_, bf16[2,1024,256]{2,1,0:T(8,128)(2,1)} %copy-done.2, bf16[2,1024,256]{2,1,0:T(8,128)(2,1)} %copy-done.6, ...), custom_call_target="tpu_custom_call" | custom-call | flops 8589934592 | bytes 1048576 | tf_op jit(solution)/shard_map/pallas_call | solution.py:174
  117.1 10.9 %shard_map.48 = bf16[256,128,128]{2,1,0:T(8,128)(2,1)S(1)} custom-call(s32[128]{0:T(128)S(1)} %multiply_add_fusion.slot_ref, s32[128]{0:T(128)S(1)} %select_reduce_fusion.empty_ref, bf16[1024,4096]{1,0:T(8,128)(2,1)S(1)} %get-tuple-element.53.refs_0_, f32[1024,2048]{1,0:T(8,128)S(1)} %get-tuple-element.54.refs_1_, ...), custom_call_target="tpu_custom_call" | custom-call | flops 8589934592 | bytes 1048576 | tf_op jit(solution)/shard_map/pallas_call | solution.py:189
  128.0 101.4 %all_to_all.5.arrived_ref = bf16[256,128,128]{2,1,0:T(8,128)(2,1)S(1)} all-to-all(bf16[256,128,128]{2,1,0:T(8,128)(2,1)S(1)} %shard_map.48), channel_id=1, replica_groups=mesh['row'=16,'col'=8] {'row','col'}, dimensions={0} | all-to-all | bytes 16777216 | tf_op jit(solution)/shard_map/all_to_all | solution.py:258
  229.4 3.3 %shard_map.49 = bf16[1,256,128,128]{3,2,1,0:T(8,128)(2,1)} custom-call(bf16[256,128,128]{2,1,0:T(8,128)(2,1)S(1)} %all_to_all.5.arrived_ref), custom_call_target="tpu_custom_call" | custom-call | tf_op jit(solution)/shard_map/pallas_call | solution.py:208
  (47 shorter events, 2.9 us)
Async XLA Ops:
  0.9 1.2 copy-start
  2.9 34.0 %copy-start.1 = (bf16[2,1024,256]{2,1,0:T(8,128)(2,1)}, bf16[2,1024,256]{2,1,0:T(8,128)(2,1)S(1)}, u32[]{:S(2)}) copy-start(bf16[2,1024,256]{2,1,0:T(8,128)(2,1)S(1)} %shard_map.46.refs_0_) | copy-start | bytes 3145732
  2.9 37.1 %copy-start.3 = (bf16[2,128,2048]{2,1,0:T(8,128)(2,1)S(1)}, bf16[2,128,2048]{2,1,0:T(8,128)(2,1)}, u32[]{:S(2)}) copy-start(bf16[2,128,2048]{2,1,0:T(8,128)(2,1)} %refs_8_) | copy-start | bytes 3145732
  2.9 43.6 %copy-start.7 = (s32[128,1]{0,1:T(1,128)S(1)}, s32[128,1]{0,1:T(1,128)}, u32[]{:S(2)}) copy-start(s32[128,1]{0,1:T(1,128)} %param.7) | copy-start | bytes 1540
  2.9 25.3 %collective-permute-start.4 = (bf16[2,1024,256]{2,1,0:T(8,128)(2,1)S(1)}, bf16[2,1024,256]{2,1,0:T(8,128)(2,1)}, u32[]{:S(2)}, u32[]{:S(2)}) collective-permute-start(bf16[2,1024,256]{2,1,0:T(8,128)(2,1)S(1)} %shard_map.46.refs_0_), channel_id=1, source_target_pairs={{0,1},{1,0},{2,3},{3,2},{4,5},{5,4},{6,7},{7,6},{8,9},{9,8},{10,11... | collective-permute-start | bytes 3145736 | tf_op jit(solution)/shard_map/ppermute | solution.py:51
  5.0 24.9 %collective-permute-start.3 = (bf16[2,1024,256]{2,1,0:T(8,128)(2,1)S(1)}, bf16[2,1024,256]{2,1,0:T(8,128)(2,1)S(1)}, u32[]{:S(2)}, u32[]{:S(2)}) collective-permute-start(bf16[2,1024,256]{2,1,0:T(8,128)(2,1)S(1)} %shard_map.46.refs_0_), channel_id=1, source_target_pairs={{0,6},{1,7},{2,0},{3,1},{4,2},{5,3},{6,4},{7,5},{8,14},{9,15},{10,... | collective-permute-start | bytes 3145736 | tf_op jit(solution)/shard_map/ppermute | solution.py:51
  7.7 25.5 %collective-permute-start.2 = (bf16[2,1024,256]{2,1,0:T(8,128)(2,1)S(1)}, bf16[2,1024,256]{2,1,0:T(8,128)(2,1)S(1)}, u32[]{:S(2)}, u32[]{:S(2)}) collective-permute-start(bf16[2,1024,256]{2,1,0:T(8,128)(2,1)S(1)} %shard_map.46.refs_0_), channel_id=1, source_target_pairs={{0,2},{1,3},{2,4},{3,5},{4,6},{5,7},{6,0},{7,1},{8,10},{9,11},{10,... | collective-permute-start | bytes 3145736 | tf_op jit(solution)/shard_map/ppermute | solution.py:51
  7.7 25.8 %collective-permute-start = (bf16[2,128,2048]{2,1,0:T(8,128)(2,1)}, bf16[2,128,2048]{2,1,0:T(8,128)(2,1)S(1)}, u32[]{:S(2)}, u32[]{:S(2)}) collective-permute-start(bf16[2,128,2048]{2,1,0:T(8,128)(2,1)} %refs_8_), channel_id=1, source_target_pairs={{0,16},{1,17},{2,18},{3,19},{4,20},{5,21},{6,22},{7,23},{8,24},{9,... | collective-permute-start | bytes 3145736 | tf_op jit(solution)/shard_map/ppermute | solution.py:51
  9.3 24.3 %collective-permute-start.1 = (bf16[2,128,2048]{2,1,0:T(8,128)(2,1)}, bf16[2,128,2048]{2,1,0:T(8,128)(2,1)S(1)}, u32[]{:S(2)}, u32[]{:S(2)}) collective-permute-start(bf16[2,128,2048]{2,1,0:T(8,128)(2,1)} %refs_8_), channel_id=1, source_target_pairs={{0,48},{1,49},{2,50},{3,51},{4,52},{5,53},{6,54},{7,55},{8,56},{9,... | collective-permute-start | bytes 3145736 | tf_op jit(solution)/shard_map/ppermute | solution.py:51
  29.9 3.7 %copy-start.6 = (bf16[2,1024,256]{2,1,0:T(8,128)(2,1)}, bf16[2,1024,256]{2,1,0:T(8,128)(2,1)S(1)}, u32[]{:S(2)}) copy-start(bf16[2,1024,256]{2,1,0:T(8,128)(2,1)S(1)} %collective-permute-done.3.refs_3_) | copy-start | bytes 3145732
  33.3 15.1 %copy-start.2 = (bf16[2,1024,256]{2,1,0:T(8,128)(2,1)}, bf16[2,1024,256]{2,1,0:T(8,128)(2,1)S(1)}, u32[]{:S(2)}) copy-start(bf16[2,1024,256]{2,1,0:T(8,128)(2,1)S(1)} %collective-permute-done.2.refs_2_) | copy-start | bytes 3145732
  33.6 3.3 %copy-start.4 = (bf16[2,128,2048]{2,1,0:T(8,128)(2,1)}, bf16[2,128,2048]{2,1,0:T(8,128)(2,1)S(1)}, u32[]{:S(2)}) copy-start(bf16[2,128,2048]{2,1,0:T(8,128)(2,1)S(1)} %collective-permute-done.refs_9_) | copy-start | bytes 3145732
  33.6 3.3 %copy-start.5 = (bf16[2,128,2048]{2,1,0:T(8,128)(2,1)}, bf16[2,128,2048]{2,1,0:T(8,128)(2,1)S(1)}, u32[]{:S(2)}) copy-start(bf16[2,128,2048]{2,1,0:T(8,128)(2,1)S(1)} %collective-permute-done.1.refs_10_) | copy-start | bytes 3145732
  36.9 32.8 %collective-permute-start.9 = (bf16[6,128,2048]{2,1,0:T(8,128)(2,1)}, bf16[6,128,2048]{2,1,0:T(8,128)(2,1)}, u32[]{:S(2)}, u32[]{:S(2)}) collective-permute-start(bf16[6,128,2048]{2,1,0:T(8,128)(2,1)} %pad_maximum_fusion), channel_id=1, source_target_pairs={{0,8},{1,9},{2,10},{3,11},{4,12},{5,13},{6,14},{7,15},{8,0},{9,1},... | collective-permute-start | bytes 9437192 | tf_op jit(solution)/shard_map/ppermute | solution.py:51
  37.0 26.3 %collective-permute-start.6 = (bf16[2,1024,256]{2,1,0:T(8,128)(2,1)}, bf16[2,1024,256]{2,1,0:T(8,128)(2,1)}, u32[]{:S(2)}, u32[]{:S(2)}) collective-permute-start(bf16[2,1024,256]{2,1,0:T(8,128)(2,1)} %collective-permute-done.4.refs_1_), channel_id=1, source_target_pairs={{0,6},{1,7},{2,0},{3,1},{4,2},{5,3},{6,4},{7,5},{8,14},{9,15},{10,... | collective-permute-start | bytes 3145736 | tf_op jit(solution)/shard_map/ppermute | solution.py:51
  40.0 26.8 %collective-permute-start.5 = (bf16[2,1024,256]{2,1,0:T(8,128)(2,1)}, bf16[2,1024,256]{2,1,0:T(8,128)(2,1)}, u32[]{:S(2)}, u32[]{:S(2)}) collective-permute-start(bf16[2,1024,256]{2,1,0:T(8,128)(2,1)} %collective-permute-done.4.refs_1_), channel_id=1, source_target_pairs={{0,2},{1,3},{2,4},{3,5},{4,6},{5,7},{6,0},{7,1},{8,10},{9,11},{10,... | collective-permute-start | bytes 3145736 | tf_op jit(solution)/shard_map/ppermute | solution.py:51
  40.0 28.1 %collective-permute-start.8 = (bf16[2,128,2048]{2,1,0:T(8,128)(2,1)S(1)}, bf16[2,128,2048]{2,1,0:T(8,128)(2,1)}, u32[]{:S(2)}, u32[]{:S(2)}) collective-permute-start(bf16[2,128,2048]{2,1,0:T(8,128)(2,1)S(1)} %copy-done.3), channel_id=1, source_target_pairs={{0,32},{1,33},{2,34},{3,35},{4,36},{5,37},{6,38},{7,39},{8,40},{9,... | collective-permute-start | bytes 3145736 | tf_op jit(solution)/shard_map/ppermute | solution.py:51
  42.9 26.9 %collective-permute-start.7 = (bf16[2,128,2048]{2,1,0:T(8,128)(2,1)S(1)}, bf16[2,128,2048]{2,1,0:T(8,128)(2,1)}, u32[]{:S(2)}, u32[]{:S(2)}) collective-permute-start(bf16[2,128,2048]{2,1,0:T(8,128)(2,1)S(1)} %copy-done.3), channel_id=1, source_target_pairs={{0,64},{1,65},{2,66},{3,67},{4,68},{5,69},{6,70},{7,71},{8,72},{9,... | collective-permute-start | bytes 3145736 | tf_op jit(solution)/shard_map/ppermute | solution.py:51
  48.4 19.6 %slice-start = ((bf16[2,1024,256]{2,1,0:T(8,128)(2,1)}), bf16[1,1024,256]{2,1,0:T(8,128)(2,1)S(1)}, s32[]{:S(2)}) async-start(bf16[2,1024,256]{2,1,0:T(8,128)(2,1)} %copy-done.2), calls=%async_computation.1 | async-start | bytes 1048576 | tf_op jit(solution)/shard_map/slice | solution.py:243
  69.8 25.6 %collective-permute-start.13 = (bf16[2,1024,256]{2,1,0:T(8,128)(2,1)S(1)}, bf16[2,1024,256]{2,1,0:T(8,128)(2,1)S(1)}, u32[]{:S(2)}, u32[]{:S(2)}) collective-permute-start(bf16[2,1024,256]{2,1,0:T(8,128)(2,1)S(1)} %pad_maximum_fusion.2), channel_id=1, source_target_pairs={{0,2},{1,3},{2,4},{3,5},{4,6},{5,7},{6,0},{7,1},{8,10},{9,11},{10,... | collective-permute-start | bytes 3145736 | tf_op jit(solution)/shard_map/ppermute | solution.py:51
  69.8 25.6 %collective-permute-start.14 = (bf16[2,1024,256]{2,1,0:T(8,128)(2,1)S(1)}, bf16[2,1024,256]{2,1,0:T(8,128)(2,1)S(1)}, u32[]{:S(2)}, u32[]{:S(2)}) collective-permute-start(bf16[2,1024,256]{2,1,0:T(8,128)(2,1)S(1)} %pad_maximum_fusion.3), channel_id=1, source_target_pairs={{0,6},{1,7},{2,0},{3,1},{4,2},{5,3},{6,4},{7,5},{8,14},{9,15},{10,... | collective-permute-start | bytes 3145736 | tf_op jit(solution)/shard_map/ppermute | solution.py:51
  73.0 25.5 %collective-permute-start.12 = (bf16[2,128,2048]{2,1,0:T(8,128)(2,1)}, bf16[2,128,2048]{2,1,0:T(8,128)(2,1)S(1)}, u32[]{:S(2)}, u32[]{:S(2)}) collective-permute-start(bf16[2,128,2048]{2,1,0:T(8,128)(2,1)} %collective-permute-done.8.refs_11_), channel_id=1, source_target_pairs={{0,64},{1,65},{2,66},{3,67},{4,68},{5,69},{6,70},{7,71},{8,72},{9,... | collective-permute-start | bytes 3145736 | tf_op jit(solution)/shard_map/ppermute | solution.py:51
  76.2 23.4 %collective-permute-start.11 = (bf16[2,128,2048]{2,1,0:T(8,128)(2,1)}, bf16[2,128,2048]{2,1,0:T(8,128)(2,1)S(1)}, u32[]{:S(2)}, u32[]{:S(2)}) collective-permute-start(bf16[2,128,2048]{2,1,0:T(8,128)(2,1)} %collective-permute-done.7.refs_12_), channel_id=1, source_target_pairs={{0,48},{1,49},{2,50},{3,51},{4,52},{5,53},{6,54},{7,55},{8,56},{9,... | collective-permute-start | bytes 3145736 | tf_op jit(solution)/shard_map/ppermute | solution.py:51
  77.9 24.7 %collective-permute-start.10 = (bf16[2,128,2048]{2,1,0:T(8,128)(2,1)}, bf16[2,128,2048]{2,1,0:T(8,128)(2,1)S(1)}, u32[]{:S(2)}, u32[]{:S(2)}) collective-permute-start(bf16[2,128,2048]{2,1,0:T(8,128)(2,1)} %collective-permute-done.7.refs_12_), channel_id=1, source_target_pairs={{0,16},{1,17},{2,18},{3,19},{4,20},{5,21},{6,22},{7,23},{8,24},{9,... | collective-permute-start | bytes 3145736 | tf_op jit(solution)/shard_map/ppermute | solution.py:51
  102.6 14.5 %collective-permute-start.15 = (bf16[4,128,2048]{2,1,0:T(8,128)(2,1)S(1)}, bf16[4,128,2048]{2,1,0:T(8,128)(2,1)S(1)}, u32[]{:S(2)}, u32[]{:S(2)}) collective-permute-start(bf16[4,128,2048]{2,1,0:T(8,128)(2,1)S(1)} %pad_maximum_fusion.1), channel_id=1, source_target_pairs={{0,8},{1,9},{2,10},{3,11},{4,12},{5,13},{6,14},{7,15},{8,0},{9,1},... | collective-permute-start | bytes 6291464 | tf_op jit(solution)/shard_map/ppermute | solution.py:51
  102.6 14.5 %collective-permute-start.16 = (bf16[2,128,2048]{2,1,0:T(8,128)(2,1)S(1)}, bf16[2,128,2048]{2,1,0:T(8,128)(2,1)S(1)}, u32[]{:S(2)}, u32[]{:S(2)}) collective-permute-start(bf16[2,128,2048]{2,1,0:T(8,128)(2,1)S(1)} %collective-permute-done.10.refs_2_), channel_id=1, source_target_pairs={{0,8},{1,9},{2,10},{3,11},{4,12},{5,13},{6,14},{7,15},{8,0},{9,1},... | collective-permute-start | bytes 3145736 | tf_op jit(solution)/shard_map/ppermute | solution.py:51
  103.1 14.0 %collective-permute-start.17 = (bf16[2,128,2048]{2,1,0:T(8,128)(2,1)S(1)}, bf16[2,128,2048]{2,1,0:T(8,128)(2,1)S(1)}, u32[]{:S(2)}, u32[]{:S(2)}) collective-permute-start(bf16[2,128,2048]{2,1,0:T(8,128)(2,1)S(1)} %collective-permute-done.11.refs_3_), channel_id=1, source_target_pairs={{0,8},{1,9},{2,10},{3,11},{4,12},{5,13},{6,14},{7,15},{8,0},{9,1},... | collective-permute-start | bytes 3145736 | tf_op jit(solution)/shard_map/ppermute | solution.py:51
  103.1 14.0 %collective-permute-start.18 = (bf16[2,128,2048]{2,1,0:T(8,128)(2,1)S(1)}, bf16[2,128,2048]{2,1,0:T(8,128)(2,1)S(1)}, u32[]{:S(2)}, u32[]{:S(2)}) collective-permute-start(bf16[2,128,2048]{2,1,0:T(8,128)(2,1)S(1)} %collective-permute-done.12.refs_4_), channel_id=1, source_target_pairs={{0,8},{1,9},{2,10},{3,11},{4,12},{5,13},{6,14},{7,15},{8,0},{9,1},... | collective-permute-start | bytes 3145736 | tf_op jit(solution)/shard_map/ppermute | solution.py:51

commit v3 on v2

v3 whole, which is shorter than its diff:
```python
import functools

import jax
import jax.numpy as jnp
from jax import lax
from jax.experimental import pallas as pl
from jax.experimental.pallas import tpu as pltpu
from jax.sharding import PartitionSpec as P

TILE = 128
AXES = ("row", "col")
ROWS, COLS, DEPTH = 1024, 2048, 256
UNITS = 16
WIDE = 512
SLOTS = 256
VMEM = pl.BlockSpec(memory_space=pltpu.VMEM)
SMEM = pl.BlockSpec(memory_space=pltpu.SMEM)
ANY = pl.BlockSpec(memory_space=pl.ANY)
HBM = pl.BlockSpec(memory_space=pltpu.HBM)


def index_of(x, y, z, core):
    return ((z // 2) * 8 + y * 2 + core) * 8 + x * 2 + z % 2


def pairs(move):
    found = []
    for row in range(16):
        for col in range(8):
            place = (col // 2, (row // 2) % 4, (row // 8) * 2 + col % 2, row % 2)
            found.append((row * 8 + col, index_of(*move(*place))))
    return found


def along_x(step):
    return pairs(lambda x, y, z, core: ((x + step) % 4, y, z, core))


def along_y(step):
    return pairs(lambda x, y, z, core: (x, (y + step) % 4, z, core))


def across_z(bit):
    return pairs(lambda x, y, z, core: (x, y, z ^ bit, core))


def mate():
    return pairs(lambda x, y, z, core: (x, y, z, 1 - core))


def send(value, where):
    return lax.ppermute(value, AXES, where)


def hbm(value):
    return pltpu.with_memory_space_constraint(value, pltpu.HBM)


def vmem(value):
    return pltpu.with_memory_space_constraint(value, pltpu.VMEM)


def mask_kernel(mask_ref, a_ref, out_ref):
    for panel in range(2):
        for i in range(ROWS // TILE):
            for k in range(DEPTH // TILE):
                at = (panel, pl.ds(i * TILE, TILE), pl.ds(k * TILE, TILE))
                kept = mask_ref[(panel * 8 + i) * 2 + k] != 0
                block = a_ref[at]
                out_ref[at] = jnp.where(kept, block, jnp.zeros_like(block))


def apply_mask(amplitudes, tile_mask):
    return pl.pallas_call(
        mask_kernel,
        out_shape=jax.ShapeDtypeStruct(amplitudes.shape, amplitudes.dtype),
        in_specs=[
            pl.BlockSpec(memory_space=pltpu.SMEM),
            pl.BlockSpec(memory_space=pltpu.VMEM),
        ],
        out_specs=pl.BlockSpec(memory_space=pltpu.VMEM),
        compiler_params=pltpu.CompilerParams(vmem_limit_bytes=8 << 20),
        cost_estimate=pl.CostEstimate(flops=0, bytes_accessed=2 << 20, transcendentals=0),
    )(tile_mask.reshape(-1), amplitudes)


CAME = ((0, 0), (0, 1), (3, 0), (1, 0), (3, 1), (1, 1), (2, 0), (2, 1))
LAST = (6, 7)


def unit_of(n, side):
    row, col = lax.axis_index("row"), lax.axis_index("col")
    dx, dz = CAME[n]
    chunk = ((col // 2 + dx) % 4) * 2 + jnp.bitwise_xor(col % 2, dz)
    across = jnp.bitwise_xor(chunk // 4, row // 8)
    along = (chunk % 4 - (row // 2) % 4 + 4) % 4
    return jnp.bitwise_xor(row % 2, side) * 8 + across * 4 + along


def comes_last(unit):
    found = [unit_of(n, side) == unit for n in LAST for side in range(2)]
    return functools.reduce(jnp.logical_or, found)


def placed(plan, a_all, sem):
    for ref, panel_there, n, panel in plan:
        for side in range(2):
            to = pl.multiple_of(unit_of(n, side) * DEPTH + panel * TILE, TILE)
            yield pltpu.make_async_copy(
                ref.at[panel_there, :, pl.ds(side * TILE, TILE)], a_all.at[:, pl.ds(to, TILE)], sem
            )


def when(wanted, act):
    if wanted is None:
        act()
    else:
        pl.when(wanted)(act)


def add_shards(groups, b_refs, a_all, total_ref, held, sems, ready, use=None):
    conditions = [None if wanted is None else comes_last(unit) == wanted for unit, _, wanted in groups]
    spots, refs = [], iter(b_refs)
    for (unit, count, _), condition in zip(groups, conditions):
        spots += [(next(refs), condition) for _ in range(count)]

    def copies(part):
        columns = pl.ds(pl.multiple_of(part * WIDE, WIDE), WIDE)
        for n, (ref, condition) in enumerate(spots):
            yield condition, pltpu.make_async_copy(
                ref.at[:, :, columns], held.at[part % 2, pl.ds(2 * n, 2)], sems.at[part % 2, n]
            )

    def start(part):
        for condition, copy in copies(part):
            when(condition, copy.start)

    def step(part, carry):
        pl.when(part + 1 < COLS // WIDE)(lambda: start(part + 1))
        for condition, copy in copies(part):
            when(condition, copy.wait)
        columns = pl.ds(pl.multiple_of(part * WIDE, WIDE), WIDE)
        n = 0
        for (unit, count, _), condition in zip(groups, conditions):

            def add(unit=unit, count=count, n=n):
                right = held[part % 2, pl.ds(2 * n, 2 * count)].reshape(count * DEPTH, WIDE)
                left = a_all[:, pl.ds(unit * DEPTH, count * DEPTH)]
                total_ref[:, columns] += jnp.dot(left, right, preferred_element_type=jnp.float32)

            when(condition, add)
            n += count
        if use is not None:
            use(part, columns)
        return carry

    start(0)
    ready()
    lax.fori_loop(0, COLS // WIDE, step, 0)


def first_kernel(slot_ref, empty_ref, *refs):
    a_refs, b_refs = refs[:6], refs[6:11]
    a_all, total_ref, held, held_sems, sem = refs[11:]
    plan = [(ref, panel, n, panel) for n, ref in enumerate(a_refs) for panel in range(2)]
    for copy in placed(plan, a_all, sem):
        copy.start()

    def ready():
        total_ref[...] = jnp.zeros_like(total_ref)
        came = a_all.at[:, pl.ds(0, 12 * DEPTH)]
        pltpu.make_async_copy(came, came, sem).wait()

    add_shards(FIRST, b_refs, a_all, total_ref, held, held_sems, ready)


def second_kernel(*refs):
    b_refs = refs[2:5]
    a_all, total_ref, held, held_sems = refs[5:]
    add_shards(SECOND, b_refs, a_all, total_ref, held, held_sems, lambda: None)


def third_kernel(*refs):
    (fm_a, fp_a), b_refs = refs[:2], refs[4:17]
    a_all, total_ref, held, held_sems, sem = refs[17:]
    plan = [(fm_a, 0, 6, 0), (fp_a, 0, 6, 1), (fm_a, 1, 7, 0), (fp_a, 1, 7, 1)]
    for copy in placed(plan, a_all, sem):
        copy.start()

    def ready():
        came = a_all.at[:, pl.ds(0, 4 * DEPTH)]
        pltpu.make_async_copy(came, came, sem).wait()

    add_shards(THIRD, b_refs, a_all, total_ref, held, held_sems, ready)


def fourth_kernel(slot_ref, empty_ref, *refs):
    a_all, b_refs = refs[0], refs[2:5]
    out_ref, total_ref, held, held_sems = refs[5:]

    def use(part, columns):
        total = total_ref[:, columns].astype(jnp.bfloat16)
        for i in range(ROWS // TILE):
            for j in range(WIDE // TILE):
                number = i * (COLS // TILE) + part * (WIDE // TILE) + j
                out_ref[slot_ref[number]] = total[i * TILE : (i + 1) * TILE, j * TILE : (j + 1) * TILE]
                out_ref[empty_ref[number]] = jnp.zeros((TILE, TILE), jnp.bfloat16)

    add_shards(FOURTH, b_refs, a_all, total_ref, held, held_sems, lambda: None, use)


FIRST = tuple((n, 1, False) for n in range(5))
SECOND = tuple((5 + n, 1, False) for n in range(3))
THIRD = ((8, 5, None), *((n, 1, True) for n in range(8)))
FOURTH = ((13, 3, None),)


def scratch(groups):
    units = sum(count for _, count, _ in groups)
    return [pltpu.VMEM((2, 2 * units, TILE, WIDE), jnp.bfloat16), pltpu.SemaphoreType.DMA((2, units))]


def cost(units):
    return pl.CostEstimate(flops=2 * ROWS * COLS * DEPTH * units, bytes_accessed=1 << 20, transcendentals=0)


SUMS = (
    jax.ShapeDtypeStruct((ROWS, UNITS * DEPTH), jnp.bfloat16),
    jax.ShapeDtypeStruct((ROWS, COLS), jnp.float32),
)
PARAMS = pltpu.CompilerParams(vmem_limit_bytes=16 << 20)


def first_product(slots, empties, a_parts, b_parts):
    return pl.pallas_call(
        first_kernel,
        out_shape=SUMS,
        in_specs=[SMEM] * 2 + [HBM] * 11,
        out_specs=(VMEM, VMEM),
        scratch_shapes=[*scratch(FIRST), pltpu.SemaphoreType.DMA(())],
        compiler_params=PARAMS,
        cost_estimate=cost(5),
    )(slots, empties, *[hbm(v) for v in (*a_parts, *b_parts)])


def second_product(sums, b_parts):
    return pl.pallas_call(
        second_kernel,
        out_shape=SUMS,
        in_specs=[VMEM] * 5,
        out_specs=(VMEM, VMEM),
        input_output_aliases={0: 0, 1: 1},
        scratch_shapes=scratch(SECOND),
        compiler_params=PARAMS,
        cost_estimate=cost(4),
    )(*[vmem(v) for v in (*sums, *b_parts)])


def third_product(a_parts, sums, b_parts):
    return pl.pallas_call(
        third_kernel,
        out_shape=SUMS,
        in_specs=[HBM] * 2 + [VMEM] * 2 + [HBM] * 13,
        out_specs=(VMEM, VMEM),
        input_output_aliases={2: 0, 3: 1},
        scratch_shapes=[*scratch(THIRD), pltpu.SemaphoreType.DMA(())],
        compiler_params=PARAMS,
        cost_estimate=cost(5),
    )(*[hbm(v) for v in a_parts], *[vmem(v) for v in sums], *[hbm(v) for v in b_parts])


def fourth_product(slots, empties, sums, b_parts):
    return pl.pallas_call(
        fourth_kernel,
        out_shape=(jax.ShapeDtypeStruct((SLOTS, TILE, TILE), jnp.bfloat16), SUMS[1]),
        in_specs=[SMEM] * 2 + [VMEM] * 5,
        out_specs=(VMEM, VMEM),
        input_output_aliases={3: 1},
        scratch_shapes=scratch(FOURTH),
        compiler_params=PARAMS,
        cost_estimate=cost(5),
    )(slots, empties, *[vmem(v) for v in (*sums, *b_parts)])[0]


def forward_kernel(xm_a, zxm_a, xp_a, zxp_a, to_m, to_p, sem):
    for out_ref, panel, refs in ((to_m, 0, (xm_a, zxm_a)), (to_p, 1, (xp_a, zxp_a))):
        for n, ref in enumerate(refs):
            pltpu.make_async_copy(ref.at[panel], out_ref.at[n], sem).start()
    for out_ref in (to_m, to_p):
        pltpu.make_async_copy(out_ref, out_ref, sem).wait()


def forwarded(a_xm, a_zxm, a_xp, a_zxp):
    shape = jax.ShapeDtypeStruct((2, ROWS, DEPTH), jnp.bfloat16)
    return pl.pallas_call(
        forward_kernel,
        out_shape=(shape, shape),
        in_specs=[ANY] * 4,
        out_specs=(VMEM, VMEM),
        scratch_shapes=[pltpu.SemaphoreType.DMA(())],
        compiler_params=pltpu.CompilerParams(vmem_limit_bytes=8 << 20),
        cost_estimate=pl.CostEstimate(flops=0, bytes_accessed=4 << 20, transcendentals=0),
    )(a_xm, a_zxm, a_xp, a_zxp)


def write_kernel(arrived_ref, out_ref, sem):
    for part in range(8):
        at = pl.ds(part * (SLOTS // 8), SLOTS // 8)
        pltpu.make_async_copy(arrived_ref.at[at], out_ref.at[0, at], sem).start()
    pltpu.make_async_copy(out_ref, out_ref, sem).wait()


def write_out(arrived):
    return pl.pallas_call(
        write_kernel,
        out_shape=jax.ShapeDtypeStruct((1, SLOTS, TILE, TILE), jnp.bfloat16),
        in_specs=[VMEM],
        out_specs=ANY,
        scratch_shapes=[pltpu.SemaphoreType.DMA(())],
        compiler_params=pltpu.CompilerParams(vmem_limit_bytes=12 << 20),
    )(arrived)


def after(values, earlier):
    held = lax.optimization_barrier((tuple(values), tuple(earlier)))
    return held[0], held[1]


def local(amplitudes, integrals, tile_mask, next_owner):
    owners = next_owner[:, 0]
    before = jnp.arange(TILE)[None, :] < jnp.arange(TILE)[:, None]
    rank = jnp.sum(((owners[None, :] == owners[:, None]) & before).astype(jnp.int32), axis=1)
    slots = owners * 2 + rank
    every = jnp.arange(SLOTS, dtype=jnp.int32)
    empty = jnp.logical_not(jnp.any(slots[None, :] == every[:, None], axis=1))
    below = jnp.sum((empty[None, :] & (every[None, :] < every[:, None])).astype(jnp.int32), axis=1)
    pick = empty[None, :] & (below[None, :] == every[: SLOTS // 2, None])
    empties = jnp.sum(jnp.where(pick, every[None, :], 0), axis=1)
    b = integrals
    a = apply_mask(amplitudes, tile_mask)
    b_ym, b_yp = send(b, along_y(1)), send(b, along_y(-1))
    a_xm, a_xp, a_z = send(a, along_x(1)), send(a, along_x(-1)), send(a, across_z(1))
    (a_m,), _ = after((a_z,), (a_xm,))
    (a_p,), _ = after((a_z,), (a_xp,))
    a_zxm, a_zxp = send(a_m, along_x(1)), send(a_p, along_x(-1))
    (b_for_z,), _ = after((b,), (a_z,))
    (b_for_y,), _ = after((b,), (b_ym, b_yp))
    b_z, b_y2 = send(b_for_z, across_z(2)), send(b_for_y, along_y(2))
    onward_m, onward_p = forwarded(a_xm, a_zxm, a_xp, a_zxp)
    a_fm, a_fp = send(onward_m, along_x(1)), send(onward_p, along_x(-1))
    (b_for_y,), _ = after((b_z,), (b_y2,))
    b_zym, b_zyp, b_zy2 = send(b_for_y, along_y(1)), send(b_for_y, along_y(-1)), send(b_y2, across_z(2))
    early = (b, b_yp, b_y2, b_ym, b_z)
    sums = first_product(slots, empties, (a, a_z, a_xm, a_xp, a_zxm, a_zxp), early)
    held, sums = after((*early, b_zyp, b_zy2, b_zym), sums)
    early, late = held[:5], held[5:]
    early_mate, late_mate = [send(v, mate()) for v in early], [send(v, mate()) for v in late]
    sums = second_product(sums, late)
    sums = third_product((a_fm, a_fp), sums, (*early_mate, *early, *late))
    outgoing = fourth_product(slots, empties, sums, late_mate)
    arrived = lax.all_to_all(outgoing, AXES, split_axis=0, concat_axis=0, tiled=True)
    return write_out(arrived)


def solution(mesh):
    return jax.shard_map(
        local,
        mesh=mesh,
        in_specs=(
            P(None, "row", "col"),
            P(None, "row", "col"),
            P(None, "row", "col"),
            P(AXES, None),
        ),
        out_specs=P(AXES, None, None, None),
        check_vma=False,
    )
```

time: 233 us -> 223 us (0.957)
  waiting for transfers between devices: 63 us -> 44.8 us
  Pallas kernels: 28.4 us -> 36.4 us
  blocking collectives: 101 us -> 106 us
  other arithmetic: 5.84 us -> 1.99 us
    ppermute x19 -> x22, waiting for transfers between devices: 63 us -> 44.8 us  [send(): return lax.ppermute(value, AXES, where)]
    pallas_call x2 -> x5, Pallas kernels: 24.4 us -> 32.3 us  [the longest x1 12.1 us: third_product(): pl.pallas_call(third_kernel, out_shape=SUMS, in_specs=[HBM] * 2 + [VMEM]...]
    concatenate x4 -> x0, other arithmetic: 5.24 us -> none  [the longest x1 3.32 us: local(): e1 = send(jnp.concatenate([b, b_ym, b_yp], axis=0), mate())]
    all_to_all x1, blocking collectives: 101 us -> 106 us  [local(): lax.all_to_all(outgoing, AXES, split_axis=0, concat_axis=0, tiled=True)]
    slice x5 -> x0, local copies, waits for them, and re-layouts: 3.29 us -> none  [the longest x2 2.21 us: local(): from_p = jnp.concatenate([a_xp[1:], a_zxp[1:]], axis=0)]
    ppermute x19 -> x22, starting transfers between devices: 27.1 us -> 28.9 us  [send(): return lax.ppermute(value, AXES, where)]
  transfers between devices with their start and end apart: 19 -> 22, of which waited for: 11 -> 8; matrix products, arithmetic and copies ran while one was open for 3% -> 1% of each run, Pallas kernels for 6% -> 12%
where the time goes in v3:
time: 223 us
  blocking collectives  106 us (48%)
  waiting for transfers between devices  44.8 us (20%)
  Pallas kernels  36.4 us (16%)
  starting transfers between devices  28.9 us (13%)
  local copies, waits for them, and re-layouts  4.35 us (2%)
    all_to_all x1, blocking collectives, local(): lax.all_to_all(outgoing, AXES, split_axis=0, concat_axis=0, tiled=True)  106 us
    ppermute x22, waiting for transfers between devices, send(): return lax.ppermute(value, AXES, where)  44.8 us
    ppermute x22, starting transfers between devices, send(): return lax.ppermute(value, AXES, where)  28.9 us
    pallas_call x1, Pallas kernels, third_product(): pl.pallas_call(third_kernel, out_shape=SUMS, in_specs=[HBM] * 2 + [VMEM]...  12.1 us
    pallas_call x1, Pallas kernels, first_product(): pl.pallas_call(first_kernel, out_shape=SUMS, in_specs=[SMEM] * 2 + [HBM]...  10.9 us
    pallas_call x1, Pallas kernels, fourth_product(): pl.pallas_call(fourth_kernel, out_shape=(jax.ShapeDtypeStruct((SLOTS, TIL...  5.24 us
  transfers between devices with their start and end apart: 22, of which 8 were waited for; matrix products, arithmetic and copies ran while one was open for 1% of the time, Pallas kernels for 12%

profile of v3, /device:TPU:0, one launch (start us, length us, event | category | flops | bytes accessed | tf_op | source)
XLA Modules:
  0.0 223.0 jit_solution(14050674227061883057)
XLA Ops:
  0.0 0.8 copy.12
  0.9 1.2 copy-done.3
  2.1 0.8 shard_map.46.refs_0_
  2.9 2.1 collective-permute-start.1
  5.0 1.6 collective-permute-start.8
  6.5 1.7 collective-permute-start.7
  8.2 2.8 %collective-permute-start.3 = (bf16[2,1024,256]{2,1,0:T(8,128)(2,1)S(1)}, bf16[2,1024,256]{2,1,0:T(8,128)(2,1)S(1)}, u32[]{:S(2)}, u32[]{:S(2)}) collective-permute-start(bf16[2,1024,256]{2,1,0:T(8,128)(2,1)S(1)} %shard_map.46.refs_0_), channel_id=1, source_target_pairs={{0,6},{1,7},{2,0},{3,1},{4,2},{5,3},{6,4},{7,5},{8,14},{9,15},{10,... | collective-permute-start | bytes 3145736 | tf_op jit(solution)/shard_map/ppermute | solution.py:52
  11.0 17.2 %collective-permute-done.1.refs_1_ = bf16[2,1024,256]{2,1,0:T(8,128)(2,1)S(1)} collective-permute-done((bf16[2,1024,256]{2,1,0:T(8,128)(2,1)S(1)}, bf16[2,1024,256]{2,1,0:T(8,128)(2,1)S(1)}, u32[]{:S(2)}, u32[]{:S(2)}) %collective-permute-start.1) | collective-permute-done | bytes 1048608 | tf_op jit(solution)/shard_map/ppermute | solution.py:52
  28.1 3.7 %collective-permute-start.10 = (bf16[2,128,2048]{2,1,0:T(8,128)(2,1)}, bf16[2,128,2048]{2,1,0:T(8,128)(2,1)S(1)}, u32[]{:S(2)}, u32[]{:S(2)}) collective-permute-start(bf16[2,128,2048]{2,1,0:T(8,128)(2,1)} %refs_9_), channel_id=1, source_target_pairs={{0,64},{1,65},{2,66},{3,67},{4,68},{5,69},{6,70},{7,71},{8,72},{9,... | collective-permute-start | bytes 3145736 | tf_op jit(solution)/shard_map/ppermute | solution.py:52
  31.8 3.3 %collective-permute-start.9 = (bf16[2,128,2048]{2,1,0:T(8,128)(2,1)}, bf16[2,128,2048]{2,1,0:T(8,128)(2,1)S(1)}, u32[]{:S(2)}, u32[]{:S(2)}) collective-permute-start(bf16[2,128,2048]{2,1,0:T(8,128)(2,1)} %refs_9_), channel_id=1, source_target_pairs={{0,32},{1,33},{2,34},{3,35},{4,36},{5,37},{6,38},{7,39},{8,40},{9,... | collective-permute-start | bytes 3145736 | tf_op jit(solution)/shard_map/ppermute | solution.py:52
  35.1 2.8 %collective-permute-start.4 = (bf16[2,1024,256]{2,1,0:T(8,128)(2,1)S(1)}, bf16[2,1024,256]{2,1,0:T(8,128)(2,1)S(1)}, u32[]{:S(2)}, u32[]{:S(2)}) collective-permute-start(bf16[2,1024,256]{2,1,0:T(8,128)(2,1)S(1)} %collective-permute-done.1.refs_1_), channel_id=1, source_target_pairs={{0,6},{1,7},{2,0},{3,1},{4,2},{5,3},{6,4},{7,5},{8,14},{9,15},{10,... | collective-permute-start | bytes 3145736 | tf_op jit(solution)/shard_map/ppermute | solution.py:52
  37.9 0.9 convert_reduce_fusion.1
  38.8 15.5 %collective-permute-done.10.refs_10_.refs_13_ = bf16[2,128,2048]{2,1,0:T(8,128)(2,1)S(1)} collective-permute-done((bf16[2,128,2048]{2,1,0:T(8,128)(2,1)}, bf16[2,128,2048]{2,1,0:T(8,128)(2,1)S(1)}, u32[]{:S(2)}, u32[]{:S(2)}) %collective-permute-start.10) | collective-permute-done | bytes 1048608 | tf_op jit(solution)/shard_map/ppermute | solution.py:52
  54.3 3.1 %collective-permute-done.9.refs_8_.refs_11_ = bf16[2,128,2048]{2,1,0:T(8,128)(2,1)S(1)} collective-permute-done((bf16[2,128,2048]{2,1,0:T(8,128)(2,1)}, bf16[2,128,2048]{2,1,0:T(8,128)(2,1)S(1)}, u32[]{:S(2)}, u32[]{:S(2)}) %collective-permute-start.9) | collective-permute-done | bytes 1048608 | tf_op jit(solution)/shard_map/ppermute | solution.py:52
  57.4 1.6 collective-permute-start.13
  59.0 1.7 collective-permute-start.11
  60.6 2.8 %collective-permute-start.12 = (bf16[2,128,2048]{2,1,0:T(8,128)(2,1)S(1)}, bf16[2,128,2048]{2,1,0:T(8,128)(2,1)S(1)}, u32[]{:S(2)}, u32[]{:S(2)}) collective-permute-start(bf16[2,128,2048]{2,1,0:T(8,128)(2,1)S(1)} %collective-permute-done.9.refs_8_.refs_11_), channel_id=1, source_target_pairs={{0,64},{1,65},{2,66},{3,67},{4,68},{5,69},{6,70},{7,71},{8,72},{9,... | collective-permute-start | bytes 3145736 | tf_op jit(solution)/shard_map/ppermute | solution.py:52
  63.5 0.7 multiply_add_fusion.slot_ref
  64.8 1.2 copy-done.8
  66.0 1.5 collective-permute-start.5
  67.5 1.7 collective-permute-start.6
  69.3 10.9 %shard_map.48 = (bf16[1024,4096]{1,0:T(8,128)(2,1)S(1)}, f32[1024,2048]{1,0:T(8,128)S(1)}) custom-call(s32[128]{0:T(128)S(1)} %multiply_add_fusion.slot_ref, s32[128]{0:T(128)S(1)} %select_reduce_fusion.empty_ref, bf16[2,1024,256]{2,1,0:T(8,128)(2,1)} %copy-done.4, bf16[2,1024,256]{2,1,0:T(8,128)(2,1)} %copy-done.21, bf16[2,1024,256]{2,1,0:T(8,128)(2,1)} %copy-done.6, ...), custom_call_target="tpu_custom_call" | custom-call | flops 5368709120 | bytes 1048576 | tf_op jit(solution)/shard_map/pallas_call | solution.py:235
  80.2 1.2 collective-permute-done.13.refs_4_.refs_16_
  81.5 2.9 %collective-permute-done.12.refs_3_.refs_15_ = bf16[2,128,2048]{2,1,0:T(8,128)(2,1)S(1)} collective-permute-done((bf16[2,128,2048]{2,1,0:T(8,128)(2,1)S(1)}, bf16[2,128,2048]{2,1,0:T(8,128)(2,1)S(1)}, u32[]{:S(2)}, u32[]{:S(2)}) %collective-permute-start.12) | collective-permute-done | bytes 1048608 | tf_op jit(solution)/shard_map/ppermute | solution.py:52
  85.1 4.2 %collective-permute-done.5.refs_0_ = bf16[2,1024,256]{2,1,0:T(8,128)(2,1)S(1)} collective-permute-done((bf16[2,1024,256]{2,1,0:T(8,128)(2,1)S(1)}, bf16[2,1024,256]{2,1,0:T(8,128)(2,1)S(1)}, u32[]{:S(2)}, u32[]{:S(2)}) %collective-permute-start.5) | collective-permute-done | bytes 1048608 | tf_op jit(solution)/shard_map/ppermute | solution.py:52
  90.5 3.9 %shard_map.49 = (bf16[1024,4096]{1,0:T(8,128)(2,1)S(1)}, f32[1024,2048]{1,0:T(8,128)S(1)}) custom-call(bf16[1024,4096]{1,0:T(8,128)(2,1)S(1)} %get-tuple-element.38.refs_0_, f32[1024,2048]{1,0:T(8,128)S(1)} %get-tuple-element.39.refs_1_, ...), custom_call_target="tpu_custom_call", output_to_operand_aliasing={{0}: (0, {}), {1}: (1, {})} | custom-call | flops 4294967296 | bytes 1048576 | tf_op jit(solution)/shard_map/pallas_call | solution.py:247
  94.5 0.6 collective-permute-done.18.refs_8_
  95.5 0.5 copy-done.20
  96.1 12.1 %shard_map.50 = (bf16[1024,4096]{1,0:T(8,128)(2,1)S(1)}, f32[1024,2048]{1,0:T(8,128)S(1)}) custom-call(bf16[2,1024,256]{2,1,0:T(8,128)(2,1)} %copy-done.14, bf16[2,1024,256]{2,1,0:T(8,128)(2,1)} %copy-done.15, bf16[1024,4096]{1,0:T(8,128)(2,1)S(1)} %get-tuple-element.43.refs_2_, ...), custom_call_target="tpu_custom_call", output_to_operand_aliasing={{0}: (2, {}), {1}: (3, {})} | custom-call | flops 5368709120 | bytes 1048576 | tf_op jit(solution)/shard_map/pallas_call | solution.py:260
  108.2 5.2 %shard_map.51 = (bf16[256,128,128]{2,1,0:T(8,128)(2,1)S(1)}, f32[1024,2048]{1,0:T(8,128)S(1)}) custom-call(s32[128]{0:T(128)S(1)} %multiply_add_fusion.slot_ref, s32[128]{0:T(128)S(1)} %select_reduce_fusion.empty_ref, bf16[1024,4096]{1,0:T(8,128)(2,1)S(1)} %get-tuple-element.50.refs_0_, ...), custom_call_target="tpu_custom_call", output_to_operand_aliasing={{1}: (3, {})} | custom-call | flops 5368709120 | bytes 1048576 | tf_op jit(solution)/shard_map/pallas_call | solution.py:273
  113.4 106.1 %all_to_all.5.arrived_ref = bf16[256,128,128]{2,1,0:T(8,128)(2,1)S(1)} all-to-all(bf16[256,128,128]{2,1,0:T(8,128)(2,1)S(1)} %get-tuple-element.52), channel_id=1, replica_groups=mesh['row'=16,'col'=8] {'row','col'}, dimensions={0} | all-to-all | bytes 16777216 | tf_op jit(solution)/shard_map/all_to_all | solution.py:361
  219.5 3.3 %shard_map.52 = bf16[1,256,128,128]{3,2,1,0:T(8,128)(2,1)} custom-call(bf16[256,128,128]{2,1,0:T(8,128)(2,1)S(1)} %all_to_all.5.arrived_ref), custom_call_target="tpu_custom_call" | custom-call | tf_op jit(solution)/shard_map/pallas_call | solution.py:314
  (74 shorter events, 3.1 us)
Async XLA Ops:
  2.9 66.4 %copy-start.4 = (bf16[2,1024,256]{2,1,0:T(8,128)(2,1)}, bf16[2,1024,256]{2,1,0:T(8,128)(2,1)S(1)}, u32[]{:S(2)}) copy-start(bf16[2,1024,256]{2,1,0:T(8,128)(2,1)S(1)} %shard_map.46.refs_0_) | copy-start | bytes 3145732
  2.9 25.2 %collective-permute-start.1 = (bf16[2,1024,256]{2,1,0:T(8,128)(2,1)S(1)}, bf16[2,1024,256]{2,1,0:T(8,128)(2,1)S(1)}, u32[]{:S(2)}, u32[]{:S(2)}) collective-permute-start(bf16[2,1024,256]{2,1,0:T(8,128)(2,1)S(1)} %shard_map.46.refs_0_), channel_id=1, source_target_pairs={{0,1},{1,0},{2,3},{3,2},{4,5},{5,4},{6,7},{7,6},{8,9},{9,8},{10,11... | collective-permute-start | bytes 3145736 | tf_op jit(solution)/shard_map/ppermute | solution.py:52
  5.0 26.9 %collective-permute-start.8 = (bf16[2,128,2048]{2,1,0:T(8,128)(2,1)}, bf16[2,128,2048]{2,1,0:T(8,128)(2,1)S(1)}, u32[]{:S(2)}, u32[]{:S(2)}) collective-permute-start(bf16[2,128,2048]{2,1,0:T(8,128)(2,1)} %refs_9_), channel_id=1, source_target_pairs={{0,16},{1,17},{2,18},{3,19},{4,20},{5,21},{6,22},{7,23},{8,24},{9,... | collective-permute-start | bytes 3145736 | tf_op jit(solution)/shard_map/ppermute | solution.py:52
  6.5 25.3 %collective-permute-start.7 = (bf16[2,128,2048]{2,1,0:T(8,128)(2,1)}, bf16[2,128,2048]{2,1,0:T(8,128)(2,1)S(1)}, u32[]{:S(2)}, u32[]{:S(2)}) collective-permute-start(bf16[2,128,2048]{2,1,0:T(8,128)(2,1)} %refs_9_), channel_id=1, source_target_pairs={{0,48},{1,49},{2,50},{3,51},{4,52},{5,53},{6,54},{7,55},{8,56},{9,... | collective-permute-start | bytes 3145736 | tf_op jit(solution)/shard_map/ppermute | solution.py:52
  8.2 26.9 %collective-permute-start.3 = (bf16[2,1024,256]{2,1,0:T(8,128)(2,1)S(1)}, bf16[2,1024,256]{2,1,0:T(8,128)(2,1)S(1)}, u32[]{:S(2)}, u32[]{:S(2)}) collective-permute-start(bf16[2,1024,256]{2,1,0:T(8,128)(2,1)S(1)} %shard_map.46.refs_0_), channel_id=1, source_target_pairs={{0,6},{1,7},{2,0},{3,1},{4,2},{5,3},{6,4},{7,5},{8,14},{9,15},{10,... | collective-permute-start | bytes 3145736 | tf_op jit(solution)/shard_map/ppermute | solution.py:52
  11.0 26.9 %collective-permute-start = (bf16[2,1024,256]{2,1,0:T(8,128)(2,1)S(1)}, bf16[2,1024,256]{2,1,0:T(8,128)(2,1)S(1)}, u32[]{:S(2)}, u32[]{:S(2)}) collective-permute-start(bf16[2,1024,256]{2,1,0:T(8,128)(2,1)S(1)} %shard_map.46.refs_0_), channel_id=1, source_target_pairs={{0,2},{1,3},{2,4},{3,5},{4,6},{5,7},{6,0},{7,1},{8,10},{9,11},{10,... | collective-permute-start | bytes 3145736 | tf_op jit(solution)/shard_map/ppermute | solution.py:52
  28.1 41.1 %copy-start.21 = (bf16[2,1024,256]{2,1,0:T(8,128)(2,1)}, bf16[2,1024,256]{2,1,0:T(8,128)(2,1)S(1)}, u32[]{:S(2)}) copy-start(bf16[2,1024,256]{2,1,0:T(8,128)(2,1)S(1)} %collective-permute-done.1.refs_1_) | copy-start | bytes 3145732
  28.1 26.2 %collective-permute-start.10 = (bf16[2,128,2048]{2,1,0:T(8,128)(2,1)}, bf16[2,128,2048]{2,1,0:T(8,128)(2,1)S(1)}, u32[]{:S(2)}, u32[]{:S(2)}) collective-permute-start(bf16[2,128,2048]{2,1,0:T(8,128)(2,1)} %refs_9_), channel_id=1, source_target_pairs={{0,64},{1,65},{2,66},{3,67},{4,68},{5,69},{6,70},{7,71},{8,72},{9,... | collective-permute-start | bytes 3145736 | tf_op jit(solution)/shard_map/ppermute | solution.py:52
  31.8 37.4 %copy-start.10 = (bf16[2,128,2048]{2,1,0:T(8,128)(2,1)}, bf16[2,128,2048]{2,1,0:T(8,128)(2,1)S(1)}, u32[]{:S(2)}) copy-start(bf16[2,128,2048]{2,1,0:T(8,128)(2,1)S(1)} %collective-permute-done.8.refs_9_.refs_12_) | copy-start | bytes 3145732
  31.8 37.4 %copy-start.11 = (bf16[2,128,2048]{2,1,0:T(8,128)(2,1)}, bf16[2,128,2048]{2,1,0:T(8,128)(2,1)S(1)}, u32[]{:S(2)}) copy-start(bf16[2,128,2048]{2,1,0:T(8,128)(2,1)S(1)} %collective-permute-done.7.refs_7_.refs_10_) | copy-start | bytes 3145732
  31.8 25.5 %collective-permute-start.9 = (bf16[2,128,2048]{2,1,0:T(8,128)(2,1)}, bf16[2,128,2048]{2,1,0:T(8,128)(2,1)S(1)}, u32[]{:S(2)}, u32[]{:S(2)}) collective-permute-start(bf16[2,128,2048]{2,1,0:T(8,128)(2,1)} %refs_9_), channel_id=1, source_target_pairs={{0,32},{1,33},{2,34},{3,35},{4,36},{5,37},{6,38},{7,39},{8,40},{9,... | collective-permute-start | bytes 3145736 | tf_op jit(solution)/shard_map/ppermute | solution.py:52
  35.1 34.1 %copy-start.5 = (bf16[2,1024,256]{2,1,0:T(8,128)(2,1)}, bf16[2,1024,256]{2,1,0:T(8,128)(2,1)S(1)}, u32[]{:S(2)}) copy-start(bf16[2,1024,256]{2,1,0:T(8,128)(2,1)S(1)} %collective-permute-done.3.xp_a.refs_3_) | copy-start | bytes 3145732
  35.1 29.4 %collective-permute-start.4 = (bf16[2,1024,256]{2,1,0:T(8,128)(2,1)S(1)}, bf16[2,1024,256]{2,1,0:T(8,128)(2,1)S(1)}, u32[]{:S(2)}, u32[]{:S(2)}) collective-permute-start(bf16[2,1024,256]{2,1,0:T(8,128)(2,1)S(1)} %collective-permute-done.1.refs_1_), channel_id=1, source_target_pairs={{0,6},{1,7},{2,0},{3,1},{4,2},{5,3},{6,4},{7,5},{8,14},{9,15},{10,... | collective-permute-start | bytes 3145736 | tf_op jit(solution)/shard_map/ppermute | solution.py:52
  37.9 31.4 %copy-start.6 = (bf16[2,1024,256]{2,1,0:T(8,128)(2,1)}, bf16[2,1024,256]{2,1,0:T(8,128)(2,1)S(1)}, u32[]{:S(2)}) copy-start(bf16[2,1024,256]{2,1,0:T(8,128)(2,1)S(1)} %collective-permute-done.xm_a.refs_2_) | copy-start | bytes 3145732
  37.9 26.7 %collective-permute-start.2 = (bf16[2,1024,256]{2,1,0:T(8,128)(2,1)S(1)}, bf16[2,1024,256]{2,1,0:T(8,128)(2,1)S(1)}, u32[]{:S(2)}, u32[]{:S(2)}) collective-permute-start(bf16[2,1024,256]{2,1,0:T(8,128)(2,1)S(1)} %collective-permute-done.1.refs_1_), channel_id=1, source_target_pairs={{0,2},{1,3},{2,4},{3,5},{4,6},{5,7},{6,0},{7,1},{8,10},{9,11},{10,... | collective-permute-start | bytes 3145736 | tf_op jit(solution)/shard_map/ppermute | solution.py:52
  54.3 14.9 %copy-start.12 = (bf16[2,128,2048]{2,1,0:T(8,128)(2,1)}, bf16[2,128,2048]{2,1,0:T(8,128)(2,1)S(1)}, u32[]{:S(2)}) copy-start(bf16[2,128,2048]{2,1,0:T(8,128)(2,1)S(1)} %collective-permute-done.10.refs_10_.refs_13_) | copy-start | bytes 3145732
  57.4 24.1 %collective-permute-start.13 = (bf16[2,128,2048]{2,1,0:T(8,128)(2,1)S(1)}, bf16[2,128,2048]{2,1,0:T(8,128)(2,1)S(1)}, u32[]{:S(2)}, u32[]{:S(2)}) collective-permute-start(bf16[2,128,2048]{2,1,0:T(8,128)(2,1)S(1)} %collective-permute-done.10.refs_10_.refs_13_), channel_id=1, source_target_pairs={{0,16},{1,17},{2,18},{3,19},{4,20},{5,21},{6,22},{7,23},{8,24},{9,... | collective-permute-start | bytes 3145736 | tf_op jit(solution)/shard_map/ppermute | solution.py:52
  59.0 22.5 %collective-permute-start.11 = (bf16[2,128,2048]{2,1,0:T(8,128)(2,1)S(1)}, bf16[2,128,2048]{2,1,0:T(8,128)(2,1)S(1)}, u32[]{:S(2)}, u32[]{:S(2)}) collective-permute-start(bf16[2,128,2048]{2,1,0:T(8,128)(2,1)S(1)} %collective-permute-done.10.refs_10_.refs_13_), channel_id=1, source_target_pairs={{0,48},{1,49},{2,50},{3,51},{4,52},{5,53},{6,54},{7,55},{8,56},{9,... | collective-permute-start | bytes 3145736 | tf_op jit(solution)/shard_map/ppermute | solution.py:52
  60.6 23.8 %collective-permute-start.12 = (bf16[2,128,2048]{2,1,0:T(8,128)(2,1)S(1)}, bf16[2,128,2048]{2,1,0:T(8,128)(2,1)S(1)}, u32[]{:S(2)}, u32[]{:S(2)}) collective-permute-start(bf16[2,128,2048]{2,1,0:T(8,128)(2,1)S(1)} %collective-permute-done.9.refs_8_.refs_11_), channel_id=1, source_target_pairs={{0,64},{1,65},{2,66},{3,67},{4,68},{5,69},{6,70},{7,71},{8,72},{9,... | collective-permute-start | bytes 3145736 | tf_op jit(solution)/shard_map/ppermute | solution.py:52
  66.0 23.2 %collective-permute-start.5 = (bf16[2,1024,256]{2,1,0:T(8,128)(2,1)S(1)}, bf16[2,1024,256]{2,1,0:T(8,128)(2,1)S(1)}, u32[]{:S(2)}, u32[]{:S(2)}) collective-permute-start(bf16[2,1024,256]{2,1,0:T(8,128)(2,1)S(1)} %get-tuple-element.31), channel_id=1, source_target_pairs={{0,2},{1,3},{2,4},{3,5},{4,6},{5,7},{6,0},{7,1},{8,10},{9,11},{10,... | collective-permute-start | bytes 3145736 | tf_op jit(solution)/shard_map/ppermute | solution.py:52
  67.5 17.0 %copy-start.9 = (bf16[2,128,2048]{2,1,0:T(8,128)(2,1)S(1)}, bf16[2,128,2048]{2,1,0:T(8,128)(2,1)}, u32[]{:S(2)}) copy-start(bf16[2,128,2048]{2,1,0:T(8,128)(2,1)} %refs_9_) | copy-start | bytes 3145732
  67.5 21.7 %collective-permute-start.6 = (bf16[2,1024,256]{2,1,0:T(8,128)(2,1)S(1)}, bf16[2,1024,256]{2,1,0:T(8,128)(2,1)S(1)}, u32[]{:S(2)}, u32[]{:S(2)}) collective-permute-start(bf16[2,1024,256]{2,1,0:T(8,128)(2,1)S(1)} %get-tuple-element.32), channel_id=1, source_target_pairs={{0,6},{1,7},{2,0},{3,1},{4,2},{5,3},{6,4},{7,5},{8,14},{9,15},{10,... | collective-permute-start | bytes 3145736 | tf_op jit(solution)/shard_map/ppermute | solution.py:52
  81.5 12.9 %copy-start = (bf16[2,128,2048]{2,1,0:T(8,128)(2,1)}, bf16[2,128,2048]{2,1,0:T(8,128)(2,1)S(1)}, u32[]{:S(2)}) copy-start(bf16[2,128,2048]{2,1,0:T(8,128)(2,1)S(1)} %collective-permute-done.13.refs_4_.refs_16_) | copy-start | bytes 3145732
  81.5 12.9 %copy-start.1 = (bf16[2,128,2048]{2,1,0:T(8,128)(2,1)}, bf16[2,128,2048]{2,1,0:T(8,128)(2,1)S(1)}, u32[]{:S(2)}) copy-start(bf16[2,128,2048]{2,1,0:T(8,128)(2,1)S(1)} %collective-permute-done.11.refs_2_.refs_14_) | copy-start | bytes 3145732
  84.5 5.3 %collective-permute-start.14 = (bf16[2,128,2048]{2,1,0:T(8,128)(2,1)S(1)}, bf16[2,128,2048]{2,1,0:T(8,128)(2,1)S(1)}, u32[]{:S(2)}, u32[]{:S(2)}) collective-permute-start(bf16[2,128,2048]{2,1,0:T(8,128)(2,1)S(1)} %copy-done.9), channel_id=1, source_target_pairs={{0,8},{1,9},{2,10},{3,11},{4,12},{5,13},{6,14},{7,15},{8,0},{9,1},... | collective-permute-start | bytes 3145736 | tf_op jit(solution)/shard_map/ppermute | solution.py:52
  84.5 5.4 %collective-permute-start.15 = (bf16[2,128,2048]{2,1,0:T(8,128)(2,1)}, bf16[2,128,2048]{2,1,0:T(8,128)(2,1)S(1)}, u32[]{:S(2)}, u32[]{:S(2)}) collective-permute-start(bf16[2,128,2048]{2,1,0:T(8,128)(2,1)} %copy-done.11), channel_id=1, source_target_pairs={{0,8},{1,9},{2,10},{3,11},{4,12},{5,13},{6,14},{7,15},{8,0},{9,1},... | collective-permute-start | bytes 3145736 | tf_op jit(solution)/shard_map/ppermute | solution.py:52
  85.0 5.4 %collective-permute-start.16 = (bf16[2,128,2048]{2,1,0:T(8,128)(2,1)}, bf16[2,128,2048]{2,1,0:T(8,128)(2,1)S(1)}, u32[]{:S(2)}, u32[]{:S(2)}) collective-permute-start(bf16[2,128,2048]{2,1,0:T(8,128)(2,1)} %copy-done.13), channel_id=1, source_target_pairs={{0,8},{1,9},{2,10},{3,11},{4,12},{5,13},{6,14},{7,15},{8,0},{9,1},... | collective-permute-start | bytes 3145736 | tf_op jit(solution)/shard_map/ppermute | solution.py:52
  89.2 5.3 %collective-permute-start.17 = (bf16[2,128,2048]{2,1,0:T(8,128)(2,1)}, bf16[2,128,2048]{2,1,0:T(8,128)(2,1)S(1)}, u32[]{:S(2)}, u32[]{:S(2)}) collective-permute-start(bf16[2,128,2048]{2,1,0:T(8,128)(2,1)} %copy-done.10), channel_id=1, source_target_pairs={{0,8},{1,9},{2,10},{3,11},{4,12},{5,13},{6,14},{7,15},{8,0},{9,1},... | collective-permute-start | bytes 3145736 | tf_op jit(solution)/shard_map/ppermute | solution.py:52
  89.2 5.9 %collective-permute-start.18 = (bf16[2,128,2048]{2,1,0:T(8,128)(2,1)}, bf16[2,128,2048]{2,1,0:T(8,128)(2,1)S(1)}, u32[]{:S(2)}, u32[]{:S(2)}) collective-permute-start(bf16[2,128,2048]{2,1,0:T(8,128)(2,1)} %copy-done.12), channel_id=1, source_target_pairs={{0,8},{1,9},{2,10},{3,11},{4,12},{5,13},{6,14},{7,15},{8,0},{9,1},... | collective-permute-start | bytes 3145736 | tf_op jit(solution)/shard_map/ppermute | solution.py:52
  89.7 18.4 %collective-permute-start.19 = (bf16[2,128,2048]{2,1,0:T(8,128)(2,1)S(1)}, bf16[2,128,2048]{2,1,0:T(8,128)(2,1)S(1)}, u32[]{:S(2)}, u32[]{:S(2)}) collective-permute-start(bf16[2,128,2048]{2,1,0:T(8,128)(2,1)S(1)} %collective-permute-done.11.refs_2_.refs_14_), channel_id=1, source_target_pairs={{0,8},{1,9},{2,10},{3,11},{4,12},{5,13},{6,14},{7,15},{8,0},{9,1},... | collective-permute-start | bytes 3145736 | tf_op jit(solution)/shard_map/ppermute | solution.py:52
  89.8 18.3 %collective-permute-start.20 = (bf16[2,128,2048]{2,1,0:T(8,128)(2,1)S(1)}, bf16[2,128,2048]{2,1,0:T(8,128)(2,1)S(1)}, u32[]{:S(2)}, u32[]{:S(2)}) collective-permute-start(bf16[2,128,2048]{2,1,0:T(8,128)(2,1)S(1)} %collective-permute-done.12.refs_3_.refs_15_), channel_id=1, source_target_pairs={{0,8},{1,9},{2,10},{3,11},{4,12},{5,13},{6,14},{7,15},{8,0},{9,1},... | collective-permute-start | bytes 3145736 | tf_op jit(solution)/shard_map/ppermute | solution.py:52
  90.3 17.8 %collective-permute-start.21 = (bf16[2,128,2048]{2,1,0:T(8,128)(2,1)S(1)}, bf16[2,128,2048]{2,1,0:T(8,128)(2,1)S(1)}, u32[]{:S(2)}, u32[]{:S(2)}) collective-permute-start(bf16[2,128,2048]{2,1,0:T(8,128)(2,1)S(1)} %collective-permute-done.13.refs_4_.refs_16_), channel_id=1, source_target_pairs={{0,8},{1,9},{2,10},{3,11},{4,12},{5,13},{6,14},{7,15},{8,0},{9,1},... | collective-permute-start | bytes 3145736 | tf_op jit(solution)/shard_map/ppermute | solution.py:52
  (12 other events, 55.0 us)

commit v4 on v3

--- a/solution.py
+++ b/solution.py
@@ -181,8 +181,8 @@
 
 
 def third_kernel(*refs):
-    (fm_a, fp_a), b_refs = refs[:2], refs[4:17]
-    a_all, total_ref, held, held_sems, sem = refs[17:]
+    (fm_a, fp_a), b_refs = refs[:2], refs[4:15]
+    a_all, total_ref, held, held_sems, sem = refs[15:]
     plan = [(fm_a, 0, 6, 0), (fp_a, 0, 6, 1), (fm_a, 1, 7, 0), (fp_a, 1, 7, 1)]
     for copy in placed(plan, a_all, sem):
         copy.start()
@@ -195,8 +195,8 @@
 
 
 def fourth_kernel(slot_ref, empty_ref, *refs):
-    a_all, b_refs = refs[0], refs[2:5]
-    out_ref, total_ref, held, held_sems = refs[5:]
+    a_all, b_refs = refs[0], refs[2:7]
+    out_ref, total_ref, held, held_sems = refs[7:]
 
     def use(part, columns):
         total = total_ref[:, columns].astype(jnp.bfloat16)
@@ -211,8 +211,8 @@
 
 FIRST = tuple((n, 1, False) for n in range(5))
 SECOND = tuple((5 + n, 1, False) for n in range(3))
-THIRD = ((8, 5, None), *((n, 1, True) for n in range(8)))
-FOURTH = ((13, 3, None),)
+THIRD = ((8, 2, None), (11, 1, None), *((n, 1, True) for n in range(8)))
+FOURTH = ((10, 1, None), (12, 4, None))
 
 
 def scratch(groups):
@@ -235,12 +235,12 @@
     return pl.pallas_call(
         first_kernel,
         out_shape=SUMS,
-        in_specs=[SMEM] * 2 + [HBM] * 11,
+        in_specs=[SMEM] * 2 + [HBM] * 4 + [VMEM] * 2 + [HBM] * 5,
         out_specs=(VMEM, VMEM),
         scratch_shapes=[*scratch(FIRST), pltpu.SemaphoreType.DMA(())],
         compiler_params=PARAMS,
         cost_estimate=cost(5),
-    )(slots, empties, *[hbm(v) for v in (*a_parts, *b_parts)])
+    )(slots, empties, *[hbm(v) for v in a_parts[:4]], *[vmem(v) for v in a_parts[4:]], *[hbm(v) for v in b_parts])
 
 
 def second_product(sums, b_parts):
@@ -260,20 +260,20 @@
     return pl.pallas_call(
         third_kernel,
         out_shape=SUMS,
-        in_specs=[HBM] * 2 + [VMEM] * 2 + [HBM] * 13,
+        in_specs=[HBM] * 2 + [VMEM] * 5 + [HBM] * 8,
         out_specs=(VMEM, VMEM),
         input_output_aliases={2: 0, 3: 1},
         scratch_shapes=[*scratch(THIRD), pltpu.SemaphoreType.DMA(())],
         compiler_params=PARAMS,
         cost_estimate=cost(5),
-    )(*[hbm(v) for v in a_parts], *[vmem(v) for v in sums], *[hbm(v) for v in b_parts])
+    )(*[hbm(v) for v in a_parts], *[vmem(v) for v in (*sums, *b_parts[:3])], *[hbm(v) for v in b_parts[3:]])
 
 
 def fourth_product(slots, empties, sums, b_parts):
     return pl.pallas_call(
         fourth_kernel,
         out_shape=(jax.ShapeDtypeStruct((SLOTS, TILE, TILE), jnp.bfloat16), SUMS[1]),
-        in_specs=[SMEM] * 2 + [VMEM] * 5,
+        in_specs=[SMEM] * 2 + [VMEM] * 7,
         out_specs=(VMEM, VMEM),
         input_output_aliases={3: 1},
         scratch_shapes=scratch(FOURTH),
@@ -352,12 +352,14 @@
     b_zym, b_zyp, b_zy2 = send(b_for_y, along_y(1)), send(b_for_y, along_y(-1)), send(b_y2, across_z(2))
     early = (b, b_yp, b_y2, b_ym, b_z)
     sums = first_product(slots, empties, (a, a_z, a_xm, a_xp, a_zxm, a_zxp), early)
-    held, sums = after((*early, b_zyp, b_zy2, b_zym), sums)
-    early, late = held[:5], held[5:]
-    early_mate, late_mate = [send(v, mate()) for v in early], [send(v, mate()) for v in late]
+    held, sums = after((b, b_yp, b_ym, b_y2, b_z, b_zyp, b_zy2, b_zym), sums)
+    early, late = (held[0], held[1], held[3], held[2], held[4]), held[5:]
+    first_mates = [send(v, mate()) for v in held[:3]]
     sums = second_product(sums, late)
-    sums = third_product((a_fm, a_fp), sums, (*early_mate, *early, *late))
-    outgoing = fourth_product(slots, empties, sums, late_mate)
+    rest, sums = after(held[3:], sums)
+    last_mates = [send(v, mate()) for v in rest]
+    sums = third_product((a_fm, a_fp), sums, (*first_mates, *early, *late))
+    outgoing = fourth_product(slots, empties, sums, last_mates)
     arrived = lax.all_to_all(outgoing, AXES, split_axis=0, concat_axis=0, tiled=True)
     return write_out(arrived)
 

time: 223 us -> 220 us (0.987)
  starting transfers between devices: 28.9 us -> 26.6 us
    pallas_call x1, Pallas kernels: 12.1 us -> 9.5 us  [third_product(): pl.pallas_call(third_kernel, out_shape=SUMS, in_specs=[HBM] * 2 + [VMEM]...]
    pallas_call x1, Pallas kernels: 5.24 us -> 7.61 us  [fourth_product(): pl.pallas_call(fourth_kernel, out_shape=(jax.ShapeDtypeStruct((SLOTS, TIL...]
  transfers between devices with their start and end apart: 22 -> 22, of which waited for: 8 -> 8; matrix products, arithmetic and copies ran while one was open for 1% -> 1% of each run, Pallas kernels for 12% -> 11%
where the time goes in v4:
time: 220 us; the launch traced here: 219 us
  blocking collectives  108 us (49%)
  waiting for transfers between devices  44.7 us (20%)
  Pallas kernels  35.6 us (16%)
  starting transfers between devices  26.6 us (12%)
    all_to_all x1, blocking collectives, local(): lax.all_to_all(outgoing, AXES, split_axis=0, concat_axis=0, tiled=True)  108 us
    ppermute x22, waiting for transfers between devices, send(): return lax.ppermute(value, AXES, where)  44.7 us
    ppermute x22, starting transfers between devices, send(): return lax.ppermute(value, AXES, where)  26.6 us
    pallas_call x1, Pallas kernels, first_product(): pl.pallas_call(first_kernel, out_shape=SUMS, in_specs=[SMEM] * 2 + [HBM]...  10.4 us
    pallas_call x1, Pallas kernels, third_product(): pl.pallas_call(third_kernel, out_shape=SUMS, in_specs=[HBM] * 2 + [VMEM]...  9.5 us
    pallas_call x1, Pallas kernels, fourth_product(): pl.pallas_call(fourth_kernel, out_shape=(jax.ShapeDtypeStruct((SLOTS, TIL...  7.61 us
  transfers between devices with their start and end apart: 22, of which 8 were waited for; matrix products, arithmetic and copies ran while one was open for 1% of the time, Pallas kernels for 11%

profile of v4, /device:TPU:0, one launch (start us, length us, event | category | flops | bytes accessed | tf_op | source)
XLA Modules:
  0.0 219.4 jit_solution(6758803196381987130)
XLA Ops:
  0.0 0.8 copy.12
  0.9 1.2 copy-done.3
  2.1 0.8 shard_map.46.refs_0_
  2.9 2.1 collective-permute-start.1
  5.0 3.0 %collective-permute-start.7 = (bf16[2,128,2048]{2,1,0:T(8,128)(2,1)}, bf16[2,128,2048]{2,1,0:T(8,128)(2,1)S(1)}, u32[]{:S(2)}, u32[]{:S(2)}) collective-permute-start(bf16[2,128,2048]{2,1,0:T(8,128)(2,1)} %refs_7_), channel_id=1, source_target_pairs={{0,48},{1,49},{2,50},{3,51},{4,52},{5,53},{6,54},{7,55},{8,56},{9,... | collective-permute-start | bytes 3145736 | tf_op jit(solution)/shard_map/ppermute | solution.py:52
  8.0 2.8 %collective-permute-start.3 = (bf16[2,1024,256]{2,1,0:T(8,128)(2,1)S(1)}, bf16[2,1024,256]{2,1,0:T(8,128)(2,1)S(1)}, u32[]{:S(2)}, u32[]{:S(2)}) collective-permute-start(bf16[2,1024,256]{2,1,0:T(8,128)(2,1)S(1)} %shard_map.46.refs_0_), channel_id=1, source_target_pairs={{0,6},{1,7},{2,0},{3,1},{4,2},{5,3},{6,4},{7,5},{8,14},{9,15},{10,... | collective-permute-start | bytes 3145736 | tf_op jit(solution)/shard_map/ppermute | solution.py:52
  10.7 17.4 %collective-permute-done.1.refs_1_ = bf16[2,1024,256]{2,1,0:T(8,128)(2,1)S(1)} collective-permute-done((bf16[2,1024,256]{2,1,0:T(8,128)(2,1)S(1)}, bf16[2,1024,256]{2,1,0:T(8,128)(2,1)S(1)}, u32[]{:S(2)}, u32[]{:S(2)}) %collective-permute-start.1) | collective-permute-done | bytes 1048608 | tf_op jit(solution)/shard_map/ppermute | solution.py:52
  28.1 3.7 %collective-permute-start.10 = (bf16[2,128,2048]{2,1,0:T(8,128)(2,1)}, bf16[2,128,2048]{2,1,0:T(8,128)(2,1)S(1)}, u32[]{:S(2)}, u32[]{:S(2)}) collective-permute-start(bf16[2,128,2048]{2,1,0:T(8,128)(2,1)} %refs_7_), channel_id=1, source_target_pairs={{0,64},{1,65},{2,66},{3,67},{4,68},{5,69},{6,70},{7,71},{8,72},{9,... | collective-permute-start | bytes 3145736 | tf_op jit(solution)/shard_map/ppermute | solution.py:52
  31.8 1.9 collective-permute-done.8.refs_9_.refs_10_
  33.7 1.4 collective-permute-start.9
  35.1 2.8 %collective-permute-start.4 = (bf16[2,1024,256]{2,1,0:T(8,128)(2,1)S(1)}, bf16[2,1024,256]{2,1,0:T(8,128)(2,1)S(1)}, u32[]{:S(2)}, u32[]{:S(2)}) collective-permute-start(bf16[2,1024,256]{2,1,0:T(8,128)(2,1)S(1)} %collective-permute-done.1.refs_1_), channel_id=1, source_target_pairs={{0,6},{1,7},{2,0},{3,1},{4,2},{5,3},{6,4},{7,5},{8,14},{9,15},{10,... | collective-permute-start | bytes 3145736 | tf_op jit(solution)/shard_map/ppermute | solution.py:52
  37.9 0.9 convert_reduce_fusion.1
  38.8 15.5 %collective-permute-done.10.refs_10_.refs_11_ = bf16[2,128,2048]{2,1,0:T(8,128)(2,1)S(1)} collective-permute-done((bf16[2,128,2048]{2,1,0:T(8,128)(2,1)}, bf16[2,128,2048]{2,1,0:T(8,128)(2,1)S(1)}, u32[]{:S(2)}, u32[]{:S(2)}) %collective-permute-start.10) | collective-permute-done | bytes 1048608 | tf_op jit(solution)/shard_map/ppermute | solution.py:52
  54.3 4.5 %collective-permute-done.9.refs_8_.refs_9_ = bf16[2,128,2048]{2,1,0:T(8,128)(2,1)S(1)} collective-permute-done((bf16[2,128,2048]{2,1,0:T(8,128)(2,1)}, bf16[2,128,2048]{2,1,0:T(8,128)(2,1)S(1)}, u32[]{:S(2)}, u32[]{:S(2)}) %collective-permute-start.9) | collective-permute-done | bytes 1048608 | tf_op jit(solution)/shard_map/ppermute | solution.py:52
  58.9 1.5 collective-permute-start.11
  60.4 0.5 collective-permute-start.13
  60.9 3.6 %collective-permute-start.12 = (bf16[2,128,2048]{2,1,0:T(8,128)(2,1)S(1)}, bf16[2,128,2048]{2,1,0:T(8,128)(2,1)S(1)}, u32[]{:S(2)}, u32[]{:S(2)}) collective-permute-start(bf16[2,128,2048]{2,1,0:T(8,128)(2,1)S(1)} %collective-permute-done.9.refs_8_.refs_9_), channel_id=1, source_target_pairs={{0,64},{1,65},{2,66},{3,67},{4,68},{5,69},{6,70},{7,71},{8,72},{9,... | collective-permute-start | bytes 3145736 | tf_op jit(solution)/shard_map/ppermute | solution.py:52
  64.5 0.7 multiply_add_fusion.slot_ref
  65.8 1.6 collective-permute-start.5
  67.3 1.7 collective-permute-start.6
  69.1 10.4 %shard_map.48 = (bf16[1024,4096]{1,0:T(8,128)(2,1)S(1)}, f32[1024,2048]{1,0:T(8,128)S(1)}) custom-call(s32[128]{0:T(128)S(1)} %multiply_add_fusion.slot_ref, s32[128]{0:T(128)S(1)} %select_reduce_fusion.empty_ref, bf16[2,1024,256]{2,1,0:T(8,128)(2,1)} %copy-done.4, bf16[2,1024,256]{2,1,0:T(8,128)(2,1)} %copy-done.16, bf16[2,1024,256]{2,1,0:T(8,128)(2,1)} %copy-done.6, ...), custom_call_target="tpu_custom_call" | custom-call | flops 5368709120 | bytes 1048576 | tf_op jit(solution)/shard_map/pallas_call | solution.py:235
  79.6 1.8 collective-permute-done.11.refs_2_.refs_12_
  81.4 2.8 %collective-permute-done.13.refs_4_.refs_14_ = bf16[2,128,2048]{2,1,0:T(8,128)(2,1)S(1)} collective-permute-done((bf16[2,128,2048]{2,1,0:T(8,128)(2,1)S(1)}, bf16[2,128,2048]{2,1,0:T(8,128)(2,1)S(1)}, u32[]{:S(2)}, u32[]{:S(2)}) %collective-permute-start.13) | collective-permute-done | bytes 1048608 | tf_op jit(solution)/shard_map/ppermute | solution.py:52
  84.2 0.5 collective-permute-done.12.refs_3_.refs_13_
  84.8 0.5 collective-permute-start.15
  85.4 3.8 %shard_map.49 = (bf16[1024,4096]{1,0:T(8,128)(2,1)S(1)}, f32[1024,2048]{1,0:T(8,128)S(1)}) custom-call(bf16[1024,4096]{1,0:T(8,128)(2,1)S(1)} %get-tuple-element.50.refs_0_, f32[1024,2048]{1,0:T(8,128)S(1)} %get-tuple-element.51.refs_1_, ...), custom_call_target="tpu_custom_call", output_to_operand_aliasing={{0}: (0, {}), {1}: (1, {})} | custom-call | flops 4294967296 | bytes 1048576 | tf_op jit(solution)/shard_map/pallas_call | solution.py:247
  89.2 0.5 collective-permute-start.17
  89.8 0.4 collective-permute-start.19
  90.8 9.5 %shard_map.50 = (bf16[1024,4096]{1,0:T(8,128)(2,1)S(1)}, f32[1024,2048]{1,0:T(8,128)S(1)}) custom-call(bf16[2,1024,256]{2,1,0:T(8,128)(2,1)} %copy-done.14, bf16[2,1024,256]{2,1,0:T(8,128)(2,1)} %copy-done.15, bf16[1024,4096]{1,0:T(8,128)(2,1)S(1)} %get-tuple-element.54.refs_2_, ...), custom_call_target="tpu_custom_call", output_to_operand_aliasing={{0}: (2, {}), {1}: (3, {})} | custom-call | flops 5368709120 | bytes 1048576 | tf_op jit(solution)/shard_map/pallas_call | solution.py:260
  100.4 7.6 %shard_map.51 = (bf16[256,128,128]{2,1,0:T(8,128)(2,1)S(1)}, f32[1024,2048]{1,0:T(8,128)S(1)}) custom-call(s32[128]{0:T(128)S(1)} %multiply_add_fusion.slot_ref, s32[128]{0:T(128)S(1)} %select_reduce_fusion.empty_ref, bf16[1024,4096]{1,0:T(8,128)(2,1)S(1)} %get-tuple-element.59.refs_0_, ...), custom_call_target="tpu_custom_call", output_to_operand_aliasing={{1}: (3, {})} | custom-call | flops 5368709120 | bytes 1048576 | tf_op jit(solution)/shard_map/pallas_call | solution.py:273
  108.0 107.9 %all_to_all.5.arrived_ref = bf16[256,128,128]{2,1,0:T(8,128)(2,1)S(1)} all-to-all(bf16[256,128,128]{2,1,0:T(8,128)(2,1)S(1)} %get-tuple-element.66), channel_id=1, replica_groups=mesh['row'=16,'col'=8] {'row','col'}, dimensions={0} | all-to-all | bytes 16777216 | tf_op jit(solution)/shard_map/all_to_all | solution.py:363
  215.9 3.3 %shard_map.52 = bf16[1,256,128,128]{3,2,1,0:T(8,128)(2,1)} custom-call(bf16[256,128,128]{2,1,0:T(8,128)(2,1)S(1)} %all_to_all.5.arrived_ref), custom_call_target="tpu_custom_call" | custom-call | tf_op jit(solution)/shard_map/pallas_call | solution.py:314
  (64 shorter events, 1.6 us)
Async XLA Ops:
  2.9 66.2 %copy-start.4 = (bf16[2,1024,256]{2,1,0:T(8,128)(2,1)}, bf16[2,1024,256]{2,1,0:T(8,128)(2,1)S(1)}, u32[]{:S(2)}) copy-start(bf16[2,1024,256]{2,1,0:T(8,128)(2,1)S(1)} %shard_map.46.refs_0_) | copy-start | bytes 3145732
  2.9 25.2 %collective-permute-start.1 = (bf16[2,1024,256]{2,1,0:T(8,128)(2,1)S(1)}, bf16[2,1024,256]{2,1,0:T(8,128)(2,1)S(1)}, u32[]{:S(2)}, u32[]{:S(2)}) collective-permute-start(bf16[2,1024,256]{2,1,0:T(8,128)(2,1)S(1)} %shard_map.46.refs_0_), channel_id=1, source_target_pairs={{0,1},{1,0},{2,3},{3,2},{4,5},{5,4},{6,7},{7,6},{8,9},{9,8},{10,11... | collective-permute-start | bytes 3145736 | tf_op jit(solution)/shard_map/ppermute | solution.py:52
  5.0 26.9 %collective-permute-start.7 = (bf16[2,128,2048]{2,1,0:T(8,128)(2,1)}, bf16[2,128,2048]{2,1,0:T(8,128)(2,1)S(1)}, u32[]{:S(2)}, u32[]{:S(2)}) collective-permute-start(bf16[2,128,2048]{2,1,0:T(8,128)(2,1)} %refs_7_), channel_id=1, source_target_pairs={{0,48},{1,49},{2,50},{3,51},{4,52},{5,53},{6,54},{7,55},{8,56},{9,... | collective-permute-start | bytes 3145736 | tf_op jit(solution)/shard_map/ppermute | solution.py:52
  8.0 25.8 %collective-permute-start.8 = (bf16[2,128,2048]{2,1,0:T(8,128)(2,1)}, bf16[2,128,2048]{2,1,0:T(8,128)(2,1)S(1)}, u32[]{:S(2)}, u32[]{:S(2)}) collective-permute-start(bf16[2,128,2048]{2,1,0:T(8,128)(2,1)} %refs_7_), channel_id=1, source_target_pairs={{0,16},{1,17},{2,18},{3,19},{4,20},{5,21},{6,22},{7,23},{8,24},{9,... | collective-permute-start | bytes 3145736 | tf_op jit(solution)/shard_map/ppermute | solution.py:52
  8.0 27.1 %collective-permute-start.3 = (bf16[2,1024,256]{2,1,0:T(8,128)(2,1)S(1)}, bf16[2,1024,256]{2,1,0:T(8,128)(2,1)S(1)}, u32[]{:S(2)}, u32[]{:S(2)}) collective-permute-start(bf16[2,1024,256]{2,1,0:T(8,128)(2,1)S(1)} %shard_map.46.refs_0_), channel_id=1, source_target_pairs={{0,6},{1,7},{2,0},{3,1},{4,2},{5,3},{6,4},{7,5},{8,14},{9,15},{10,... | collective-permute-start | bytes 3145736 | tf_op jit(solution)/shard_map/ppermute | solution.py:52
  10.7 27.1 %collective-permute-start = (bf16[2,1024,256]{2,1,0:T(8,128)(2,1)S(1)}, bf16[2,1024,256]{2,1,0:T(8,128)(2,1)S(1)}, u32[]{:S(2)}, u32[]{:S(2)}) collective-permute-start(bf16[2,1024,256]{2,1,0:T(8,128)(2,1)S(1)} %shard_map.46.refs_0_), channel_id=1, source_target_pairs={{0,2},{1,3},{2,4},{3,5},{4,6},{5,7},{6,0},{7,1},{8,10},{9,11},{10,... | collective-permute-start | bytes 3145736 | tf_op jit(solution)/shard_map/ppermute | solution.py:52
  28.1 41.0 %copy-start.16 = (bf16[2,1024,256]{2,1,0:T(8,128)(2,1)}, bf16[2,1024,256]{2,1,0:T(8,128)(2,1)S(1)}, u32[]{:S(2)}) copy-start(bf16[2,1024,256]{2,1,0:T(8,128)(2,1)S(1)} %collective-permute-done.1.refs_1_) | copy-start | bytes 3145732
  28.1 26.2 %collective-permute-start.10 = (bf16[2,128,2048]{2,1,0:T(8,128)(2,1)}, bf16[2,128,2048]{2,1,0:T(8,128)(2,1)S(1)}, u32[]{:S(2)}, u32[]{:S(2)}) collective-permute-start(bf16[2,128,2048]{2,1,0:T(8,128)(2,1)} %refs_7_), channel_id=1, source_target_pairs={{0,64},{1,65},{2,66},{3,67},{4,68},{5,69},{6,70},{7,71},{8,72},{9,... | collective-permute-start | bytes 3145736 | tf_op jit(solution)/shard_map/ppermute | solution.py:52
  31.8 37.3 %copy-start.8 = (bf16[2,128,2048]{2,1,0:T(8,128)(2,1)}, bf16[2,128,2048]{2,1,0:T(8,128)(2,1)S(1)}, u32[]{:S(2)}) copy-start(bf16[2,128,2048]{2,1,0:T(8,128)(2,1)S(1)} %collective-permute-done.7.refs_7_.refs_8_) | copy-start | bytes 3145732
  33.7 35.4 %copy-start.9 = (bf16[2,128,2048]{2,1,0:T(8,128)(2,1)}, bf16[2,128,2048]{2,1,0:T(8,128)(2,1)S(1)}, u32[]{:S(2)}) copy-start(bf16[2,128,2048]{2,1,0:T(8,128)(2,1)S(1)} %collective-permute-done.8.refs_9_.refs_10_) | copy-start | bytes 3145732
  33.7 25.1 %collective-permute-start.9 = (bf16[2,128,2048]{2,1,0:T(8,128)(2,1)}, bf16[2,128,2048]{2,1,0:T(8,128)(2,1)S(1)}, u32[]{:S(2)}, u32[]{:S(2)}) collective-permute-start(bf16[2,128,2048]{2,1,0:T(8,128)(2,1)} %refs_7_), channel_id=1, source_target_pairs={{0,32},{1,33},{2,34},{3,35},{4,36},{5,37},{6,38},{7,39},{8,40},{9,... | collective-permute-start | bytes 3145736 | tf_op jit(solution)/shard_map/ppermute | solution.py:52
  35.1 34.0 %copy-start.5 = (bf16[2,1024,256]{2,1,0:T(8,128)(2,1)}, bf16[2,1024,256]{2,1,0:T(8,128)(2,1)S(1)}, u32[]{:S(2)}) copy-start(bf16[2,1024,256]{2,1,0:T(8,128)(2,1)S(1)} %collective-permute-done.3.xp_a.refs_3_) | copy-start | bytes 3145732
  35.1 30.5 %collective-permute-start.4 = (bf16[2,1024,256]{2,1,0:T(8,128)(2,1)S(1)}, bf16[2,1024,256]{2,1,0:T(8,128)(2,1)S(1)}, u32[]{:S(2)}, u32[]{:S(2)}) collective-permute-start(bf16[2,1024,256]{2,1,0:T(8,128)(2,1)S(1)} %collective-permute-done.1.refs_1_), channel_id=1, source_target_pairs={{0,6},{1,7},{2,0},{3,1},{4,2},{5,3},{6,4},{7,5},{8,14},{9,15},{10,... | collective-permute-start | bytes 3145736 | tf_op jit(solution)/shard_map/ppermute | solution.py:52
  37.9 31.2 %copy-start.6 = (bf16[2,1024,256]{2,1,0:T(8,128)(2,1)}, bf16[2,1024,256]{2,1,0:T(8,128)(2,1)S(1)}, u32[]{:S(2)}) copy-start(bf16[2,1024,256]{2,1,0:T(8,128)(2,1)S(1)} %collective-permute-done.xm_a.refs_2_) | copy-start | bytes 3145732
  37.9 27.7 %collective-permute-start.2 = (bf16[2,1024,256]{2,1,0:T(8,128)(2,1)S(1)}, bf16[2,1024,256]{2,1,0:T(8,128)(2,1)S(1)}, u32[]{:S(2)}, u32[]{:S(2)}) collective-permute-start(bf16[2,1024,256]{2,1,0:T(8,128)(2,1)S(1)} %collective-permute-done.1.refs_1_), channel_id=1, source_target_pairs={{0,2},{1,3},{2,4},{3,5},{4,6},{5,7},{6,0},{7,1},{8,10},{9,11},{10,... | collective-permute-start | bytes 3145736 | tf_op jit(solution)/shard_map/ppermute | solution.py:52
  54.3 14.8 %copy-start.10 = (bf16[2,128,2048]{2,1,0:T(8,128)(2,1)}, bf16[2,128,2048]{2,1,0:T(8,128)(2,1)S(1)}, u32[]{:S(2)}) copy-start(bf16[2,128,2048]{2,1,0:T(8,128)(2,1)S(1)} %collective-permute-done.10.refs_10_.refs_11_) | copy-start | bytes 3145732
  58.9 10.3 %copy-start.12 = (bf16[2,128,2048]{2,1,0:T(8,128)(2,1)}, bf16[2,128,2048]{2,1,0:T(8,128)(2,1)S(1)}, u32[]{:S(2)}) copy-start(bf16[2,128,2048]{2,1,0:T(8,128)(2,1)S(1)} %collective-permute-done.9.refs_8_.refs_9_) | copy-start | bytes 3145732
  58.9 22.5 %collective-permute-start.11 = (bf16[2,128,2048]{2,1,0:T(8,128)(2,1)S(1)}, bf16[2,128,2048]{2,1,0:T(8,128)(2,1)S(1)}, u32[]{:S(2)}, u32[]{:S(2)}) collective-permute-start(bf16[2,128,2048]{2,1,0:T(8,128)(2,1)S(1)} %collective-permute-done.10.refs_10_.refs_11_), channel_id=1, source_target_pairs={{0,48},{1,49},{2,50},{3,51},{4,52},{5,53},{6,54},{7,55},{8,56},{9,... | collective-permute-start | bytes 3145736 | tf_op jit(solution)/shard_map/ppermute | solution.py:52
  60.4 23.8 %collective-permute-start.13 = (bf16[2,128,2048]{2,1,0:T(8,128)(2,1)S(1)}, bf16[2,128,2048]{2,1,0:T(8,128)(2,1)S(1)}, u32[]{:S(2)}, u32[]{:S(2)}) collective-permute-start(bf16[2,128,2048]{2,1,0:T(8,128)(2,1)S(1)} %collective-permute-done.10.refs_10_.refs_11_), channel_id=1, source_target_pairs={{0,16},{1,17},{2,18},{3,19},{4,20},{5,21},{6,22},{7,23},{8,24},{9,... | collective-permute-start | bytes 3145736 | tf_op jit(solution)/shard_map/ppermute | solution.py:52
  60.9 23.8 %collective-permute-start.12 = (bf16[2,128,2048]{2,1,0:T(8,128)(2,1)S(1)}, bf16[2,128,2048]{2,1,0:T(8,128)(2,1)S(1)}, u32[]{:S(2)}, u32[]{:S(2)}) collective-permute-start(bf16[2,128,2048]{2,1,0:T(8,128)(2,1)S(1)} %collective-permute-done.9.refs_8_.refs_9_), channel_id=1, source_target_pairs={{0,64},{1,65},{2,66},{3,67},{4,68},{5,69},{6,70},{7,71},{8,72},{9,... | collective-permute-start | bytes 3145736 | tf_op jit(solution)/shard_map/ppermute | solution.py:52
  65.8 23.4 %collective-permute-start.5 = (bf16[2,1024,256]{2,1,0:T(8,128)(2,1)S(1)}, bf16[2,1024,256]{2,1,0:T(8,128)(2,1)S(1)}, u32[]{:S(2)}, u32[]{:S(2)}) collective-permute-start(bf16[2,1024,256]{2,1,0:T(8,128)(2,1)S(1)} %get-tuple-element.38), channel_id=1, source_target_pairs={{0,2},{1,3},{2,4},{3,5},{4,6},{5,7},{6,0},{7,1},{8,10},{9,11},{10,... | collective-permute-start | bytes 3145736 | tf_op jit(solution)/shard_map/ppermute | solution.py:52
  67.3 17.3 %copy-start.7 = (bf16[2,128,2048]{2,1,0:T(8,128)(2,1)S(1)}, bf16[2,128,2048]{2,1,0:T(8,128)(2,1)}, u32[]{:S(2)}) copy-start(bf16[2,128,2048]{2,1,0:T(8,128)(2,1)} %refs_7_) | copy-start | bytes 3145732
  67.3 22.3 %collective-permute-start.6 = (bf16[2,1024,256]{2,1,0:T(8,128)(2,1)S(1)}, bf16[2,1024,256]{2,1,0:T(8,128)(2,1)S(1)}, u32[]{:S(2)}, u32[]{:S(2)}) collective-permute-start(bf16[2,1024,256]{2,1,0:T(8,128)(2,1)S(1)} %get-tuple-element.39), channel_id=1, source_target_pairs={{0,6},{1,7},{2,0},{3,1},{4,2},{5,3},{6,4},{7,5},{8,14},{9,15},{10,... | collective-permute-start | bytes 3145736 | tf_op jit(solution)/shard_map/ppermute | solution.py:52
  81.4 8.5 %copy-start.1 = (bf16[2,128,2048]{2,1,0:T(8,128)(2,1)}, bf16[2,128,2048]{2,1,0:T(8,128)(2,1)S(1)}, u32[]{:S(2)}) copy-start(bf16[2,128,2048]{2,1,0:T(8,128)(2,1)S(1)} %collective-permute-done.11.refs_2_.refs_12_) | copy-start | bytes 3145732
  84.7 5.2 %collective-permute-start.14 = (bf16[2,128,2048]{2,1,0:T(8,128)(2,1)S(1)}, bf16[2,128,2048]{2,1,0:T(8,128)(2,1)S(1)}, u32[]{:S(2)}, u32[]{:S(2)}) collective-permute-start(bf16[2,128,2048]{2,1,0:T(8,128)(2,1)S(1)} %copy-done.7), channel_id=1, source_target_pairs={{0,8},{1,9},{2,10},{3,11},{4,12},{5,13},{6,14},{7,15},{8,0},{9,1},... | collective-permute-start | bytes 3145736 | tf_op jit(solution)/shard_map/ppermute | solution.py:52
  84.8 5.5 %collective-permute-start.15 = (bf16[2,128,2048]{2,1,0:T(8,128)(2,1)}, bf16[2,128,2048]{2,1,0:T(8,128)(2,1)S(1)}, u32[]{:S(2)}, u32[]{:S(2)}) collective-permute-start(bf16[2,128,2048]{2,1,0:T(8,128)(2,1)} %copy-done.8), channel_id=1, source_target_pairs={{0,8},{1,9},{2,10},{3,11},{4,12},{5,13},{6,14},{7,15},{8,0},{9,1},... | collective-permute-start | bytes 3145736 | tf_op jit(solution)/shard_map/ppermute | solution.py:52
  85.3 5.4 %collective-permute-start.16 = (bf16[2,128,2048]{2,1,0:T(8,128)(2,1)}, bf16[2,128,2048]{2,1,0:T(8,128)(2,1)S(1)}, u32[]{:S(2)}, u32[]{:S(2)}) collective-permute-start(bf16[2,128,2048]{2,1,0:T(8,128)(2,1)} %copy-done.9), channel_id=1, source_target_pairs={{0,8},{1,9},{2,10},{3,11},{4,12},{5,13},{6,14},{7,15},{8,0},{9,1},... | collective-permute-start | bytes 3145736 | tf_op jit(solution)/shard_map/ppermute | solution.py:52
  89.2 11.1 %collective-permute-start.17 = (bf16[2,128,2048]{2,1,0:T(8,128)(2,1)S(1)}, bf16[2,128,2048]{2,1,0:T(8,128)(2,1)S(1)}, u32[]{:S(2)}, u32[]{:S(2)}) collective-permute-start(bf16[2,128,2048]{2,1,0:T(8,128)(2,1)S(1)} %copy-done.13), channel_id=1, source_target_pairs={{0,8},{1,9},{2,10},{3,11},{4,12},{5,13},{6,14},{7,15},{8,0},{9,1},... | collective-permute-start | bytes 3145736 | tf_op jit(solution)/shard_map/ppermute | solution.py:52
  89.7 10.6 %collective-permute-start.18 = (bf16[2,128,2048]{2,1,0:T(8,128)(2,1)S(1)}, bf16[2,128,2048]{2,1,0:T(8,128)(2,1)S(1)}, u32[]{:S(2)}, u32[]{:S(2)}) collective-permute-start(bf16[2,128,2048]{2,1,0:T(8,128)(2,1)S(1)} %copy-done.11), channel_id=1, source_target_pairs={{0,8},{1,9},{2,10},{3,11},{4,12},{5,13},{6,14},{7,15},{8,0},{9,1},... | collective-permute-start | bytes 3145736 | tf_op jit(solution)/shard_map/ppermute | solution.py:52
  89.8 10.5 %collective-permute-start.19 = (bf16[2,128,2048]{2,1,0:T(8,128)(2,1)S(1)}, bf16[2,128,2048]{2,1,0:T(8,128)(2,1)S(1)}, u32[]{:S(2)}, u32[]{:S(2)}) collective-permute-start(bf16[2,128,2048]{2,1,0:T(8,128)(2,1)S(1)} %collective-permute-done.11.refs_2_.refs_12_), channel_id=1, source_target_pairs={{0,8},{1,9},{2,10},{3,11},{4,12},{5,13},{6,14},{7,15},{8,0},{9,1},... | collective-permute-start | bytes 3145736 | tf_op jit(solution)/shard_map/ppermute | solution.py:52
  90.3 10.1 %collective-permute-start.20 = (bf16[2,128,2048]{2,1,0:T(8,128)(2,1)S(1)}, bf16[2,128,2048]{2,1,0:T(8,128)(2,1)S(1)}, u32[]{:S(2)}, u32[]{:S(2)}) collective-permute-start(bf16[2,128,2048]{2,1,0:T(8,128)(2,1)S(1)} %collective-permute-done.12.refs_3_.refs_13_), channel_id=1, source_target_pairs={{0,8},{1,9},{2,10},{3,11},{4,12},{5,13},{6,14},{7,15},{8,0},{9,1},... | collective-permute-start | bytes 3145736 | tf_op jit(solution)/shard_map/ppermute | solution.py:52
  90.6 9.7 %collective-permute-start.21 = (bf16[2,128,2048]{2,1,0:T(8,128)(2,1)S(1)}, bf16[2,128,2048]{2,1,0:T(8,128)(2,1)S(1)}, u32[]{:S(2)}, u32[]{:S(2)}) collective-permute-start(bf16[2,128,2048]{2,1,0:T(8,128)(2,1)S(1)} %collective-permute-done.13.refs_4_.refs_14_), channel_id=1, source_target_pairs={{0,8},{1,9},{2,10},{3,11},{4,12},{5,13},{6,14},{7,15},{8,0},{9,1},... | collective-permute-start | bytes 3145736 | tf_op jit(solution)/shard_map/ppermute | solution.py:52
  (7 other events, 25.6 us)

commit v5 on v4

--- a/solution.py
+++ b/solution.py
@@ -160,8 +160,8 @@
 
 
 def first_kernel(slot_ref, empty_ref, *refs):
-    a_refs, b_refs = refs[:6], refs[6:11]
-    a_all, total_ref, held, held_sems, sem = refs[11:]
+    a_refs, b_refs = refs[:6], refs[6:12]
+    a_all, total_ref, held, held_sems, sem = refs[12:]
     plan = [(ref, panel, n, panel) for n, ref in enumerate(a_refs) for panel in range(2)]
     for copy in placed(plan, a_all, sem):
         copy.start()
@@ -209,9 +209,9 @@
     add_shards(FOURTH, b_refs, a_all, total_ref, held, held_sems, lambda: None, use)
 
 
-FIRST = tuple((n, 1, False) for n in range(5))
+FIRST = tuple((n, 1, False) for n in (0, 1, 2, 3, 4, 8))
 SECOND = tuple((5 + n, 1, False) for n in range(3))
-THIRD = ((8, 2, None), (11, 1, None), *((n, 1, True) for n in range(8)))
+THIRD = ((9, 1, None), (11, 1, None), *((n, 1, True) for n in range(9)))
 FOURTH = ((10, 1, None), (12, 4, None))
 
 
@@ -235,7 +235,7 @@
     return pl.pallas_call(
         first_kernel,
         out_shape=SUMS,
-        in_specs=[SMEM] * 2 + [HBM] * 4 + [VMEM] * 2 + [HBM] * 5,
+        in_specs=[SMEM] * 2 + [HBM] * 4 + [VMEM] * 2 + [HBM] * 6,
         out_specs=(VMEM, VMEM),
         scratch_shapes=[*scratch(FIRST), pltpu.SemaphoreType.DMA(())],
         compiler_params=PARAMS,
@@ -260,13 +260,13 @@
     return pl.pallas_call(
         third_kernel,
         out_shape=SUMS,
-        in_specs=[HBM] * 2 + [VMEM] * 5 + [HBM] * 8,
+        in_specs=[HBM] * 2 + [VMEM] * 4 + [HBM] * 9,
         out_specs=(VMEM, VMEM),
         input_output_aliases={2: 0, 3: 1},
         scratch_shapes=[*scratch(THIRD), pltpu.SemaphoreType.DMA(())],
         compiler_params=PARAMS,
         cost_estimate=cost(5),
-    )(*[hbm(v) for v in a_parts], *[vmem(v) for v in (*sums, *b_parts[:3])], *[hbm(v) for v in b_parts[3:]])
+    )(*[hbm(v) for v in a_parts], *[vmem(v) for v in (*sums, *b_parts[:2])], *[hbm(v) for v in b_parts[2:]])
 
 
 def fourth_product(slots, empties, sums, b_parts):
@@ -337,7 +337,9 @@
     pick = empty[None, :] & (below[None, :] == every[: SLOTS // 2, None])
     empties = jnp.sum(jnp.where(pick, every[None, :], 0), axis=1)
     b = integrals
+    own_mate = send(b, mate())
     a = apply_mask(amplitudes, tile_mask)
+    (a,), (own_mate,) = after((a,), (own_mate,))
     b_ym, b_yp = send(b, along_y(1)), send(b, along_y(-1))
     a_xm, a_xp, a_z = send(a, along_x(1)), send(a, along_x(-1)), send(a, across_z(1))
     (a_m,), _ = after((a_z,), (a_xm,))
@@ -351,14 +353,14 @@
     (b_for_y,), _ = after((b_z,), (b_y2,))
     b_zym, b_zyp, b_zy2 = send(b_for_y, along_y(1)), send(b_for_y, along_y(-1)), send(b_y2, across_z(2))
     early = (b, b_yp, b_y2, b_ym, b_z)
-    sums = first_product(slots, empties, (a, a_z, a_xm, a_xp, a_zxm, a_zxp), early)
+    sums = first_product(slots, empties, (a, a_z, a_xm, a_xp, a_zxm, a_zxp), (*early, own_mate))
     held, sums = after((b, b_yp, b_ym, b_y2, b_z, b_zyp, b_zy2, b_zym), sums)
     early, late = (held[0], held[1], held[3], held[2], held[4]), held[5:]
-    first_mates = [send(v, mate()) for v in held[:3]]
+    first_mates = [send(v, mate()) for v in held[1:3]]
     sums = second_product(sums, late)
     rest, sums = after(held[3:], sums)
     last_mates = [send(v, mate()) for v in rest]
-    sums = third_product((a_fm, a_fp), sums, (*first_mates, *early, *late))
+    sums = third_product((a_fm, a_fp), sums, (*first_mates, *early, *late, own_mate))
     outgoing = fourth_product(slots, empties, sums, last_mates)
     arrived = lax.all_to_all(outgoing, AXES, split_axis=0, concat_axis=0, tiled=True)
     return write_out(arrived)

time: 220 us -> 218 us (level)
  transfers between devices with their start and end apart: 22 -> 22, of which waited for: 8 -> 7; matrix products, arithmetic and copies ran while one was open for 1% -> 1% of each run, Pallas kernels for 11% -> 12%
where the time goes in v5:
time: 218 us; the launch traced here: 217 us
  blocking collectives  107 us (49%)
  waiting for transfers between devices  43.3 us (20%)
  Pallas kernels  36.3 us (17%)
  starting transfers between devices  26.5 us (12%)
  local copies, waits for them, and re-layouts  2.23 us (1%)
    all_to_all x1, blocking collectives, local(): lax.all_to_all(outgoing, AXES, split_axis=0, concat_axis=0, tiled=True)  107 us
    ppermute x22, waiting for transfers between devices, send(): return lax.ppermute(value, AXES, where)  43.3 us
    ppermute x22, starting transfers between devices, send(): return lax.ppermute(value, AXES, where)  26.5 us
    pallas_call x1, Pallas kernels, first_product(): pl.pallas_call(first_kernel, out_shape=SUMS, in_specs=[SMEM] * 2 + [HBM]...  12.3 us
    pallas_call x1, Pallas kernels, third_product(): pl.pallas_call(third_kernel, out_shape=SUMS, in_specs=[HBM] * 2 + [VMEM]...  8.39 us
    pallas_call x1, Pallas kernels, fourth_product(): pl.pallas_call(fourth_kernel, out_shape=(jax.ShapeDtypeStruct((SLOTS, TIL...  7.61 us
  transfers between devices with their start and end apart: 22, of which 7 were waited for; matrix products, arithmetic and copies ran while one was open for 1% of the time, Pallas kernels for 12%

profile of v5, /device:TPU:0, one launch (start us, length us, event | category | flops | bytes accessed | tf_op | source)
XLA Modules:
  0.0 217.3 jit_solution(7340544309014582458)
XLA Ops:
  0.0 3.1 %collective-permute-start.8 = (bf16[2,128,2048]{2,1,0:T(8,128)(2,1)}, bf16[2,128,2048]{2,1,0:T(8,128)(2,1)S(1)}, u32[]{:S(2)}, u32[]{:S(2)}) collective-permute-start(bf16[2,128,2048]{2,1,0:T(8,128)(2,1)} %refs_6_.2), channel_id=1, source_target_pairs={{0,48},{1,49},{2,50},{3,51},{4,52},{5,53},{6,54},{7,55},{8,56},{9,... | collective-permute-start | bytes 3145736 | tf_op jit(solution)/shard_map/ppermute | solution.py:52
  3.1 0.8 copy.12
  4.0 1.2 copy-done.3
  5.2 0.8 shard_map.46.refs_0_
  6.0 2.0 collective-permute-start.2
  8.0 1.5 collective-permute-start.1
  9.5 1.7 collective-permute-start.4
  11.2 15.3 %collective-permute-done.8.refs_7_ = bf16[2,128,2048]{2,1,0:T(8,128)(2,1)S(1)} collective-permute-done((bf16[2,128,2048]{2,1,0:T(8,128)(2,1)}, bf16[2,128,2048]{2,1,0:T(8,128)(2,1)S(1)}, u32[]{:S(2)}, u32[]{:S(2)}) %collective-permute-start.8) | collective-permute-done | bytes 1048608 | tf_op jit(solution)/shard_map/ppermute | solution.py:52
  26.5 3.4 %collective-permute-done.9.refs_9_ = bf16[2,128,2048]{2,1,0:T(8,128)(2,1)} collective-permute-done((bf16[2,128,2048]{2,1,0:T(8,128)(2,1)}, bf16[2,128,2048]{2,1,0:T(8,128)(2,1)}, u32[]{:S(2)}, u32[]{:S(2)}) %collective-permute-start.9) | collective-permute-done | bytes 1048608 | tf_op jit(solution)/shard_map/ppermute | solution.py:52
  29.9 1.6 collective-permute-done.2.refs_1_
  31.6 3.7 %collective-permute-start.11 = (bf16[2,128,2048]{2,1,0:T(8,128)(2,1)}, bf16[2,128,2048]{2,1,0:T(8,128)(2,1)S(1)}, u32[]{:S(2)}, u32[]{:S(2)}) collective-permute-start(bf16[2,128,2048]{2,1,0:T(8,128)(2,1)} %refs_6_.2), channel_id=1, source_target_pairs={{0,64},{1,65},{2,66},{3,67},{4,68},{5,69},{6,70},{7,71},{8,72},{9,... | collective-permute-start | bytes 3145736 | tf_op jit(solution)/shard_map/ppermute | solution.py:52
  35.3 1.5 collective-permute-start.3
  36.8 1.7 collective-permute-start.5
  38.5 0.9 convert_reduce_fusion.1
  39.4 16.7 %collective-permute-done.10.refs_8_ = bf16[2,128,2048]{2,1,0:T(8,128)(2,1)S(1)} collective-permute-done((bf16[2,128,2048]{2,1,0:T(8,128)(2,1)}, bf16[2,128,2048]{2,1,0:T(8,128)(2,1)S(1)}, u32[]{:S(2)}, u32[]{:S(2)}) %collective-permute-start.10) | collective-permute-done | bytes 1048608 | tf_op jit(solution)/shard_map/ppermute | solution.py:52
  56.1 3.9 %collective-permute-start.13 = (bf16[2,128,2048]{2,1,0:T(8,128)(2,1)S(1)}, bf16[2,128,2048]{2,1,0:T(8,128)(2,1)S(1)}, u32[]{:S(2)}, u32[]{:S(2)}) collective-permute-start(bf16[2,128,2048]{2,1,0:T(8,128)(2,1)S(1)} %collective-permute-done.10.refs_8_), channel_id=1, source_target_pairs={{0,64},{1,65},{2,66},{3,67},{4,68},{5,69},{6,70},{7,71},{8,72},{9,... | collective-permute-start | bytes 3145736 | tf_op jit(solution)/shard_map/ppermute | solution.py:52
  60.0 1.4 collective-permute-start.12
  61.4 0.6 collective-permute-start.14
  62.0 0.7 multiply_add_fusion.slot_ref
  63.3 1.6 collective-permute-start.6
  64.9 1.7 collective-permute-start.7
  66.7 12.3 %shard_map.48 = (bf16[1024,4096]{1,0:T(8,128)(2,1)S(1)}, f32[1024,2048]{1,0:T(8,128)S(1)}) custom-call(s32[128]{0:T(128)S(1)} %multiply_add_fusion.slot_ref, s32[128]{0:T(128)S(1)} %select_reduce_fusion.empty_ref, bf16[2,1024,256]{2,1,0:T(8,128)(2,1)} %copy-done.4, bf16[2,1024,256]{2,1,0:T(8,128)(2,1)} %copy-done.15, bf16[2,1024,256]{2,1,0:T(8,128)(2,1)} %copy-done.5, ...), custom_call_target="tpu_custom_call" | custom-call | flops 5368709120 | bytes 1048576 | tf_op jit(solution)/shard_map/pallas_call | solution.py:235
  79.0 2.8 %collective-permute-done.13.refs_3_.refs_12_ = bf16[2,128,2048]{2,1,0:T(8,128)(2,1)S(1)} collective-permute-done((bf16[2,128,2048]{2,1,0:T(8,128)(2,1)S(1)}, bf16[2,128,2048]{2,1,0:T(8,128)(2,1)S(1)}, u32[]{:S(2)}, u32[]{:S(2)}) %collective-permute-start.13) | collective-permute-done | bytes 1048608 | tf_op jit(solution)/shard_map/ppermute | solution.py:52
  81.8 1.5 collective-permute-done.12.refs_2_.refs_11_
  83.3 2.0 collective-permute-done.14.refs_4_.refs_13_
  85.3 0.5 collective-permute-start.16
  85.8 3.8 %shard_map.49 = (bf16[1024,4096]{1,0:T(8,128)(2,1)S(1)}, f32[1024,2048]{1,0:T(8,128)S(1)}) custom-call(bf16[1024,4096]{1,0:T(8,128)(2,1)S(1)} %get-tuple-element.54.refs_0_, f32[1024,2048]{1,0:T(8,128)S(1)} %get-tuple-element.55.refs_1_, ...), custom_call_target="tpu_custom_call", output_to_operand_aliasing={{0}: (0, {}), {1}: (1, {})} | custom-call | flops 4294967296 | bytes 1048576 | tf_op jit(solution)/shard_map/pallas_call | solution.py:247
  89.8 0.5 collective-permute-start.18
  91.3 8.4 %shard_map.50 = (bf16[1024,4096]{1,0:T(8,128)(2,1)S(1)}, f32[1024,2048]{1,0:T(8,128)S(1)}) custom-call(bf16[2,1024,256]{2,1,0:T(8,128)(2,1)} %copy-done.13, bf16[2,1024,256]{2,1,0:T(8,128)(2,1)} %copy-done.14, bf16[1024,4096]{1,0:T(8,128)(2,1)S(1)} %get-tuple-element.58.refs_2_, ...), custom_call_target="tpu_custom_call", output_to_operand_aliasing={{0}: (2, {}), {1}: (3, {})} | custom-call | flops 5368709120 | bytes 1048576 | tf_op jit(solution)/shard_map/pallas_call | solution.py:260
  99.7 7.6 %shard_map.51 = (bf16[256,128,128]{2,1,0:T(8,128)(2,1)S(1)}, f32[1024,2048]{1,0:T(8,128)S(1)}) custom-call(s32[128]{0:T(128)S(1)} %multiply_add_fusion.slot_ref, s32[128]{0:T(128)S(1)} %select_reduce_fusion.empty_ref, bf16[1024,4096]{1,0:T(8,128)(2,1)S(1)} %get-tuple-element.63.refs_0_, ...), custom_call_target="tpu_custom_call", output_to_operand_aliasing={{1}: (3, {})} | custom-call | flops 5368709120 | bytes 1048576 | tf_op jit(solution)/shard_map/pallas_call | solution.py:273
  107.3 106.5 %all_to_all.5.arrived_ref = bf16[256,128,128]{2,1,0:T(8,128)(2,1)S(1)} all-to-all(bf16[256,128,128]{2,1,0:T(8,128)(2,1)S(1)} %get-tuple-element.70), channel_id=1, replica_groups=mesh['row'=16,'col'=8] {'row','col'}, dimensions={0} | all-to-all | bytes 16777216 | tf_op jit(solution)/shard_map/all_to_all | solution.py:365
  213.8 3.3 %shard_map.52 = bf16[1,256,128,128]{3,2,1,0:T(8,128)(2,1)} custom-call(bf16[256,128,128]{2,1,0:T(8,128)(2,1)S(1)} %all_to_all.5.arrived_ref), custom_call_target="tpu_custom_call" | custom-call | tf_op jit(solution)/shard_map/pallas_call | solution.py:314
  (62 shorter events, 1.9 us)
Async XLA Ops:
  0.0 6.0 %collective-permute-start = (bf16[2,128,2048]{2,1,0:T(8,128)(2,1)}, bf16[2,128,2048]{2,1,0:T(8,128)(2,1)S(1)}, u32[]{:S(2)}, u32[]{:S(2)}) collective-permute-start(bf16[2,128,2048]{2,1,0:T(8,128)(2,1)} %refs_6_.2), channel_id=1, source_target_pairs={{0,8},{1,9},{2,10},{3,11},{4,12},{5,13},{6,14},{7,15},{8,0},{9,1},... | collective-permute-start | bytes 3145736 | tf_op jit(solution)/shard_map/ppermute | solution.py:52
  0.0 26.5 %collective-permute-start.8 = (bf16[2,128,2048]{2,1,0:T(8,128)(2,1)}, bf16[2,128,2048]{2,1,0:T(8,128)(2,1)S(1)}, u32[]{:S(2)}, u32[]{:S(2)}) collective-permute-start(bf16[2,128,2048]{2,1,0:T(8,128)(2,1)} %refs_6_.2), channel_id=1, source_target_pairs={{0,48},{1,49},{2,50},{3,51},{4,52},{5,53},{6,54},{7,55},{8,56},{9,... | collective-permute-start | bytes 3145736 | tf_op jit(solution)/shard_map/ppermute | solution.py:52
  3.1 26.8 %collective-permute-start.9 = (bf16[2,128,2048]{2,1,0:T(8,128)(2,1)}, bf16[2,128,2048]{2,1,0:T(8,128)(2,1)}, u32[]{:S(2)}, u32[]{:S(2)}) collective-permute-start(bf16[2,128,2048]{2,1,0:T(8,128)(2,1)} %refs_6_.2), channel_id=1, source_target_pairs={{0,16},{1,17},{2,18},{3,19},{4,20},{5,21},{6,22},{7,23},{8,24},{9,... | collective-permute-start | bytes 3145736 | tf_op jit(solution)/shard_map/ppermute | solution.py:52
  6.0 60.6 %copy-start.4 = (bf16[2,1024,256]{2,1,0:T(8,128)(2,1)}, bf16[2,1024,256]{2,1,0:T(8,128)(2,1)S(1)}, u32[]{:S(2)}) copy-start(bf16[2,1024,256]{2,1,0:T(8,128)(2,1)S(1)} %shard_map.46.refs_0_) | copy-start | bytes 3145732
  6.0 60.6 %copy-start.7 = (bf16[2,128,2048]{2,1,0:T(8,128)(2,1)}, bf16[2,128,2048]{2,1,0:T(8,128)(2,1)S(1)}, u32[]{:S(2)}) copy-start(bf16[2,128,2048]{2,1,0:T(8,128)(2,1)S(1)} %collective-permute-done.refs_11_.refs_14_) | copy-start | bytes 3145732
  6.0 25.5 %collective-permute-start.2 = (bf16[2,1024,256]{2,1,0:T(8,128)(2,1)S(1)}, bf16[2,1024,256]{2,1,0:T(8,128)(2,1)S(1)}, u32[]{:S(2)}, u32[]{:S(2)}) collective-permute-start(bf16[2,1024,256]{2,1,0:T(8,128)(2,1)S(1)} %shard_map.46.refs_0_), channel_id=1, source_target_pairs={{0,1},{1,0},{2,3},{3,2},{4,5},{5,4},{6,7},{7,6},{8,9},{9,8},{10,11... | collective-permute-start | bytes 3145736 | tf_op jit(solution)/shard_map/ppermute | solution.py:52
  8.0 27.3 %collective-permute-start.1 = (bf16[2,1024,256]{2,1,0:T(8,128)(2,1)S(1)}, bf16[2,1024,256]{2,1,0:T(8,128)(2,1)S(1)}, u32[]{:S(2)}, u32[]{:S(2)}) collective-permute-start(bf16[2,1024,256]{2,1,0:T(8,128)(2,1)S(1)} %shard_map.46.refs_0_), channel_id=1, source_target_pairs={{0,2},{1,3},{2,4},{3,5},{4,6},{5,7},{6,0},{7,1},{8,10},{9,11},{10,... | collective-permute-start | bytes 3145736 | tf_op jit(solution)/shard_map/ppermute | solution.py:52
  9.5 27.3 %collective-permute-start.4 = (bf16[2,1024,256]{2,1,0:T(8,128)(2,1)S(1)}, bf16[2,1024,256]{2,1,0:T(8,128)(2,1)S(1)}, u32[]{:S(2)}, u32[]{:S(2)}) collective-permute-start(bf16[2,1024,256]{2,1,0:T(8,128)(2,1)S(1)} %shard_map.46.refs_0_), channel_id=1, source_target_pairs={{0,6},{1,7},{2,0},{3,1},{4,2},{5,3},{6,4},{7,5},{8,14},{9,15},{10,... | collective-permute-start | bytes 3145736 | tf_op jit(solution)/shard_map/ppermute | solution.py:52
  26.5 40.1 %copy-start.8 = (bf16[2,128,2048]{2,1,0:T(8,128)(2,1)}, bf16[2,128,2048]{2,1,0:T(8,128)(2,1)S(1)}, u32[]{:S(2)}) copy-start(bf16[2,128,2048]{2,1,0:T(8,128)(2,1)S(1)} %collective-permute-done.8.refs_7_) | copy-start | bytes 3145732
  29.9 26.2 %collective-permute-start.10 = (bf16[2,128,2048]{2,1,0:T(8,128)(2,1)}, bf16[2,128,2048]{2,1,0:T(8,128)(2,1)S(1)}, u32[]{:S(2)}, u32[]{:S(2)}) collective-permute-start(bf16[2,128,2048]{2,1,0:T(8,128)(2,1)} %refs_6_.2), channel_id=1, source_target_pairs={{0,32},{1,33},{2,34},{3,35},{4,36},{5,37},{6,38},{7,39},{8,40},{9,... | collective-permute-start | bytes 3145736 | tf_op jit(solution)/shard_map/ppermute | solution.py:52
  31.6 35.1 %copy-start.15 = (bf16[2,1024,256]{2,1,0:T(8,128)(2,1)}, bf16[2,1024,256]{2,1,0:T(8,128)(2,1)S(1)}, u32[]{:S(2)}) copy-start(bf16[2,1024,256]{2,1,0:T(8,128)(2,1)S(1)} %collective-permute-done.2.refs_1_) | copy-start | bytes 3145732
  31.6 28.4 %collective-permute-start.11 = (bf16[2,128,2048]{2,1,0:T(8,128)(2,1)}, bf16[2,128,2048]{2,1,0:T(8,128)(2,1)S(1)}, u32[]{:S(2)}, u32[]{:S(2)}) collective-permute-start(bf16[2,128,2048]{2,1,0:T(8,128)(2,1)} %refs_6_.2), channel_id=1, source_target_pairs={{0,64},{1,65},{2,66},{3,67},{4,68},{5,69},{6,70},{7,71},{8,72},{9,... | collective-permute-start | bytes 3145736 | tf_op jit(solution)/shard_map/ppermute | solution.py:52
  35.3 31.4 %copy-start.5 = (bf16[2,1024,256]{2,1,0:T(8,128)(2,1)}, bf16[2,1024,256]{2,1,0:T(8,128)(2,1)S(1)}, u32[]{:S(2)}) copy-start(bf16[2,1024,256]{2,1,0:T(8,128)(2,1)S(1)} %collective-permute-done.1.xm_a.refs_2_) | copy-start | bytes 3145732
  35.3 27.9 %collective-permute-start.3 = (bf16[2,1024,256]{2,1,0:T(8,128)(2,1)S(1)}, bf16[2,1024,256]{2,1,0:T(8,128)(2,1)S(1)}, u32[]{:S(2)}, u32[]{:S(2)}) collective-permute-start(bf16[2,1024,256]{2,1,0:T(8,128)(2,1)S(1)} %collective-permute-done.2.refs_1_), channel_id=1, source_target_pairs={{0,2},{1,3},{2,4},{3,5},{4,6},{5,7},{6,0},{7,1},{8,10},{9,11},{10,... | collective-permute-start | bytes 3145736 | tf_op jit(solution)/shard_map/ppermute | solution.py:52
  36.8 29.9 %copy-start.6 = (bf16[2,1024,256]{2,1,0:T(8,128)(2,1)}, bf16[2,1024,256]{2,1,0:T(8,128)(2,1)S(1)}, u32[]{:S(2)}) copy-start(bf16[2,1024,256]{2,1,0:T(8,128)(2,1)S(1)} %collective-permute-done.4.xp_a.refs_3_) | copy-start | bytes 3145732
  36.8 26.4 %collective-permute-start.5 = (bf16[2,1024,256]{2,1,0:T(8,128)(2,1)S(1)}, bf16[2,1024,256]{2,1,0:T(8,128)(2,1)S(1)}, u32[]{:S(2)}, u32[]{:S(2)}) collective-permute-start(bf16[2,1024,256]{2,1,0:T(8,128)(2,1)S(1)} %collective-permute-done.2.refs_1_), channel_id=1, source_target_pairs={{0,6},{1,7},{2,0},{3,1},{4,2},{5,3},{6,4},{7,5},{8,14},{9,15},{10,... | collective-permute-start | bytes 3145736 | tf_op jit(solution)/shard_map/ppermute | solution.py:52
  56.1 10.5 %copy-start.9 = (bf16[2,128,2048]{2,1,0:T(8,128)(2,1)}, bf16[2,128,2048]{2,1,0:T(8,128)(2,1)S(1)}, u32[]{:S(2)}) copy-start(bf16[2,128,2048]{2,1,0:T(8,128)(2,1)S(1)} %collective-permute-done.10.refs_8_) | copy-start | bytes 3145732
  56.1 25.7 %collective-permute-start.13 = (bf16[2,128,2048]{2,1,0:T(8,128)(2,1)S(1)}, bf16[2,128,2048]{2,1,0:T(8,128)(2,1)S(1)}, u32[]{:S(2)}, u32[]{:S(2)}) collective-permute-start(bf16[2,128,2048]{2,1,0:T(8,128)(2,1)S(1)} %collective-permute-done.10.refs_8_), channel_id=1, source_target_pairs={{0,64},{1,65},{2,66},{3,67},{4,68},{5,69},{6,70},{7,71},{8,72},{9,... | collective-permute-start | bytes 3145736 | tf_op jit(solution)/shard_map/ppermute | solution.py:52
  60.0 6.7 %copy-start.11 = (bf16[2,128,2048]{2,1,0:T(8,128)(2,1)}, bf16[2,128,2048]{2,1,0:T(8,128)(2,1)S(1)}, u32[]{:S(2)}) copy-start(bf16[2,128,2048]{2,1,0:T(8,128)(2,1)S(1)} %collective-permute-done.11.refs_10_) | copy-start | bytes 3145732
  60.0 23.3 %collective-permute-start.12 = (bf16[2,128,2048]{2,1,0:T(8,128)(2,1)S(1)}, bf16[2,128,2048]{2,1,0:T(8,128)(2,1)S(1)}, u32[]{:S(2)}, u32[]{:S(2)}) collective-permute-start(bf16[2,128,2048]{2,1,0:T(8,128)(2,1)S(1)} %collective-permute-done.11.refs_10_), channel_id=1, source_target_pairs={{0,48},{1,49},{2,50},{3,51},{4,52},{5,53},{6,54},{7,55},{8,56},{9,... | collective-permute-start | bytes 3145736 | tf_op jit(solution)/shard_map/ppermute | solution.py:52
  61.4 23.9 %collective-permute-start.14 = (bf16[2,128,2048]{2,1,0:T(8,128)(2,1)S(1)}, bf16[2,128,2048]{2,1,0:T(8,128)(2,1)S(1)}, u32[]{:S(2)}, u32[]{:S(2)}) collective-permute-start(bf16[2,128,2048]{2,1,0:T(8,128)(2,1)S(1)} %collective-permute-done.11.refs_10_), channel_id=1, source_target_pairs={{0,16},{1,17},{2,18},{3,19},{4,20},{5,21},{6,22},{7,23},{8,24},{9,... | collective-permute-start | bytes 3145736 | tf_op jit(solution)/shard_map/ppermute | solution.py:52
  63.3 26.4 %collective-permute-start.6 = (bf16[2,1024,256]{2,1,0:T(8,128)(2,1)S(1)}, bf16[2,1024,256]{2,1,0:T(8,128)(2,1)S(1)}, u32[]{:S(2)}, u32[]{:S(2)}) collective-permute-start(bf16[2,1024,256]{2,1,0:T(8,128)(2,1)S(1)} %get-tuple-element.41), channel_id=1, source_target_pairs={{0,2},{1,3},{2,4},{3,5},{4,6},{5,7},{6,0},{7,1},{8,10},{9,11},{10,... | collective-permute-start | bytes 3145736 | tf_op jit(solution)/shard_map/ppermute | solution.py:52
  64.9 25.4 %collective-permute-start.7 = (bf16[2,1024,256]{2,1,0:T(8,128)(2,1)S(1)}, bf16[2,1024,256]{2,1,0:T(8,128)(2,1)S(1)}, u32[]{:S(2)}, u32[]{:S(2)}) collective-permute-start(bf16[2,1024,256]{2,1,0:T(8,128)(2,1)S(1)} %get-tuple-element.42), channel_id=1, source_target_pairs={{0,6},{1,7},{2,0},{3,1},{4,2},{5,3},{6,4},{7,5},{8,14},{9,15},{10,... | collective-permute-start | bytes 3145736 | tf_op jit(solution)/shard_map/ppermute | solution.py:52
  81.8 8.6 %copy-start = (bf16[2,128,2048]{2,1,0:T(8,128)(2,1)}, bf16[2,128,2048]{2,1,0:T(8,128)(2,1)S(1)}, u32[]{:S(2)}) copy-start(bf16[2,128,2048]{2,1,0:T(8,128)(2,1)S(1)} %collective-permute-done.13.refs_3_.refs_12_) | copy-start | bytes 3145732
  83.3 7.0 %copy-start.2 = (bf16[2,128,2048]{2,1,0:T(8,128)(2,1)}, bf16[2,128,2048]{2,1,0:T(8,128)(2,1)S(1)}, u32[]{:S(2)}) copy-start(bf16[2,128,2048]{2,1,0:T(8,128)(2,1)S(1)} %collective-permute-done.12.refs_2_.refs_11_) | copy-start | bytes 3145732
  85.3 5.1 %collective-permute-start.15 = (bf16[2,128,2048]{2,1,0:T(8,128)(2,1)}, bf16[2,128,2048]{2,1,0:T(8,128)(2,1)S(1)}, u32[]{:S(2)}, u32[]{:S(2)}) collective-permute-start(bf16[2,128,2048]{2,1,0:T(8,128)(2,1)} %copy-done.8), channel_id=1, source_target_pairs={{0,8},{1,9},{2,10},{3,11},{4,12},{5,13},{6,14},{7,15},{8,0},{9,1},... | collective-permute-start | bytes 3145736 | tf_op jit(solution)/shard_map/ppermute | solution.py:52
  85.3 5.6 %collective-permute-start.16 = (bf16[2,128,2048]{2,1,0:T(8,128)(2,1)}, bf16[2,128,2048]{2,1,0:T(8,128)(2,1)S(1)}, u32[]{:S(2)}, u32[]{:S(2)}) collective-permute-start(bf16[2,128,2048]{2,1,0:T(8,128)(2,1)} %collective-permute-done.9.refs_9_), channel_id=1, source_target_pairs={{0,8},{1,9},{2,10},{3,11},{4,12},{5,13},{6,14},{7,15},{8,0},{9,1},... | collective-permute-start | bytes 3145736 | tf_op jit(solution)/shard_map/ppermute | solution.py:52
  89.6 10.1 %collective-permute-start.17 = (bf16[2,128,2048]{2,1,0:T(8,128)(2,1)S(1)}, bf16[2,128,2048]{2,1,0:T(8,128)(2,1)S(1)}, u32[]{:S(2)}, u32[]{:S(2)}) collective-permute-start(bf16[2,128,2048]{2,1,0:T(8,128)(2,1)S(1)} %copy-done.10), channel_id=1, source_target_pairs={{0,8},{1,9},{2,10},{3,11},{4,12},{5,13},{6,14},{7,15},{8,0},{9,1},... | collective-permute-start | bytes 3145736 | tf_op jit(solution)/shard_map/ppermute | solution.py:52
  89.8 9.9 %collective-permute-start.18 = (bf16[2,128,2048]{2,1,0:T(8,128)(2,1)S(1)}, bf16[2,128,2048]{2,1,0:T(8,128)(2,1)S(1)}, u32[]{:S(2)}, u32[]{:S(2)}) collective-permute-start(bf16[2,128,2048]{2,1,0:T(8,128)(2,1)S(1)} %copy-done.12), channel_id=1, source_target_pairs={{0,8},{1,9},{2,10},{3,11},{4,12},{5,13},{6,14},{7,15},{8,0},{9,1},... | collective-permute-start | bytes 3145736 | tf_op jit(solution)/shard_map/ppermute | solution.py:52
  90.3 9.4 %collective-permute-start.19 = (bf16[2,128,2048]{2,1,0:T(8,128)(2,1)S(1)}, bf16[2,128,2048]{2,1,0:T(8,128)(2,1)S(1)}, u32[]{:S(2)}, u32[]{:S(2)}) collective-permute-start(bf16[2,128,2048]{2,1,0:T(8,128)(2,1)S(1)} %collective-permute-done.12.refs_2_.refs_11_), channel_id=1, source_target_pairs={{0,8},{1,9},{2,10},{3,11},{4,12},{5,13},{6,14},{7,15},{8,0},{9,1},... | collective-permute-start | bytes 3145736 | tf_op jit(solution)/shard_map/ppermute | solution.py:52
  90.4 9.3 %collective-permute-start.20 = (bf16[2,128,2048]{2,1,0:T(8,128)(2,1)S(1)}, bf16[2,128,2048]{2,1,0:T(8,128)(2,1)S(1)}, u32[]{:S(2)}, u32[]{:S(2)}) collective-permute-start(bf16[2,128,2048]{2,1,0:T(8,128)(2,1)S(1)} %collective-permute-done.13.refs_3_.refs_12_), channel_id=1, source_target_pairs={{0,8},{1,9},{2,10},{3,11},{4,12},{5,13},{6,14},{7,15},{8,0},{9,1},... | collective-permute-start | bytes 3145736 | tf_op jit(solution)/shard_map/ppermute | solution.py:52
  90.9 8.8 %collective-permute-start.21 = (bf16[2,128,2048]{2,1,0:T(8,128)(2,1)S(1)}, bf16[2,128,2048]{2,1,0:T(8,128)(2,1)S(1)}, u32[]{:S(2)}, u32[]{:S(2)}) collective-permute-start(bf16[2,128,2048]{2,1,0:T(8,128)(2,1)S(1)} %collective-permute-done.14.refs_4_.refs_13_), channel_id=1, source_target_pairs={{0,8},{1,9},{2,10},{3,11},{4,12},{5,13},{6,14},{7,15},{8,0},{9,1},... | collective-permute-start | bytes 3145736 | tf_op jit(solution)/shard_map/ppermute | solution.py:52
  (6 other events, 18.0 us)
